TPU v7x, 128 devices: a whole 4x4x4 slice. The times are simulated.
128 devices in a mesh: slot: 16 (over z_lo, x, core), param: 8 (over z_hi, y).
Axes of the slice: x: 4, y: 4, z: 4 (z_hi: 2, z_lo: 2; z = z_hi * 2 + z_lo), core: 2. Of those that a mesh axis runs over, the one named last changes fastest.
Arguments:
- history: float32 [256, 2048, 1024], P('slot', 'param'), may hold values from -6 to 6
- per_example: bfloat16 [64, 2048, 1024], P('slot', 'param')
- fresh: float32 [2048, 1024], P(('param', 'slot')), may hold values from -6 to 6
- moment1: float32 [2048, 1024], P(('param', 'slot')), may hold values from -4 to 4
- moment2: float32 [2048, 1024], P(('param', 'slot')), may hold values from 0.001 to 0.1
- master: float32 [2048, 1024], P(('param', 'slot')), may hold values from -6 to 6
- coef_table: float32 [64, 257], replicated, as said below
- table_index: int32 [1], replicated, may hold values from 0 to 63
- step_number: int32 [1], replicated, may hold values from 0 to 511
- cycle_slot: int32 [1], replicated, may hold values from 0 to 255
Outputs:
- new_noise: float32 [2048, 1024], P(('param', 'slot'))
- moment1_new: float32 [2048, 1024], P(('param', 'slot'))
- moment2_new: float32 [2048, 1024], P(('param', 'slot'))
- master_new: float32 [2048, 1024], P(('param', 'slot'))
- weights: bfloat16 [2048, 1024], P('param')
Inputs may be any that keep to these rules, and one draw needn't show every extreme that they name: `coef_table`: column 0 lies in [1, 2].
All inputs are finite; a program needn't handle non-finite values.
Results may differ from a plain program's by a relative error of at most 0.008.
Values may be sent and summed in bfloat16 or wider, within the bound.
No kernel may reach another device: no remote copies, remote signals or barrier semaphores. Data moves between devices by JAX's collectives and lax.ppermute only.
A program may use at most 64 MiB of HBM per device.

v0:
```python
import jax
import jax.numpy as jnp
from jax import lax
from jax.sharding import PartitionSpec as P


def shards(
    history,
    per_example,
    fresh,
    moment1,
    moment2,
    master,
    coef_table,
    table_index,
    step_number,
    cycle_slot,
):
    slots_dev = history.shape[0]
    rows_group = history.shape[1]
    lanes = history.shape[2]
    band = slots_dev * lax.axis_size("slot")
    step = step_number[0]
    cycle = cycle_slot[0]
    pick = (jnp.arange(coef_table.shape[0], dtype=jnp.int32) == table_index[0]).astype(jnp.float32)
    coefs = jnp.sum(pick[:, None] * coef_table, axis=0)
    first = lax.axis_index("slot") * slots_dev + jnp.arange(slots_dev, dtype=jnp.int32)
    lag = (cycle - first - 1) % band + 1
    lag_pick = (jnp.arange(band + 1, dtype=jnp.int32)[None, :] == lag[:, None]).astype(jnp.float32)
    slot_weight = jnp.where(lag <= step, jnp.sum(lag_pick * coefs[None, :], axis=1), 0.0)
    local_sq = jnp.einsum(
        "erl,erl->e", per_example, per_example, preferred_element_type=jnp.float32
    )
    sumsq = lax.psum(local_sq, "param")
    total = rows_group * lax.axis_size("param") * lanes
    factor = 1.0 / jnp.maximum(jnp.sqrt(sumsq / total), 1.0)
    piece = per_example
    grad_part = jnp.sum(factor[:, None, None] * piece.astype(jnp.float32), axis=0)
    piece = history
    summed = lax.psum_scatter(
        jnp.concatenate(
            [grad_part, jnp.tensordot(slot_weight, piece, axes=1, precision=lax.Precision.HIGHEST)],
            axis=1,
        ),
        "slot",
        scatter_dimension=0,
        tiled=True,
    )
    clipped = summed[:, :lanes]
    past = summed[:, lanes:]
    new_noise = (fresh - past) / coefs[0]
    noisy = clipped + new_noise
    count_steps = (step + 1).astype(jnp.float32)
    moment1_new = 0.9 * moment1 + 0.1 * noisy
    moment2_new = 0.999 * moment2 + 0.001 * noisy * noisy
    first_fix = 1.0 - jnp.power(jnp.float32(0.9), count_steps)
    second_fix = 1.0 - jnp.power(jnp.float32(0.999), count_steps)
    update = moment1_new / first_fix / (jnp.sqrt(moment2_new / second_fix) + 1e-08)
    master_new = master - 0.01 * update
    weights = lax.all_gather(master_new.astype(jnp.bfloat16), "slot", axis=0, tiled=True)
    return (new_noise, moment1_new, moment2_new, master_new, weights)


def solution(mesh):
    placed = (
        P("slot", "param", None),
        P("slot", "param", None),
        P(("param", "slot"), None),
        P(("param", "slot"), None),
        P(("param", "slot"), None),
        P(("param", "slot"), None),
        P(),
        P(),
        P(),
        P(),
    )
    return jax.shard_map(
        shards,
        mesh=mesh,
        in_specs=placed,
        out_specs=(
            P(("param", "slot"), None),
            P(("param", "slot"), None),
            P(("param", "slot"), None),
            P(("param", "slot"), None),
            P("param", None),
        ),
        check_vma=False,
    )
```

profile of v0, /device:TPU:1, one launch (start us, length us, event | category | flops | bytes accessed | tf_op | source)
XLA Modules:
  0.0 153.3 jit_solution(2531794983796706764)
XLA Ops:
  7.2 0.0 reduce-scatter.2.cloned.1.call-start
  8.5 2.2 %fusion.2 = f32[4]{0:T(128)S(1)} fusion(bf16[4,256,1024]{2,1,0:T(8,128)(2,1)} %param.11), kind=kLoop, calls=%fused_computation.3 | loop fusion | flops 3145724 | bytes 2097168 | tf_op jit(solution)/shard_map/erl,erl->e/dot_general | solution.py:31
  11.4 22.4 %psum.7 = f32[4]{0:T(128)S(1)} all-reduce(f32[4]{0:T(128)S(1)} %fusion.2), channel_id=1, replica_groups=mesh['slot'=16,'param'=8] {'param'}, use_global_device_ids=true, to_apply=%region_0.0 | all-reduce | flops 4 | bytes 32 | tf_op jit(solution)/shard_map/psum | solution.py:34
  33.8 1.0 multiply_reduce_fusion.1
  34.8 0.2 select_reduce_fusion
  35.0 0.0 copy-start
  35.0 24.0 %fusion = f32[1,256,1024]{2,0,1:T(1,128)S(1)} fusion(f32[16,256,1024]{2,1,0:T(8,128)} %param.10, f32[16]{0:T(128)S(1)} %select_reduce_fusion, s32[16]{0:T(128)S(1)} %fusion.5, s32[]{:T(128)} %bitcast.14), kind=kOutput, calls=%fused_computation | convolution fusion | flops 50331680 | bytes 17825924 | tf_op jit(solution)/shard_map/dot_general | solution.py:42
  59.0 0.2 copy.26
  59.2 0.0 copy-done
  59.2 0.0 copy-start.1
  59.2 0.0 copy-start.2
  59.2 0.0 copy-start.3
  59.3 0.0 copy-start.4
  59.3 0.5 multiply_reduce_fusion
  59.8 1.5 pad_maximum_fusion
  61.3 0.0 reduce-scatter.2.cloned.1.call-update
  61.3 0.5 slice.10
  61.9 59.7 %reduce-scatter.2.cloned.1.call-done = f32[16,2048]{1,0:T(8,128)} async-done(((f32[256,2048]{1,0:T(8,128)}), f32[16,2048]{1,0:T(8,128)}) %reduce-scatter.2.cloned.1.call-update) | async-done | bytes 131088 | tf_op jit(solution)/shard_map/reduce_scatter | solution.py:40
  121.6 0.0 copy-done.1
  121.6 0.0 copy-done.2
  121.6 0.0 copy-done.3
  121.6 0.0 copy-done.4
  121.6 2.2 %fusion.12 = (bf16[16,1024]{1,0:T(8,128)(2,1)S(1)}, f32[16,1024]{1,0:T(8,128)}, f32[16,1024]{1,0:T(8,128)}, f32[16,1024]{1,0:T(8,128)}, f32[16,1024]{1,0:T(8,128)}) fusion(f32[16,1024]{1,0:T(8,128)S(1)} %copy-done.1, f32[]{:T(128)S(6)} %sub.30, f32[]{:T(128)S(6)} %sub.29, f32[16,2048]{1,0:T(8,128)} %reduce-scatter.2.cloned.1.call-done, ...), kind=kLoop, calls=%fused_computation.29 | loop fusion | flops 278528 | bytes 688140 | tf_op jit(solution)/shard_map/convert_element_type | solution.py:60
  123.9 21.7 %all_gather.3 = bf16[256,1024]{1,0:T(8,128)(2,1)S(1)} all-gather(bf16[16,1024]{1,0:T(8,128)(2,1)S(1)} %get-tuple-element.5), channel_id=1, replica_groups=mesh['slot'=16,'param'=8] {'slot'}, dimensions={0}, use_global_device_ids=true | all-gather | bytes 557056 | tf_op jit(solution)/shard_map/all_gather | solution.py:60
  145.6 0.8 copy.31
  (3 shorter events, 0.0 us)
Async XLA Ops:
  7.2 114.5 %reduce-scatter.2.cloned.1.call-start = ((), (), s32[]{:S(2)}) async-start(), calls=%async_computation.1 | async-start | bytes 2228224 | tf_op jit(solution)/shard_map/reduce_scatter | solution.py:40
  35.0 24.3 %copy-start = (bf16[4,256,1024]{2,1,0:T(8,128)(2,1)S(1)}, bf16[4,256,1024]{2,1,0:T(8,128)(2,1)}, u32[]{:S(2)}) copy-start(bf16[4,256,1024]{2,1,0:T(8,128)(2,1)} %param.11) | copy-start | bytes 6291460
  59.2 62.4 %copy-start.1 = (f32[16,1024]{1,0:T(8,128)S(1)}, f32[16,1024]{1,0:T(8,128)}, u32[]{:S(2)}) copy-start(f32[16,1024]{1,0:T(8,128)} %param.15) | copy-start | bytes 196612
  59.2 62.4 %copy-start.2 = (f32[16,1024]{1,0:T(8,128)S(1)}, f32[16,1024]{1,0:T(8,128)}, u32[]{:S(2)}) copy-start(f32[16,1024]{1,0:T(8,128)} %param.14) | copy-start | bytes 196612
  59.2 62.4 %copy-start.3 = (f32[16,1024]{1,0:T(8,128)S(1)}, f32[16,1024]{1,0:T(8,128)}, u32[]{:S(2)}) copy-start(f32[16,1024]{1,0:T(8,128)} %param.13) | copy-start | bytes 196612
  59.3 62.4 %copy-start.4 = (f32[16,1024]{1,0:T(8,128)S(1)}, f32[16,1024]{1,0:T(8,128)}, u32[]{:S(2)}) copy-start(f32[16,1024]{1,0:T(8,128)} %param.12) | copy-start | bytes 196612
Sparse Core Ops, SparseCore 0:
  61.5 60.1 reduce-scatter.1
where the time goes:
time: 154 us; the launch traced here: 153 us
  waiting for transfers between devices  59.7 us (39%)
  blocking collectives  44.1 us (29%)
  matrix products  24 us (16%)
  between operations  16.2 us (11%)
  other arithmetic  7.7 us (5%)
    reduce_scatter x1, waiting for transfers between devices, shards(): lax.psum_scatter(jnp.concatenate([grad_part, jnp.tensordot(slot_weight, p...  59.7 us
    dot_general x1, matrix products, shards(): jnp.tensordot(slot_weight, piece, axes=1, precision=lax.Precision.HIGHEST)  24 us
    psum x1, blocking collectives, shards(): sumsq = lax.psum(local_sq, 'param')  22.4 us
    all_gather x1, blocking collectives, shards(): lax.all_gather(master_new.astype(jnp.bfloat16), 'slot', axis=0, tiled=True)  21.7 us
  transfers between devices with their start and end apart: 1, of which 1 were waited for; matrix products, arithmetic and copies ran while one was open for 0% of the time, Pallas kernels for 0%

commit v1 on v0

v1 whole, which is shorter than its diff:
```python
import jax
import jax.numpy as jnp
from jax import lax
from jax.experimental import pallas as pl
from jax.experimental.pallas import tpu as pltpu
from jax.sharding import PartitionSpec as P

MIB = 2**20
CORES = 2
VM = pl.BlockSpec(memory_space=pltpu.VMEM)
SM = pl.BlockSpec(memory_space=pltpu.SMEM)
HBM = pl.BlockSpec(memory_space=pl.ANY)


def params(mib):
    return pltpu.CompilerParams(vmem_limit_bytes=mib * MIB)


def core_index():
    return lax.rem(lax.axis_index("slot"), CORES)


def coef_row(coef_ref, index):
    row = lax.broadcasted_iota(jnp.int32, coef_ref.shape, 0)
    return jnp.sum(jnp.where(row == index, coef_ref[...], 0.0), axis=0, keepdims=True)


def square_kernel(grads_ref, out_ref, scratch):
    e = pl.program_id(0)
    total = jnp.zeros((8, 128), jnp.float32)
    for r in range(0, 256, 16):
        x = grads_ref[0, r : r + 16].astype(jnp.float32)
        x = x * x
        x = x[:8] + x[8:]
        for c in range(0, 1024, 128):
            total = total + x[:, c : c + 128]
    scratch[e] = jnp.broadcast_to(jnp.sum(total), (8, 128))

    @pl.when(e == 3)
    def _():
        rows = jnp.concatenate([scratch[k, 0:1] for k in range(4)] * 2, axis=0)
        for k in range(out_ref.shape[0]):
            out_ref[k] = rows


def squares(per_example):
    return pl.pallas_call(
        square_kernel,
        grid=(4,),
        in_specs=[pl.BlockSpec((1, 256, 1024), lambda e: (e, 0, 0))],
        out_specs=pl.BlockSpec((16, 8, 128), lambda e: (0, 0, 0)),
        out_shape=jax.ShapeDtypeStruct((16, 8, 128), jnp.float32),
        scratch_shapes=[pltpu.VMEM((4, 8, 128), jnp.float32)],
        compiler_params=params(8),
        cost_estimate=pl.CostEstimate(flops=2**30, bytes_accessed=32 * MIB, transcendentals=0),
        name="squares",
    )(per_example)


def past_kernel(table_ref, step_ref, cycle_ref, coef_ref, history_ref, keep_ref, send_ref, weight):
    slots = history_ref.shape[0]
    core = core_index()
    coefs = coef_row(coef_ref, table_ref[0])
    first = lax.axis_index("slot") * slots
    slot = first + lax.broadcasted_iota(jnp.int32, (slots, 1), 0)
    lag = ((cycle_ref[0] - slot - 1) & 255) + 1
    lane = lax.broadcasted_iota(jnp.int32, (slots, coefs.shape[1]), 1)
    picked = jnp.sum(jnp.where(lane == lag, coefs, 0.0), axis=1, keepdims=True)
    picked = jnp.where(lag <= step_ref[0], picked, 0.0)
    weight[...] = jnp.broadcast_to(picked, weight.shape)

    for part, out_ref in ((1 - core, send_ref), (core, keep_ref)):

        @pl.loop(0, 8)
        def _(b, part=part, out_ref=out_ref):
            for r in (0, 8):
                total = weight[0:1, :] * history_ref[0, b, part, r : r + 8, :]
                for s in range(1, slots):
                    total = total + weight[s : s + 1, :] * history_ref[s, b, part, r : r + 8, :]
                out_ref[b, r : r + 8, :] = total.astype(out_ref.dtype)


def past_parts(table_index, step_number, cycle_slot, coef_table, history):
    return pl.pallas_call(
        past_kernel,
        in_specs=[SM, SM, SM, VM, VM],
        out_specs=(VM, VM),
        out_shape=(
            jax.ShapeDtypeStruct((8, 16, 1024), jnp.float32),
            jax.ShapeDtypeStruct((8, 16, 1024), jnp.bfloat16),
        ),
        scratch_shapes=[pltpu.VMEM((16, 1024), jnp.float32)],
        compiler_params=params(24),
        cost_estimate=pl.CostEstimate(flops=8 * MIB, bytes_accessed=17 * MIB, transcendentals=0),
        name="past_parts",
    )(table_index, step_number, cycle_slot, coef_table, history)


def pack_kernel(sums_ref, own_ref, other_ref, keep_ref, got_ref, out_ref, factor):
    core = core_index()
    for side, part in ((0, core), (1, 1 - core)):
        total = sums_ref[0, part]
        for k in range(1, 8):
            total = total + sums_ref[k, part]
        rms = jnp.sqrt(total / (2048.0 * 1024.0))
        one = 1.0 / jnp.maximum(rms, 1.0)
        factor[side] = jnp.broadcast_to(one[:, 0:1], factor.shape[1:])

    @pl.loop(0, 8)
    def _(b):
        out_ref[b, 0] = (keep_ref[b] + got_ref[b].astype(jnp.float32)).astype(jnp.bfloat16)
        total = jnp.zeros((16, 1024), jnp.float32)
        for e in range(4):
            total = total + factor[0, e : e + 1, :] * own_ref[e, b, core].astype(jnp.float32)
            total = total + factor[1, e : e + 1, :] * other_ref[e, b, core].astype(jnp.float32)
        out_ref[b, 1] = total.astype(jnp.bfloat16)


def pack(sums, own, other, keep, got):
    return pl.pallas_call(
        pack_kernel,
        in_specs=[VM] * 5,
        out_specs=VM,
        out_shape=jax.ShapeDtypeStruct((8, 2, 16, 1024), jnp.bfloat16),
        scratch_shapes=[pltpu.VMEM((2, 8, 1024), jnp.float32)],
        compiler_params=params(12),
        cost_estimate=pl.CostEstimate(flops=4 * MIB, bytes_accessed=5 * MIB, transcendentals=0),
        name="pack",
    )(sums, own, other, keep, got)


def adam_kernel(
    table_ref, step_ref, coef_ref, parts_ref, fresh_ref, m1_ref, m2_ref, master_ref,
    noise_out, m1_out, m2_out, master_out, weights_out,
):
    past = parts_ref[0, 0].astype(jnp.float32)
    clipped = parts_ref[0, 1].astype(jnp.float32)
    for k in range(1, 8):
        past = past + parts_ref[k, 0].astype(jnp.float32)
        clipped = clipped + parts_ref[k, 1].astype(jnp.float32)
    first = coef_row(coef_ref, table_ref[0])[:, 0:1]
    new_noise = (fresh_ref[...] - past) / first
    noisy = clipped + new_noise
    count = jnp.full((1, 1), step_ref[0] + 1, jnp.int32).astype(jnp.float32)
    first_fix = 1.0 - jnp.power(jnp.float32(0.9), count)
    second_fix = 1.0 - jnp.power(jnp.float32(0.999), count)
    m1 = 0.9 * m1_ref[...] + 0.1 * noisy
    m2 = 0.999 * m2_ref[...] + 0.001 * noisy * noisy
    update = m1 / first_fix / (jnp.sqrt(m2 / second_fix) + 1e-08)
    master = master_ref[...] - 0.01 * update
    noise_out[...] = new_noise
    m1_out[...] = m1
    m2_out[...] = m2
    master_out[...] = master
    weights = master.astype(jnp.bfloat16)
    for k in range(8):
        weights_out[k] = weights


def adam(table_index, step_number, coef_table, parts, fresh, moment1, moment2, master):
    row = jax.ShapeDtypeStruct(fresh.shape, jnp.float32)
    return pl.pallas_call(
        adam_kernel,
        in_specs=[SM, SM] + [VM] * 6,
        out_specs=(VM,) * 5,
        out_shape=(row, row, row, row, jax.ShapeDtypeStruct((8, 16, 1024), jnp.bfloat16)),
        compiler_params=params(8),
        cost_estimate=pl.CostEstimate(flops=MIB, bytes_accessed=2 * MIB, transcendentals=0),
        name="adam",
    )(table_index, step_number, coef_table, parts, fresh, moment1, moment2, master)


def weave_kernel(own_ref, other_ref, out_ref, sems):
    core = core_index()
    a = pltpu.make_async_copy(own_ref, out_ref.at[:, core], sems.at[0])
    b = pltpu.make_async_copy(other_ref, out_ref.at[:, 1 - core], sems.at[1])
    a.start()
    b.start()
    a.wait()
    b.wait()


def weave(own, other):
    return pl.pallas_call(
        weave_kernel,
        in_specs=[HBM, HBM],
        out_specs=HBM,
        out_shape=jax.ShapeDtypeStruct((8, 2, 16, 1024), jnp.bfloat16),
        scratch_shapes=[pltpu.SemaphoreType.DMA((2,))],
        compiler_params=params(4),
        name="weave",
    )(own, other)


def shards(
    history,
    per_example,
    fresh,
    moment1,
    moment2,
    master,
    coef_table,
    table_index,
    step_number,
    cycle_slot,
):
    swap = [(i, i ^ 1) for i in range(16)]
    one_core = [[2 * k + c for k in range(8)] for c in range(2)]
    chips = [[16 * p + 2 * k + c for p in range(8) for c in range(2)] for k in range(8)]
    other_example = lax.ppermute(per_example, "slot", swap)
    sums = lax.all_to_all(
        squares(per_example), ("param", "slot"), 0, 0, tiled=True, axis_index_groups=chips
    )
    keep, send = past_parts(
        table_index, step_number, cycle_slot, coef_table, history.reshape(16, 8, 2, 16, 1024)
    )
    got = lax.ppermute(send, "slot", swap)
    packed = pack(
        sums.reshape(8, 2, 8, 128),
        per_example.reshape(4, 8, 2, 16, 1024),
        other_example.reshape(4, 8, 2, 16, 1024),
        keep,
        got,
    )
    parts = lax.all_to_all(packed, "slot", 0, 0, tiled=True, axis_index_groups=one_core)
    new_noise, m1, m2, master_new, weights = adam(
        table_index, step_number, coef_table, parts, fresh, moment1, moment2, master
    )
    gathered = lax.all_to_all(weights, "slot", 0, 0, tiled=True, axis_index_groups=one_core)
    gathered = weave(gathered, lax.ppermute(gathered, "slot", swap))
    return (new_noise, m1, m2, master_new, gathered.reshape(256, 1024))


def solution(mesh):
    placed = (
        P("slot", "param", None),
        P("slot", "param", None),
        P(("param", "slot"), None),
        P(("param", "slot"), None),
        P(("param", "slot"), None),
        P(("param", "slot"), None),
        P(),
        P(),
        P(),
        P(),
    )
    return jax.shard_map(
        shards,
        mesh=mesh,
        in_specs=placed,
        out_specs=(
            P(("param", "slot"), None),
            P(("param", "slot"), None),
            P(("param", "slot"), None),
            P(("param", "slot"), None),
            P("param", None),
        ),
        check_vma=False,
    )
```

time: 154 us -> 58.5 us (0.38)
  waiting for transfers between devices: 59.7 us -> 1.17 us
  matrix products: 24 us -> 0 us
  between operations: 16.2 us -> 2.66 us
  other arithmetic: 7.7 us -> 0 us
  blocking collectives: 44.1 us -> 37.8 us
  Pallas kernels: 0 us -> 5.46 us
  local copies, waits for them, and re-layouts: 1.53 us -> 6.68 us
  starting transfers between devices: 0.04 us -> 4.4 us
    reduce_scatter x1 -> x0, waiting for transfers between devices: 59.7 us -> none  [shards(): lax.psum_scatter(jnp.concatenate([grad_part, jnp.tensordot(slot_weight, p...]
    all_to_all x0 -> x3, blocking collectives: none -> 37.8 us  [the longest x1 15.5 us: shards(): lax.all_to_all(squares(per_example), ('param', 'slot'), 0, 0, tiled=True,...]
    dot_general x1 -> x0, matrix products: 24 us -> none  [shards(): jnp.tensordot(slot_weight, piece, axes=1, precision=lax.Precision.HIGHEST)]
    psum x1 -> x0, blocking collectives: 22.4 us -> none  [shards(): sumsq = lax.psum(local_sq, 'param')]
    all_gather x1 -> x0, blocking collectives: 21.7 us -> none  [shards(): lax.all_gather(master_new.astype(jnp.bfloat16), 'slot', axis=0, tiled=True)]
    unnamed x11 -> x14, local copies, waits for them, and re-layouts: 0.82 us -> 6.68 us
    pallas_call x0 -> x5, Pallas kernels: none -> 5.46 us  [the longest x1 2.05 us: past_parts(): pl.pallas_call(past_kernel, in_specs=[SM, SM, SM, VM, VM], out_specs=(VM,...]
    ppermute x0 -> x3, starting transfers between devices: none -> 4.4 us  [the longest x1 2.81 us: shards(): gathered = weave(gathered, lax.ppermute(gathered, 'slot', swap))]
  transfers between devices with their start and end apart: 1 -> 3, of which waited for: 1 -> 1; matrix products, arithmetic and copies ran while one was open for 0% -> 0% of each run, Pallas kernels for 0% -> 5%
where the time goes in v1:
time: 58.5 us; the launch traced here: 58.1 us
  blocking collectives  37.8 us (65%)
  local copies, waits for them, and re-layouts  6.68 us (11%)
  Pallas kernels  5.46 us (9%)
  starting transfers between devices  4.4 us (8%)
  between operations  2.66 us (5%)
  waiting for transfers between devices  1.17 us (2%)
    all_to_all x1, blocking collectives, shards(): lax.all_to_all(squares(per_example), ('param', 'slot'), 0, 0, tiled=True,...  15.5 us
    all_to_all x1, blocking collectives, shards(): lax.all_to_all(packed, 'slot', 0, 0, tiled=True, axis_index_groups=one_core)  13.7 us
    all_to_all x1, blocking collectives, shards(): lax.all_to_all(weights, 'slot', 0, 0, tiled=True, axis_index_groups=one_c...  8.62 us
    unnamed x14, local copies, waits for them, and re-layouts  6.68 us
    ppermute x1, starting transfers between devices, shards(): gathered = weave(gathered, lax.ppermute(gathered, 'slot', swap))  2.81 us
    pallas_call x1, Pallas kernels, past_parts(): pl.pallas_call(past_kernel, in_specs=[SM, SM, SM, VM, VM], out_specs=(VM,...  2.05 us
    ppermute x1, starting transfers between devices, shards(): other_example = lax.ppermute(per_example, 'slot', swap)  1.5 us
  transfers between devices with their start and end apart: 3, of which 1 were waited for; matrix products, arithmetic and copies ran while one was open for 0% of the time, Pallas kernels for 5%

profile of v1, /device:TPU:1, one launch (start us, length us, event | category | flops | bytes accessed | tf_op | source)
XLA Modules:
  0.0 58.1 jit_solution(7630396395583775015)
XLA Ops:
  0.6 1.5 %collective-permute-start = (bf16[4,256,1024]{2,1,0:T(8,128)(2,1)}, bf16[4,256,1024]{2,1,0:T(8,128)(2,1)S(1)}, u32[]{:S(2)}, u32[]{:S(2)}) collective-permute-start(bf16[4,256,1024]{2,1,0:T(8,128)(2,1)} %grads_ref.1), channel_id=1, source_target_pairs={{0,8},{8,0},{16,24},{24,16},{32,40},{40,32},{48,56},{56,48},{64,72... | collective-permute-start | bytes 6291464 | tf_op jit(solution)/shard_map/ppermute | solution.py:210
  4.1 0.0 copy-start
  4.1 5.8 %copy-done = f32[16,256,1024]{2,1,0:T(8,128)S(1)} copy-done((f32[16,256,1024]{2,1,0:T(8,128)S(1)}, f32[16,256,1024]{2,1,0:T(8,128)}, u32[]{:S(2)}) %copy-start) | copy-done | bytes 16777240
  9.8 0.0 copy-start.2
  9.8 0.9 %copy-done.2 = f32[64,257]{1,0:T(8,128)S(1)} copy-done((f32[64,257]{1,0:T(8,128)S(1)}, f32[64,257]{1,0:T(8,128)}, u32[]{:S(2)}) %copy-start.2) | copy-done | bytes 65816
  10.7 0.0 copy-start.1
  10.7 2.1 %past_parts.1 = (f32[8,16,1024]{2,1,0:T(8,128)S(1)}, bf16[8,16,1024]{2,1,0:T(8,128)(2,1)S(1)}) custom-call(s32[1]{0:T(128)S(6)} %copy.15.table_ref, s32[1]{0:T(128)S(6)} %copy.16.step_ref, s32[1]{0:T(128)S(6)} %copy.17.cycle_ref, f32[64,257]{1,0:T(8,128)S(1)} %copy-done.2, f32[16,8,2,16,1024]{4,3,2,1,0:T(8,128)S(1)} %bitcast.5), custom_call_target="tpu_custom_call" | custom-call | flops 8388608 | bytes 17825792 | tf_op jit(solution)/shard_map/past_parts/pallas_call | solution.py:84
  12.8 0.1 collective-permute-start.1
  12.9 0.0 copy-done.1
  12.9 1.1 %squares.1 = f32[16,8,128]{2,1,0:T(8,128)S(1)} custom-call(bf16[4,256,1024]{2,1,0:T(8,128)(2,1)S(1)} %copy-done.1), custom_call_target="tpu_custom_call" | custom-call | flops 1073741824 | bytes 33554432 | tf_op jit(solution)/shard_map/squares/pallas_call | solution.py:47
  14.0 15.5 %all_to_all.15 = f32[16,8,128]{2,1,0:T(8,128)S(1)} all-to-all(f32[16,8,128]{2,1,0:T(8,128)S(1)} %squares.1), channel_id=1, replica_groups={{0,8,1,9,2,10,3,11,4,12,5,13,6,14,7,15},{16,24,17,25,18,26,19,27,20,28,..., dimensions={0} | all-to-all | bytes 131072 | tf_op jit(solution)/shard_map/all_to_all | solution.py:211
  29.5 0.0 collective-permute-done.1.got_ref
  29.5 0.0 collective-permute-done
  29.5 0.0 copy-start.3
  29.5 0.0 copy-start.4
  29.5 0.0 copy-start.5
  29.5 0.0 copy-start.6
  29.5 0.7 %pack.1 = bf16[8,2,16,1024]{3,2,1,0:T(8,128)(2,1)S(1)} custom-call(f32[8,2,8,128]{3,2,1,0:T(8,128)S(1)} %bitcast.8, bf16[4,8,2,16,1024]{4,3,2,1,0:T(8,128)(2,1)S(1)} %bitcast.6, bf16[4,8,2,16,1024]{4,3,2,1,0:T(8,128)(2,1)S(1)} %bitcast.7, f32[8,16,1024]{2,1,0:T(8,128)S(1)} %get-tuple-element.12.keep_ref, bf16[8,16,1024]{2,1,0:T(8,128)(2,1)S(1)} %collective-permute-done.1.got_ref), custom_call_target="tpu_custom_call" | custom-call | flops 4194304 | bytes 5242880 | tf_op jit(solution)/shard_map/pack/pallas_call | solution.py:120
  30.2 13.7 %all_to_all.16.parts_ref = bf16[8,2,16,1024]{3,2,1,0:T(8,128)(2,1)S(1)} all-to-all(bf16[8,2,16,1024]{3,2,1,0:T(8,128)(2,1)S(1)} %pack.1), channel_id=1, replica_groups={{0,16,32,48,64,80,96,112},{8,24,40,56,72,88,104,120},{1,17,33,49,65,81,..., dimensions={0} | all-to-all | bytes 1048576 | tf_op jit(solution)/shard_map/all_to_all | solution.py:225
  43.9 0.0 copy-done.3
  43.9 0.0 copy-done.4
  43.9 0.0 copy-done.5
  43.9 0.0 copy-done.6
  43.9 0.8 %adam.1 = (f32[16,1024]{1,0:T(8,128)}, f32[16,1024]{1,0:T(8,128)}, f32[16,1024]{1,0:T(8,128)}, f32[16,1024]{1,0:T(8,128)}, bf16[8,16,1024]{2,1,0:T(8,128)(2,1)S(1)}) custom-call(s32[1]{0:T(128)S(6)} %copy.15.table_ref, s32[1]{0:T(128)S(6)} %copy.16.step_ref, f32[64,257]{1,0:T(8,128)S(1)} %copy-done.2, bf16[8,2,16,1024]{3,2,1,0:T(8,128)(2,1)S(1)} %all_to_all.16.parts_ref, ...), custom_call_target="tpu_custom_call" | custom-call | flops 1048576 | bytes 2097152 | tf_op jit(solution)/shard_map/adam/pallas_call | solution.py:162
  44.7 8.6 %all_to_all.17.own_ref = bf16[8,16,1024]{2,1,0:T(8,128)(2,1)S(1)} all-to-all(bf16[8,16,1024]{2,1,0:T(8,128)(2,1)S(1)} %get-tuple-element.18), channel_id=1, replica_groups={{0,16,32,48,64,80,96,112},{8,24,40,56,72,88,104,120},{1,17,33,49,65,81,..., dimensions={0} | all-to-all | bytes 524288 | tf_op jit(solution)/shard_map/all_to_all | solution.py:229
  53.4 2.8 %collective-permute-start.2 = (bf16[8,16,1024]{2,1,0:T(8,128)(2,1)S(1)}, bf16[8,16,1024]{2,1,0:T(8,128)(2,1)S(1)}, u32[]{:S(2)}, u32[]{:S(2)}) collective-permute-start(bf16[8,16,1024]{2,1,0:T(8,128)(2,1)S(1)} %all_to_all.17.own_ref), channel_id=1, source_target_pairs={{0,8},{8,0},{16,24},{24,16},{32,40},{40,32},{48,56},{56,48},{64,72... | collective-permute-start | bytes 786440 | tf_op jit(solution)/shard_map/ppermute | solution.py:230
  56.2 1.2 %collective-permute-done.2.other_ref = bf16[8,16,1024]{2,1,0:T(8,128)(2,1)S(1)} collective-permute-done((bf16[8,16,1024]{2,1,0:T(8,128)(2,1)S(1)}, bf16[8,16,1024]{2,1,0:T(8,128)(2,1)S(1)}, u32[]{:S(2)}, u32[]{:S(2)}) %collective-permute-start.2) | collective-permute-done | bytes 262176 | tf_op jit(solution)/shard_map/ppermute | solution.py:230
  57.3 0.8 %weave.1 = bf16[8,2,16,1024]{3,2,1,0:T(8,128)(2,1)} custom-call(bf16[8,16,1024]{2,1,0:T(8,128)(2,1)S(1)} %all_to_all.17.own_ref, bf16[8,16,1024]{2,1,0:T(8,128)(2,1)S(1)} %collective-permute-done.2.other_ref), custom_call_target="tpu_custom_call" | custom-call | tf_op jit(solution)/shard_map/weave/pallas_call | solution.py:184
Async XLA Ops:
  0.6 28.9 %collective-permute-start = (bf16[4,256,1024]{2,1,0:T(8,128)(2,1)}, bf16[4,256,1024]{2,1,0:T(8,128)(2,1)S(1)}, u32[]{:S(2)}, u32[]{:S(2)}) collective-permute-start(bf16[4,256,1024]{2,1,0:T(8,128)(2,1)} %grads_ref.1), channel_id=1, source_target_pairs={{0,8},{8,0},{16,24},{24,16},{32,40},{40,32},{48,56},{56,48},{64,72... | collective-permute-start | bytes 6291464 | tf_op jit(solution)/shard_map/ppermute | solution.py:210
  4.1 5.8 %copy-start = (f32[16,256,1024]{2,1,0:T(8,128)S(1)}, f32[16,256,1024]{2,1,0:T(8,128)}, u32[]{:S(2)}) copy-start(f32[16,256,1024]{2,1,0:T(8,128)} %param.10) | copy-start | bytes 50331652
  9.8 0.9 %copy-start.2 = (f32[64,257]{1,0:T(8,128)S(1)}, f32[64,257]{1,0:T(8,128)}, u32[]{:S(2)}) copy-start(f32[64,257]{1,0:T(8,128)} %coef_ref.3) | copy-start | bytes 197380
  10.7 2.2 %copy-start.1 = (bf16[4,256,1024]{2,1,0:T(8,128)(2,1)S(1)}, bf16[4,256,1024]{2,1,0:T(8,128)(2,1)}, u32[]{:S(2)}) copy-start(bf16[4,256,1024]{2,1,0:T(8,128)(2,1)} %grads_ref.1) | copy-start | bytes 6291460
  12.8 16.7 %collective-permute-start.1 = (bf16[8,16,1024]{2,1,0:T(8,128)(2,1)S(1)}, bf16[8,16,1024]{2,1,0:T(8,128)(2,1)S(1)}, u32[]{:S(2)}, u32[]{:S(2)}) collective-permute-start(bf16[8,16,1024]{2,1,0:T(8,128)(2,1)S(1)} %get-tuple-element.13), channel_id=1, source_target_pairs={{0,8},{8,0},{16,24},{24,16},{32,40},{40,32},{48,56},{56,48},{64,72... | collective-permute-start | bytes 786440 | tf_op jit(solution)/shard_map/ppermute | solution.py:217
  29.5 14.4 %copy-start.3 = (f32[16,1024]{1,0:T(8,128)S(1)}, f32[16,1024]{1,0:T(8,128)}, u32[]{:S(2)}) copy-start(f32[16,1024]{1,0:T(8,128)} %fresh_ref.1) | copy-start | bytes 196612
  29.5 14.4 %copy-start.4 = (f32[16,1024]{1,0:T(8,128)S(1)}, f32[16,1024]{1,0:T(8,128)}, u32[]{:S(2)}) copy-start(f32[16,1024]{1,0:T(8,128)} %m1_ref.1) | copy-start | bytes 196612
  29.5 14.4 %copy-start.5 = (f32[16,1024]{1,0:T(8,128)S(1)}, f32[16,1024]{1,0:T(8,128)}, u32[]{:S(2)}) copy-start(f32[16,1024]{1,0:T(8,128)} %m2_ref.1) | copy-start | bytes 196612
  29.5 14.4 %copy-start.6 = (f32[16,1024]{1,0:T(8,128)S(1)}, f32[16,1024]{1,0:T(8,128)}, u32[]{:S(2)}) copy-start(f32[16,1024]{1,0:T(8,128)} %master_ref.1) | copy-start | bytes 196612
  53.4 4.0 %collective-permute-start.2 = (bf16[8,16,1024]{2,1,0:T(8,128)(2,1)S(1)}, bf16[8,16,1024]{2,1,0:T(8,128)(2,1)S(1)}, u32[]{:S(2)}, u32[]{:S(2)}) collective-permute-start(bf16[8,16,1024]{2,1,0:T(8,128)(2,1)S(1)} %all_to_all.17.own_ref), channel_id=1, source_target_pairs={{0,8},{8,0},{16,24},{24,16},{32,40},{40,32},{48,56},{56,48},{64,72... | collective-permute-start | bytes 786440 | tf_op jit(solution)/shard_map/ppermute | solution.py:230

commit v2 on v1

v2 whole, which is shorter than its diff:
```python
import functools

import jax
import jax.numpy as jnp
from jax import lax
from jax.experimental import pallas as pl
from jax.experimental.pallas import tpu as pltpu
from jax.sharding import PartitionSpec as P

MIB = 2**20
CORES = 2
VM = pl.BlockSpec(memory_space=pltpu.VMEM)
HBM = pl.BlockSpec(memory_space=pl.ANY)


def params(mib):
    return pltpu.CompilerParams(vmem_limit_bytes=mib * MIB)


def core_index():
    return lax.rem(lax.axis_index("slot"), CORES)


def coef_row(coef_ref, index):
    row = lax.broadcasted_iota(jnp.int32, coef_ref.shape, 0)
    return jnp.sum(jnp.where(row == index, coef_ref[...], 0.0), axis=0, keepdims=True)


def square_kernel(grads_ref, out_ref):
    rows = []
    for e in range(4):
        total = [jnp.zeros((16, 128), jnp.float32) for _ in range(4)]
        for r in range(0, 256, 16):
            for c in range(0, 1024, 128):
                x = grads_ref[e, r : r + 16, c : c + 128].astype(jnp.float32)
                total[(c // 128) % 4] = total[(c // 128) % 4] + x * x
        total = (total[0] + total[1]) + (total[2] + total[3])
        rows.append(jnp.broadcast_to(jnp.sum(total), (1, 128)))
    rows = jnp.concatenate(rows * 2, axis=0)
    core = lax.broadcasted_iota(jnp.int32, rows.shape, 0) // 4
    out_ref[...] = jnp.where(core == core_index(), rows, 0.0)


def squares(per_example):
    return pl.pallas_call(
        square_kernel,
        in_specs=[VM],
        out_specs=VM,
        out_shape=jax.ShapeDtypeStruct((8, 128), jnp.float32),
        compiler_params=params(8),
        cost_estimate=pl.CostEstimate(flops=2**30, bytes_accessed=64 * MIB, transcendentals=0),
        name="squares",
    )(per_example)


def past_kernel(side, table_ref, step_ref, cycle_ref, coef_ref, history_ref, _, out_ref, weight):
    slots = history_ref.shape[0]
    part = core_index()
    if side:
        part = 1 - part
    coefs = coef_row(coef_ref, table_ref[...])
    first = lax.axis_index("slot") * slots
    slot = first + lax.broadcasted_iota(jnp.int32, (slots, 1), 0)
    lag = ((cycle_ref[...] - slot - 1) & 255) + 1
    lane = lax.broadcasted_iota(jnp.int32, (slots, coefs.shape[1]), 1)
    picked = jnp.sum(jnp.where(lane == lag, coefs, 0.0), axis=1, keepdims=True)
    picked = jnp.where(lag <= step_ref[...], picked, 0.0)
    weight[...] = jnp.broadcast_to(picked, weight.shape)

    @pl.loop(0, 8)
    def _(b):
        for r in (0, 8):
            total = weight[0:1, :] * history_ref[0, b, part, r : r + 8, :]
            for s in range(1, slots):
                total = total + weight[s : s + 1, :] * history_ref[s, b, part, r : r + 8, :]
            out_ref[b, r : r + 8, :] = total.astype(out_ref.dtype)


def past_part(side, dtype, table_index, step_number, cycle_slot, coef_table, history, after):
    return pl.pallas_call(
        functools.partial(past_kernel, side),
        in_specs=[VM] * 5 + [HBM],
        out_specs=VM,
        out_shape=jax.ShapeDtypeStruct((8, 16, 1024), dtype),
        scratch_shapes=[pltpu.VMEM((16, 1024), jnp.float32)],
        compiler_params=params(4),
        cost_estimate=pl.CostEstimate(flops=4 * MIB, bytes_accessed=8 * MIB, transcendentals=0),
        name="past_part",
    )(table_index, step_number, cycle_slot, coef_table, history, after)


def pack_kernel(sums_ref, last_ref, own_ref, other_ref, keep_ref, got_ref, out_ref, factor):
    core = core_index()
    rms = jnp.sqrt((sums_ref[...] + last_ref[...]) / (2048.0 * 1024.0))
    one = 1.0 / jnp.maximum(rms, 1.0)
    factor[0] = jnp.broadcast_to(jnp.where(core == 0, one[0:4, 0:1], one[4:8, 0:1]), factor.shape[1:])
    factor[1] = jnp.broadcast_to(jnp.where(core == 0, one[4:8, 0:1], one[0:4, 0:1]), factor.shape[1:])

    @pl.loop(0, 8)
    def _(b):
        out_ref[b, 0] = (keep_ref[b] + got_ref[b].astype(jnp.float32)).astype(jnp.bfloat16)
        total = jnp.zeros((16, 1024), jnp.float32)
        for e in range(4):
            total = total + factor[0, e : e + 1, :] * own_ref[e, b, core].astype(jnp.float32)
            total = total + factor[1, e : e + 1, :] * other_ref[e, b, core].astype(jnp.float32)
        out_ref[b, 1] = total.astype(jnp.bfloat16)


def pack(sums, last, own, other, keep, got):
    return pl.pallas_call(
        pack_kernel,
        in_specs=[VM] * 6,
        out_specs=VM,
        out_shape=jax.ShapeDtypeStruct((8, 2, 16, 1024), jnp.bfloat16),
        scratch_shapes=[pltpu.VMEM((2, 4, 1024), jnp.float32)],
        compiler_params=params(12),
        cost_estimate=pl.CostEstimate(flops=4 * MIB, bytes_accessed=5 * MIB, transcendentals=0),
        name="pack",
    )(sums, last, own, other, keep, got)


def adam_kernel(
    table_ref, step_ref, coef_ref, parts_ref, fresh_ref, m1_ref, m2_ref, master_ref,
    noise_out, m1_out, m2_out, master_out, weights_out,
):
    past = parts_ref[0, 0].astype(jnp.float32)
    clipped = parts_ref[0, 1].astype(jnp.float32)
    for k in range(1, 8):
        past = past + parts_ref[k, 0].astype(jnp.float32)
        clipped = clipped + parts_ref[k, 1].astype(jnp.float32)
    first = coef_row(coef_ref, table_ref[...])[:, 0:1]
    new_noise = (fresh_ref[...] - past) / first
    noisy = clipped + new_noise
    count = (step_ref[...] + 1).astype(jnp.float32)
    first_fix = 1.0 - jnp.power(jnp.float32(0.9), count)
    second_fix = 1.0 - jnp.power(jnp.float32(0.999), count)
    m1 = 0.9 * m1_ref[...] + 0.1 * noisy
    m2 = 0.999 * m2_ref[...] + 0.001 * noisy * noisy
    update = m1 / first_fix / (jnp.sqrt(m2 / second_fix) + 1e-08)
    master = master_ref[...] - 0.01 * update
    noise_out[...] = new_noise
    m1_out[...] = m1
    m2_out[...] = m2
    master_out[...] = master
    weights = master.astype(jnp.bfloat16)
    for k in range(8):
        weights_out[k] = weights


def adam(table_index, step_number, coef_table, parts, fresh, moment1, moment2, master):
    row = jax.ShapeDtypeStruct(fresh.shape, jnp.float32)
    return pl.pallas_call(
        adam_kernel,
        in_specs=[VM] * 8,
        out_specs=(VM,) * 5,
        out_shape=(row, row, row, row, jax.ShapeDtypeStruct((8, 16, 1024), jnp.bfloat16)),
        compiler_params=params(8),
        cost_estimate=pl.CostEstimate(flops=MIB, bytes_accessed=2 * MIB, transcendentals=0),
        name="adam",
    )(table_index, step_number, coef_table, parts, fresh, moment1, moment2, master)


def weave_kernel(own_ref, other_ref, out_ref, sems):
    core = core_index()
    a = pltpu.make_async_copy(own_ref, out_ref.at[:, core], sems.at[0])
    b = pltpu.make_async_copy(other_ref, out_ref.at[:, 1 - core], sems.at[1])
    a.start()
    b.start()
    a.wait()
    b.wait()


def weave(own, other):
    return pl.pallas_call(
        weave_kernel,
        in_specs=[HBM, HBM],
        out_specs=HBM,
        out_shape=jax.ShapeDtypeStruct((8, 2, 16, 1024), jnp.bfloat16),
        scratch_shapes=[pltpu.SemaphoreType.DMA((2,))],
        compiler_params=params(4),
        name="weave",
    )(own, other)


def shards(
    history,
    per_example,
    fresh,
    moment1,
    moment2,
    master,
    coef_table,
    table_index,
    step_number,
    cycle_slot,
):
    table_index, step_number, cycle_slot = (
        x.reshape(1, 1) for x in (table_index, step_number, cycle_slot)
    )
    swap = [(i, i ^ 1) for i in range(16)]
    one_core = [[2 * k + c for k in range(8)] for c in range(2)]
    near = [(i, i ^ 1) for i in range(8)]
    far = [(i, i ^ 3) for i in range(8)]
    across = [(i, i ^ 4) for i in range(8)]
    sums = squares(per_example)
    sums = sums + lax.ppermute(sums, "slot", swap)
    _, early = lax.optimization_barrier((sums, per_example))
    other_example = lax.ppermute(early, "slot", swap)
    sums = sums + lax.ppermute(sums, "param", near)
    sums = sums + lax.ppermute(sums, "param", far)
    last = lax.ppermute(sums, "param", across)
    blocks = history.reshape(16, 8, 2, 16, 1024)
    send = past_part(
        1, jnp.bfloat16, table_index, step_number, cycle_slot, coef_table, blocks, sums
    )
    got = lax.ppermute(send, "slot", swap)
    keep = past_part(
        0, jnp.float32, table_index, step_number, cycle_slot, coef_table, blocks, send
    )
    packed = pack(
        sums,
        last,
        per_example.reshape(4, 8, 2, 16, 1024),
        other_example.reshape(4, 8, 2, 16, 1024),
        keep,
        got,
    )
    parts = lax.all_to_all(packed, "slot", 0, 0, tiled=True, axis_index_groups=one_core)
    new_noise, m1, m2, master_new, weights = adam(
        table_index, step_number, coef_table, parts, fresh, moment1, moment2, master
    )
    gathered = lax.all_to_all(weights, "slot", 0, 0, tiled=True, axis_index_groups=one_core)
    gathered = weave(gathered, lax.ppermute(gathered, "slot", swap))
    return (new_noise, m1, m2, master_new, gathered.reshape(256, 1024))


def solution(mesh):
    placed = (
        P("slot", "param", None),
        P("slot", "param", None),
        P(("param", "slot"), None),
        P(("param", "slot"), None),
        P(("param", "slot"), None),
        P(("param", "slot"), None),
        P(),
        P(),
        P(),
        P(),
    )
    return jax.shard_map(
        shards,
        mesh=mesh,
        in_specs=placed,
        out_specs=(
            P(("param", "slot"), None),
            P(("param", "slot"), None),
            P(("param", "slot"), None),
            P(("param", "slot"), None),
            P("param", None),
        ),
        check_vma=False,
    )
```

time: 58.5 us -> 55.1 us (0.942)
  blocking collectives: 37.8 us -> 21.8 us
  starting transfers between devices: 4.4 us -> 14.7 us
  waiting for transfers between devices: 1.17 us -> 3.07 us
  local copies, waits for them, and re-layouts: 6.68 us -> 7.38 us
    all_to_all x1 -> x0, blocking collectives: 15.5 us -> none  [shards(): lax.all_to_all(squares(per_example), ('param', 'slot'), 0, 0, tiled=True,...]
    ppermute x1 -> x5, starting transfers between devices: 1.5 us -> 9.65 us  [the longest x1 3.61 us: shards(): last = lax.ppermute(sums, 'param', across)]
    ppermute x1 -> x5, waiting for transfers between devices: 0.01 us -> 1.91 us  [the longest x1 1.08 us: shards(): sums = sums + lax.ppermute(sums, 'param', near)]
    ppermute x1, starting transfers between devices: 0.09 us -> 1.68 us  [shards(): got = lax.ppermute(send, 'slot', swap)]
    unnamed x14 -> x16, local copies, waits for them, and re-layouts: 6.68 us -> 7.38 us
    pallas_call x4 -> x5, Pallas kernels: 4.65 us -> 4.4 us  [the longest x2 2.43 us: past_part(): pl.pallas_call(functools.partial(past_kernel, side), in_specs=[VM] * 5 +...]
  transfers between devices with their start and end apart: 3 -> 7, of which waited for: 1 -> 3; matrix products, arithmetic and copies ran while one was open for 0% -> 0% of each run, Pallas kernels for 5% -> 4%
where the time goes in v2:
time: 55.1 us; the launch traced here: 54.8 us
  blocking collectives  21.8 us (40%)
  starting transfers between devices  14.7 us (27%)
  local copies, waits for them, and re-layouts  7.38 us (13%)
  Pallas kernels  5.21 us (9%)
  waiting for transfers between devices  3.07 us (6%)
  between operations  2.72 us (5%)
    all_to_all x1, blocking collectives, shards(): lax.all_to_all(packed, 'slot', 0, 0, tiled=True, axis_index_groups=one_core)  13.1 us
    all_to_all x1, blocking collectives, shards(): lax.all_to_all(weights, 'slot', 0, 0, tiled=True, axis_index_groups=one_c...  8.65 us
    unnamed x16, local copies, waits for them, and re-layouts  7.38 us
    ppermute x1, starting transfers between devices, shards(): last = lax.ppermute(sums, 'param', across)  3.61 us
    ppermute x1, starting transfers between devices, shards(): gathered = weave(gathered, lax.ppermute(gathered, 'slot', swap))  3.34 us
    ppermute x1, starting transfers between devices, shards(): sums = sums + lax.ppermute(sums, 'param', far)  2.82 us
    pallas_call x2, Pallas kernels, past_part(): pl.pallas_call(functools.partial(past_kernel, side), in_specs=[VM] * 5 +...  2.43 us
    ppermute x1, starting transfers between devices, shards(): got = lax.ppermute(send, 'slot', swap)  1.68 us
  transfers between devices with their start and end apart: 7, of which 3 were waited for; matrix products, arithmetic and copies ran while one was open for 0% of the time, Pallas kernels for 4%

profile of v2, /device:TPU:1, one launch (start us, length us, event | category | flops | bytes accessed | tf_op | source)
XLA Modules:
  0.0 54.8 jit_solution(3486919769362071979)
XLA Ops:
  0.6 0.0 copy-start.1
  0.6 1.6 %copy-done.1 = bf16[4,256,1024]{2,1,0:T(8,128)(2,1)S(1)} copy-done((bf16[4,256,1024]{2,1,0:T(8,128)(2,1)S(1)}, bf16[4,256,1024]{2,1,0:T(8,128)(2,1)}, u32[]{:S(2)}) %copy-start.1) | copy-done | bytes 2097176
  2.2 0.5 squares.1
  2.8 1.5 %collective-permute-start = (f32[8,128]{1,0:T(8,128)S(1)}, f32[8,128]{1,0:T(8,128)S(1)}, u32[]{:S(2)}, u32[]{:S(2)}) collective-permute-start(f32[8,128]{1,0:T(8,128)S(1)} %squares.1), channel_id=1, source_target_pairs={{0,8},{8,0},{16,24},{24,16},{32,40},{40,32},{48,56},{56,48},{64,72... | collective-permute-start | bytes 12296 | tf_op jit(solution)/shard_map/ppermute | solution.py:206
  4.3 0.8 %collective-permute-done = f32[8,128]{1,0:T(8,128)S(1)} collective-permute-done((f32[8,128]{1,0:T(8,128)S(1)}, f32[8,128]{1,0:T(8,128)S(1)}, u32[]{:S(2)}, u32[]{:S(2)}) %collective-permute-start) | collective-permute-done | bytes 4128 | tf_op jit(solution)/shard_map/ppermute | solution.py:206
  5.1 0.3 collective-permute-start.4
  5.4 1.4 %collective-permute-start.1 = (f32[8,128]{1,0:T(8,128)S(1)}, f32[8,128]{1,0:T(8,128)S(1)}, u32[]{:S(2)}, u32[]{:S(2)}) collective-permute-start(f32[8,128]{1,0:T(8,128)S(1)} %add.9), channel_id=1, source_target_pairs={{0,1},{1,0},{2,3},{3,2},{4,5},{5,4},{6,7},{7,6},{8,9},{9,8},{10,11... | collective-permute-start | bytes 12296 | tf_op jit(solution)/shard_map/ppermute | solution.py:209
  6.8 1.1 %collective-permute-done.1 = f32[8,128]{1,0:T(8,128)S(1)} collective-permute-done((f32[8,128]{1,0:T(8,128)S(1)}, f32[8,128]{1,0:T(8,128)S(1)}, u32[]{:S(2)}, u32[]{:S(2)}) %collective-permute-start.1) | collective-permute-done | bytes 4128 | tf_op jit(solution)/shard_map/ppermute | solution.py:209
  7.9 2.8 %collective-permute-start.2 = (f32[8,128]{1,0:T(8,128)S(1)}, f32[8,128]{1,0:T(8,128)S(1)}, u32[]{:S(2)}, u32[]{:S(2)}) collective-permute-start(f32[8,128]{1,0:T(8,128)S(1)} %add.10), channel_id=1, source_target_pairs={{0,3},{1,2},{2,1},{3,0},{4,7},{5,6},{6,5},{7,4},{8,11},{9,10},{10,... | collective-permute-start | bytes 12296 | tf_op jit(solution)/shard_map/ppermute | solution.py:210
  12.7 0.0 collective-permute-done.2
  12.7 0.0 copy-start
  12.7 5.8 %copy-done = f32[16,256,1024]{2,1,0:T(8,128)S(1)} copy-done((f32[16,256,1024]{2,1,0:T(8,128)S(1)}, f32[16,256,1024]{2,1,0:T(8,128)}, u32[]{:S(2)}) %copy-start) | copy-done | bytes 16777240
  18.5 1.2 %past_part.2._ = bf16[8,16,1024]{2,1,0:T(8,128)(2,1)S(1)} custom-call(s32[1,1]{1,0:T(1,128)} %bitcast.7.table_ref, s32[1,1]{1,0:T(1,128)} %bitcast.10.step_ref, s32[1,1]{1,0:T(1,128)} %bitcast.13.cycle_ref, f32[64,257]{1,0:T(8,128)S(1)} %copy-done.3, f32[16,8,2,16,1024]{4,3,2,1,0:T(8,128)S(1)} %bitcast.15, f32[8,128]{1,0:T(8,128)S(1)} %add.11._.sums_ref), custom_call_target="tpu_custom_call" | custom-call | flops 4194304 | bytes 8388608 | tf_op jit(solution)/shard_map/past_part/pallas_call | solution.py:80
  19.7 1.7 %collective-permute-start.5 = (bf16[8,16,1024]{2,1,0:T(8,128)(2,1)S(1)}, bf16[8,16,1024]{2,1,0:T(8,128)(2,1)S(1)}, u32[]{:S(2)}, u32[]{:S(2)}) collective-permute-start(bf16[8,16,1024]{2,1,0:T(8,128)(2,1)S(1)} %past_part.2._), channel_id=1, source_target_pairs={{0,8},{8,0},{16,24},{24,16},{32,40},{40,32},{48,56},{56,48},{64,72... | collective-permute-start | bytes 786440 | tf_op jit(solution)/shard_map/ppermute | solution.py:216
  21.4 3.6 %collective-permute-start.3 = (f32[8,128]{1,0:T(8,128)S(1)}, f32[8,128]{1,0:T(8,128)S(1)}, u32[]{:S(2)}, u32[]{:S(2)}) collective-permute-start(f32[8,128]{1,0:T(8,128)S(1)} %add.11._.sums_ref), channel_id=1, source_target_pairs={{0,4},{1,5},{2,6},{3,7},{4,0},{5,1},{6,2},{7,3},{8,12},{9,13},{10,... | collective-permute-start | bytes 12296 | tf_op jit(solution)/shard_map/ppermute | solution.py:211
  25.0 1.2 %past_part.3.keep_ref = f32[8,16,1024]{2,1,0:T(8,128)S(1)} custom-call(s32[1,1]{1,0:T(1,128)} %bitcast.8.table_ref, s32[1,1]{1,0:T(1,128)} %bitcast.11.step_ref, s32[1,1]{1,0:T(1,128)} %bitcast.14.cycle_ref, f32[64,257]{1,0:T(8,128)S(1)} %copy-done.3, f32[16,8,2,16,1024]{4,3,2,1,0:T(8,128)S(1)} %bitcast.16, bf16[8,16,1024]{2,1,0:T(8,128)(2,1)S(1)} %past_part.2._), custom_call_target="tpu_custom_call" | custom-call | flops 4194304 | bytes 8388608 | tf_op jit(solution)/shard_map/past_part/pallas_call | solution.py:80
  26.2 0.0 collective-permute-done.3.last_ref
  26.2 0.0 collective-permute-done.5.got_ref
  26.2 0.0 collective-permute-done.4
  26.2 0.0 copy-start.4
  26.2 0.0 copy-start.5
  26.3 0.0 copy-start.6
  26.3 0.0 copy-start.7
  26.3 0.6 %pack.1 = bf16[8,2,16,1024]{3,2,1,0:T(8,128)(2,1)S(1)} custom-call(f32[8,128]{1,0:T(8,128)S(1)} %add.11._.sums_ref, f32[8,128]{1,0:T(8,128)S(1)} %collective-permute-done.3.last_ref, bf16[4,8,2,16,1024]{4,3,2,1,0:T(8,128)(2,1)S(1)} %bitcast.17, bf16[4,8,2,16,1024]{4,3,2,1,0:T(8,128)(2,1)S(1)} %bitcast.18, f32[8,16,1024]{2,1,0:T(8,128)S(1)} %past_part.3.keep_ref, ...), custom_call_target="tpu_custom_call" | custom-call | flops 4194304 | bytes 5242880 | tf_op jit(solution)/shard_map/pack/pallas_call | solution.py:110
  26.9 13.1 %all_to_all.10.parts_ref = bf16[8,2,16,1024]{3,2,1,0:T(8,128)(2,1)S(1)} all-to-all(bf16[8,2,16,1024]{3,2,1,0:T(8,128)(2,1)S(1)} %pack.1), channel_id=1, replica_groups={{0,16,32,48,64,80,96,112},{8,24,40,56,72,88,104,120},{1,17,33,49,65,81,..., dimensions={0} | all-to-all | bytes 1048576 | tf_op jit(solution)/shard_map/all_to_all | solution.py:228
  40.0 0.0 copy-done.4
  40.0 0.0 copy-done.6
  40.0 0.9 %adam.1 = (f32[16,1024]{1,0:T(8,128)}, f32[16,1024]{1,0:T(8,128)}, f32[16,1024]{1,0:T(8,128)}, f32[16,1024]{1,0:T(8,128)}, bf16[8,16,1024]{2,1,0:T(8,128)(2,1)S(1)}) custom-call(s32[1,1]{1,0:T(1,128)} %bitcast.9.table_ref, s32[1,1]{1,0:T(1,128)} %bitcast.12.step_ref, f32[64,257]{1,0:T(8,128)S(1)} %copy-done.3, ...), custom_call_target="tpu_custom_call" | custom-call | flops 1048576 | bytes 2097152 | tf_op jit(solution)/shard_map/adam/pallas_call | solution.py:152
  40.9 8.6 %all_to_all.11.own_ref = bf16[8,16,1024]{2,1,0:T(8,128)(2,1)S(1)} all-to-all(bf16[8,16,1024]{2,1,0:T(8,128)(2,1)S(1)} %get-tuple-element.16), channel_id=1, replica_groups={{0,16,32,48,64,80,96,112},{8,24,40,56,72,88,104,120},{1,17,33,49,65,81,..., dimensions={0} | all-to-all | bytes 524288 | tf_op jit(solution)/shard_map/all_to_all | solution.py:232
  49.5 3.3 %collective-permute-start.6 = (bf16[8,16,1024]{2,1,0:T(8,128)(2,1)S(1)}, bf16[8,16,1024]{2,1,0:T(8,128)(2,1)S(1)}, u32[]{:S(2)}, u32[]{:S(2)}) collective-permute-start(bf16[8,16,1024]{2,1,0:T(8,128)(2,1)S(1)} %all_to_all.11.own_ref), channel_id=1, source_target_pairs={{0,8},{8,0},{16,24},{24,16},{32,40},{40,32},{48,56},{56,48},{64,72... | collective-permute-start | bytes 786440 | tf_op jit(solution)/shard_map/ppermute | solution.py:233
  52.9 1.2 %collective-permute-done.6.other_ref = bf16[8,16,1024]{2,1,0:T(8,128)(2,1)S(1)} collective-permute-done((bf16[8,16,1024]{2,1,0:T(8,128)(2,1)S(1)}, bf16[8,16,1024]{2,1,0:T(8,128)(2,1)S(1)}, u32[]{:S(2)}, u32[]{:S(2)}) %collective-permute-start.6) | collective-permute-done | bytes 262176 | tf_op jit(solution)/shard_map/ppermute | solution.py:233
  54.0 0.8 %weave.1 = bf16[8,2,16,1024]{3,2,1,0:T(8,128)(2,1)} custom-call(bf16[8,16,1024]{2,1,0:T(8,128)(2,1)S(1)} %all_to_all.11.own_ref, bf16[8,16,1024]{2,1,0:T(8,128)(2,1)S(1)} %collective-permute-done.6.other_ref), custom_call_target="tpu_custom_call" | custom-call | tf_op jit(solution)/shard_map/weave/pallas_call | solution.py:174
  (9 shorter events, 0.0 us)
Async XLA Ops:
  0.6 1.6 %copy-start.1 = (bf16[4,256,1024]{2,1,0:T(8,128)(2,1)S(1)}, bf16[4,256,1024]{2,1,0:T(8,128)(2,1)}, u32[]{:S(2)}) copy-start(bf16[4,256,1024]{2,1,0:T(8,128)(2,1)} %grads_ref.1) | copy-start | bytes 6291460
  2.2 2.9 %copy-start.2 = (bf16[4,256,1024]{2,1,0:T(8,128)(2,1)S(1)}, bf16[4,256,1024]{2,1,0:T(8,128)(2,1)}, u32[]{:S(2)}) copy-start(bf16[4,256,1024]{2,1,0:T(8,128)(2,1)} %grads_ref.1) | copy-start | bytes 6291460
  2.2 10.5 %copy-start.3 = (f32[64,257]{1,0:T(8,128)S(1)}, f32[64,257]{1,0:T(8,128)}, u32[]{:S(2)}) copy-start(f32[64,257]{1,0:T(8,128)} %coef_ref.5) | copy-start | bytes 197380
  2.8 2.3 %collective-permute-start = (f32[8,128]{1,0:T(8,128)S(1)}, f32[8,128]{1,0:T(8,128)S(1)}, u32[]{:S(2)}, u32[]{:S(2)}) collective-permute-start(f32[8,128]{1,0:T(8,128)S(1)} %squares.1), channel_id=1, source_target_pairs={{0,8},{8,0},{16,24},{24,16},{32,40},{40,32},{48,56},{56,48},{64,72... | collective-permute-start | bytes 12296 | tf_op jit(solution)/shard_map/ppermute | solution.py:206
  5.1 21.1 %collective-permute-start.4 = (bf16[4,256,1024]{2,1,0:T(8,128)(2,1)S(1)}, bf16[4,256,1024]{2,1,0:T(8,128)(2,1)S(1)}, u32[]{:S(2)}, u32[]{:S(2)}) collective-permute-start(bf16[4,256,1024]{2,1,0:T(8,128)(2,1)S(1)} %copy-done.2), channel_id=1, source_target_pairs={{0,8},{8,0},{16,24},{24,16},{32,40},{40,32},{48,56},{56,48},{64,72... | collective-permute-start | bytes 6291464 | tf_op jit(solution)/shard_map/ppermute | solution.py:208
  5.4 2.5 %collective-permute-start.1 = (f32[8,128]{1,0:T(8,128)S(1)}, f32[8,128]{1,0:T(8,128)S(1)}, u32[]{:S(2)}, u32[]{:S(2)}) collective-permute-start(f32[8,128]{1,0:T(8,128)S(1)} %add.9), channel_id=1, source_target_pairs={{0,1},{1,0},{2,3},{3,2},{4,5},{5,4},{6,7},{7,6},{8,9},{9,8},{10,11... | collective-permute-start | bytes 12296 | tf_op jit(solution)/shard_map/ppermute | solution.py:209
  7.9 4.8 %collective-permute-start.2 = (f32[8,128]{1,0:T(8,128)S(1)}, f32[8,128]{1,0:T(8,128)S(1)}, u32[]{:S(2)}, u32[]{:S(2)}) collective-permute-start(f32[8,128]{1,0:T(8,128)S(1)} %add.10), channel_id=1, source_target_pairs={{0,3},{1,2},{2,1},{3,0},{4,7},{5,6},{6,5},{7,4},{8,11},{9,10},{10,... | collective-permute-start | bytes 12296 | tf_op jit(solution)/shard_map/ppermute | solution.py:210
  12.7 5.8 %copy-start = (f32[16,256,1024]{2,1,0:T(8,128)S(1)}, f32[16,256,1024]{2,1,0:T(8,128)}, u32[]{:S(2)}) copy-start(f32[16,256,1024]{2,1,0:T(8,128)} %param.10) | copy-start | bytes 50331652
  19.7 6.5 %collective-permute-start.5 = (bf16[8,16,1024]{2,1,0:T(8,128)(2,1)S(1)}, bf16[8,16,1024]{2,1,0:T(8,128)(2,1)S(1)}, u32[]{:S(2)}, u32[]{:S(2)}) collective-permute-start(bf16[8,16,1024]{2,1,0:T(8,128)(2,1)S(1)} %past_part.2._), channel_id=1, source_target_pairs={{0,8},{8,0},{16,24},{24,16},{32,40},{40,32},{48,56},{56,48},{64,72... | collective-permute-start | bytes 786440 | tf_op jit(solution)/shard_map/ppermute | solution.py:216
  21.4 4.8 %collective-permute-start.3 = (f32[8,128]{1,0:T(8,128)S(1)}, f32[8,128]{1,0:T(8,128)S(1)}, u32[]{:S(2)}, u32[]{:S(2)}) collective-permute-start(f32[8,128]{1,0:T(8,128)S(1)} %add.11._.sums_ref), channel_id=1, source_target_pairs={{0,4},{1,5},{2,6},{3,7},{4,0},{5,1},{6,2},{7,3},{8,12},{9,13},{10,... | collective-permute-start | bytes 12296 | tf_op jit(solution)/shard_map/ppermute | solution.py:211
  26.2 13.8 %copy-start.4 = (f32[16,1024]{1,0:T(8,128)S(1)}, f32[16,1024]{1,0:T(8,128)}, u32[]{:S(2)}) copy-start(f32[16,1024]{1,0:T(8,128)} %fresh_ref.1) | copy-start | bytes 196612
  26.2 13.8 %copy-start.5 = (f32[16,1024]{1,0:T(8,128)S(1)}, f32[16,1024]{1,0:T(8,128)}, u32[]{:S(2)}) copy-start(f32[16,1024]{1,0:T(8,128)} %m1_ref.1) | copy-start | bytes 196612
  26.3 13.8 %copy-start.6 = (f32[16,1024]{1,0:T(8,128)S(1)}, f32[16,1024]{1,0:T(8,128)}, u32[]{:S(2)}) copy-start(f32[16,1024]{1,0:T(8,128)} %m2_ref.1) | copy-start | bytes 196612
  26.3 13.7 %copy-start.7 = (f32[16,1024]{1,0:T(8,128)S(1)}, f32[16,1024]{1,0:T(8,128)}, u32[]{:S(2)}) copy-start(f32[16,1024]{1,0:T(8,128)} %master_ref.1) | copy-start | bytes 196612
  49.5 4.5 %collective-permute-start.6 = (bf16[8,16,1024]{2,1,0:T(8,128)(2,1)S(1)}, bf16[8,16,1024]{2,1,0:T(8,128)(2,1)S(1)}, u32[]{:S(2)}, u32[]{:S(2)}) collective-permute-start(bf16[8,16,1024]{2,1,0:T(8,128)(2,1)S(1)} %all_to_all.11.own_ref), channel_id=1, source_target_pairs={{0,8},{8,0},{16,24},{24,16},{32,40},{40,32},{48,56},{56,48},{64,72... | collective-permute-start | bytes 786440 | tf_op jit(solution)/shard_map/ppermute | solution.py:233

commit v3 on v2

--- a/solution.py
+++ b/solution.py
@@ -9,6 +9,7 @@
 
 MIB = 2**20
 CORES = 2
+SM = pl.BlockSpec(memory_space=pltpu.SMEM)
 VM = pl.BlockSpec(memory_space=pltpu.VMEM)
 HBM = pl.BlockSpec(memory_space=pl.ANY)
 
@@ -30,9 +31,9 @@
     rows = []
     for e in range(4):
         total = [jnp.zeros((16, 128), jnp.float32) for _ in range(4)]
-        for r in range(0, 256, 16):
+        for r in range(16):
             for c in range(0, 1024, 128):
-                x = grads_ref[e, r : r + 16, c : c + 128].astype(jnp.float32)
+                x = grads_ref[e, r // 2, r % 2, :, c : c + 128].astype(jnp.float32)
                 total[(c // 128) % 4] = total[(c // 128) % 4] + x * x
         total = (total[0] + total[1]) + (total[2] + total[3])
         rows.append(jnp.broadcast_to(jnp.sum(total), (1, 128)))
@@ -48,45 +49,64 @@
         out_specs=VM,
         out_shape=jax.ShapeDtypeStruct((8, 128), jnp.float32),
         compiler_params=params(8),
-        cost_estimate=pl.CostEstimate(flops=2**30, bytes_accessed=64 * MIB, transcendentals=0),
+        cost_estimate=pl.CostEstimate(flops=2**37, bytes_accessed=2 * MIB, transcendentals=0),
         name="squares",
     )(per_example)
 
 
-def past_kernel(side, table_ref, step_ref, cycle_ref, coef_ref, history_ref, _, out_ref, weight):
+def past_kernel(table_ref, step_ref, cycle_ref, coef_ref, history_ref, _, keep_ref, send_ref, weight):
     slots = history_ref.shape[0]
-    part = core_index()
-    if side:
-        part = 1 - part
-    coefs = coef_row(coef_ref, table_ref[...])
+    core = core_index()
+    coefs = coef_row(coef_ref, table_ref[0])
     first = lax.axis_index("slot") * slots
     slot = first + lax.broadcasted_iota(jnp.int32, (slots, 1), 0)
-    lag = ((cycle_ref[...] - slot - 1) & 255) + 1
+    lag = ((cycle_ref[0] - slot - 1) & 255) + 1
     lane = lax.broadcasted_iota(jnp.int32, (slots, coefs.shape[1]), 1)
     picked = jnp.sum(jnp.where(lane == lag, coefs, 0.0), axis=1, keepdims=True)
-    picked = jnp.where(lag <= step_ref[...], picked, 0.0)
+    picked = jnp.where(lag <= step_ref[0], picked, 0.0)
     weight[...] = jnp.broadcast_to(picked, weight.shape)
 
-    @pl.loop(0, 8)
-    def _(b):
-        for r in (0, 8):
-            total = weight[0:1, :] * history_ref[0, b, part, r : r + 8, :]
-            for s in range(1, slots):
-                total = total + weight[s : s + 1, :] * history_ref[s, b, part, r : r + 8, :]
-            out_ref[b, r : r + 8, :] = total.astype(out_ref.dtype)
-
-
-def past_part(side, dtype, table_index, step_number, cycle_slot, coef_table, history, after):
-    return pl.pallas_call(
-        functools.partial(past_kernel, side),
-        in_specs=[VM] * 5 + [HBM],
-        out_specs=VM,
-        out_shape=jax.ShapeDtypeStruct((8, 16, 1024), dtype),
+    for part, out_ref in ((1 - core, send_ref), (core, keep_ref)):
+
+        @pl.loop(0, 8)
+        def _(b, part=part, out_ref=out_ref):
+            for r in (0, 8):
+                total = weight[0:1, :] * history_ref[0, b, part, r : r + 8, :]
+                for s in range(1, slots):
+                    total = total + weight[s : s + 1, :] * history_ref[s, b, part, r : r + 8, :]
+                out_ref[b, r : r + 8, :] = total.astype(out_ref.dtype)
+
+
+def past_parts(table_index, step_number, cycle_slot, coef_table, history, after):
+    return pl.pallas_call(
+        past_kernel,
+        in_specs=[SM] * 3 + [VM] * 2 + [HBM],
+        out_specs=(VM, VM),
+        out_shape=(
+            jax.ShapeDtypeStruct((8, 16, 1024), jnp.float32),
+            jax.ShapeDtypeStruct((8, 16, 1024), jnp.bfloat16),
+        ),
         scratch_shapes=[pltpu.VMEM((16, 1024), jnp.float32)],
         compiler_params=params(4),
-        cost_estimate=pl.CostEstimate(flops=4 * MIB, bytes_accessed=8 * MIB, transcendentals=0),
-        name="past_part",
+        cost_estimate=pl.CostEstimate(flops=1, bytes_accessed=1, transcendentals=0),
+        name="past_parts",
     )(table_index, step_number, cycle_slot, coef_table, history, after)
+
+
+def add_kernel(a_ref, b_ref, out_ref):
+    out_ref[...] = a_ref[...] + b_ref[...]
+
+
+def add(a, b):
+    return pl.pallas_call(
+        add_kernel,
+        in_specs=[VM, VM],
+        out_specs=VM,
+        out_shape=jax.ShapeDtypeStruct(a.shape, a.dtype),
+        compiler_params=params(4),
+        cost_estimate=pl.CostEstimate(flops=2**34, bytes_accessed=12288, transcendentals=0),
+        name="add",
+    )(a, b)
 
 
 def pack_kernel(sums_ref, last_ref, own_ref, other_ref, keep_ref, got_ref, out_ref, factor):
@@ -128,10 +148,10 @@
     for k in range(1, 8):
         past = past + parts_ref[k, 0].astype(jnp.float32)
         clipped = clipped + parts_ref[k, 1].astype(jnp.float32)
-    first = coef_row(coef_ref, table_ref[...])[:, 0:1]
+    first = coef_row(coef_ref, table_ref[0])[:, 0:1]
     new_noise = (fresh_ref[...] - past) / first
     noisy = clipped + new_noise
-    count = (step_ref[...] + 1).astype(jnp.float32)
+    count = jnp.full((1, 1), step_ref[0] + 1, jnp.int32).astype(jnp.float32)
     first_fix = 1.0 - jnp.power(jnp.float32(0.9), count)
     second_fix = 1.0 - jnp.power(jnp.float32(0.999), count)
     m1 = 0.9 * m1_ref[...] + 0.1 * noisy
@@ -151,7 +171,7 @@
     row = jax.ShapeDtypeStruct(fresh.shape, jnp.float32)
     return pl.pallas_call(
         adam_kernel,
-        in_specs=[VM] * 8,
+        in_specs=[SM] * 2 + [VM] * 6,
         out_specs=(VM,) * 5,
         out_shape=(row, row, row, row, jax.ShapeDtypeStruct((8, 16, 1024), jnp.bfloat16)),
         compiler_params=params(8),
@@ -194,37 +214,25 @@
     step_number,
     cycle_slot,
 ):
-    table_index, step_number, cycle_slot = (
-        x.reshape(1, 1) for x in (table_index, step_number, cycle_slot)
-    )
     swap = [(i, i ^ 1) for i in range(16)]
     one_core = [[2 * k + c for k in range(8)] for c in range(2)]
     near = [(i, i ^ 1) for i in range(8)]
     far = [(i, i ^ 3) for i in range(8)]
     across = [(i, i ^ 4) for i in range(8)]
-    sums = squares(per_example)
+    examples = per_example.reshape(4, 8, 2, 16, 1024)
+    sums = squares(examples)
     sums = sums + lax.ppermute(sums, "slot", swap)
-    _, early = lax.optimization_barrier((sums, per_example))
-    other_example = lax.ppermute(early, "slot", swap)
-    sums = sums + lax.ppermute(sums, "param", near)
-    sums = sums + lax.ppermute(sums, "param", far)
-    last = lax.ppermute(sums, "param", across)
-    blocks = history.reshape(16, 8, 2, 16, 1024)
-    send = past_part(
-        1, jnp.bfloat16, table_index, step_number, cycle_slot, coef_table, blocks, sums
+    _, early = lax.optimization_barrier((sums, examples))
+    other = lax.ppermute(early, "slot", swap)
+    keep, send = past_parts(
+        table_index, step_number, cycle_slot, coef_table, history.reshape(16, 8, 2, 16, 1024), sums
     )
     got = lax.ppermute(send, "slot", swap)
-    keep = past_part(
-        0, jnp.float32, table_index, step_number, cycle_slot, coef_table, blocks, send
-    )
-    packed = pack(
-        sums,
-        last,
-        per_example.reshape(4, 8, 2, 16, 1024),
-        other_example.reshape(4, 8, 2, 16, 1024),
-        keep,
-        got,
-    )
+    sums = sums + lax.ppermute(sums, "param", across)
+    sums, keep = lax.optimization_barrier((sums, keep))
+    sums = add(sums, lax.ppermute(sums, "param", near))
+    last = lax.ppermute(sums, "param", far)
+    packed = pack(sums, last, examples, other, keep, got)
     parts = lax.all_to_all(packed, "slot", 0, 0, tiled=True, axis_index_groups=one_core)
     new_noise, m1, m2, master_new, weights = adam(
         table_index, step_number, coef_table, parts, fresh, moment1, moment2, master

time: 55.1 us -> 49.1 us (0.89)
  local copies, waits for them, and re-layouts: 7.38 us -> 1.78 us
  blocking collectives: 21.8 us -> 20.7 us
  starting transfers between devices: 14.7 us -> 15.5 us
    unnamed x16 -> x22, local copies, waits for them, and re-layouts: 7.38 us -> 1.78 us
    ppermute x1, starting transfers between devices: 3.34 us -> 5.05 us  [shards(): gathered = weave(gathered, lax.ppermute(gathered, 'slot', swap))]
    all_to_all x1, blocking collectives: 13.1 us -> 12.1 us  [shards(): lax.all_to_all(packed, 'slot', 0, 0, tiled=True, axis_index_groups=one_core)]
    ppermute x1, starting transfers between devices: 1.68 us -> 0.73 us  [shards(): got = lax.ppermute(send, 'slot', swap)]
  transfers between devices with their start and end apart: 7 -> 7, of which waited for: 3 -> 4; matrix products, arithmetic and copies ran while one was open for 0% -> 0% of each run, Pallas kernels for 4% -> 4%
where the time goes in v3:
time: 49.1 us; the launch traced here: 48.9 us
  blocking collectives  20.7 us (42%)
  starting transfers between devices  15.5 us (32%)
  Pallas kernels  4.79 us (10%)
  waiting for transfers between devices  3.42 us (7%)
  between operations  2.73 us (6%)
  local copies, waits for them, and re-layouts  1.78 us (4%)
    all_to_all x1, blocking collectives, shards(): lax.all_to_all(packed, 'slot', 0, 0, tiled=True, axis_index_groups=one_core)  12.1 us
    all_to_all x1, blocking collectives, shards(): lax.all_to_all(weights, 'slot', 0, 0, tiled=True, axis_index_groups=one_c...  8.54 us
    ppermute x1, starting transfers between devices, shards(): gathered = weave(gathered, lax.ppermute(gathered, 'slot', swap))  5.05 us
    ppermute x1, starting transfers between devices, shards(): sums = sums + lax.ppermute(sums, 'param', across)  3.68 us
    ppermute x1, starting transfers between devices, shards(): last = lax.ppermute(sums, 'param', far)  2.81 us
    pallas_call x1, Pallas kernels, past_parts(): pl.pallas_call(past_kernel, in_specs=[SM] * 3 + [VM] * 2 + [HBM], out_spe...  2.05 us
    unnamed x22, local copies, waits for them, and re-layouts  1.78 us
    ppermute x1, starting transfers between devices, shards(): sums = sums + lax.ppermute(sums, 'slot', swap)  1.5 us
  transfers between devices with their start and end apart: 7, of which 4 were waited for; matrix products, arithmetic and copies ran while one was open for 0% of the time, Pallas kernels for 4%

profile of v3, /device:TPU:1, one launch (start us, length us, event | category | flops | bytes accessed | tf_op | source)
XLA Modules:
  0.0 48.9 jit_solution(8831527576462850133)
XLA Ops:
  0.6 0.0 slice-start
  0.6 0.0 copy-start
  0.7 1.7 %copy-done = bf16[4,256,1024]{2,1,0:T(8,128)(2,1)S(1)} copy-done((bf16[4,256,1024]{2,1,0:T(8,128)(2,1)S(1)}, bf16[4,256,1024]{2,1,0:T(8,128)(2,1)}, u32[]{:S(2)}) %copy-start) | copy-done | bytes 2097176
  2.4 0.0 copy-start.2
  2.4 0.5 %squares.1 = f32[8,128]{1,0:T(8,128)S(1)} custom-call(bf16[4,8,2,16,1024]{4,3,2,1,0:T(8,128)(2,1)S(1)} %bitcast.6), custom_call_target="tpu_custom_call" | custom-call | flops 137438953472 | bytes 2097152 | tf_op jit(solution)/shard_map/squares/pallas_call | solution.py:46
  2.9 1.5 %collective-permute-start = (f32[8,128]{1,0:T(8,128)S(1)}, f32[8,128]{1,0:T(8,128)S(1)}, u32[]{:S(2)}, u32[]{:S(2)}) collective-permute-start(f32[8,128]{1,0:T(8,128)S(1)} %squares.1), channel_id=1, source_target_pairs={{0,8},{8,0},{16,24},{24,16},{32,40},{40,32},{48,56},{56,48},{64,72... | collective-permute-start | bytes 12296 | tf_op jit(solution)/shard_map/ppermute | solution.py:224
  4.4 0.8 %collective-permute-done = f32[8,128]{1,0:T(8,128)S(1)} collective-permute-done((f32[8,128]{1,0:T(8,128)S(1)}, f32[8,128]{1,0:T(8,128)S(1)}, u32[]{:S(2)}, u32[]{:S(2)}) %collective-permute-start) | collective-permute-done | bytes 4128 | tf_op jit(solution)/shard_map/ppermute | solution.py:224
  5.3 0.0 copy-done.1
  5.3 0.3 collective-permute-start.4
  5.6 3.7 %collective-permute-start.1 = (f32[8,128]{1,0:T(8,128)S(1)}, f32[8,128]{1,0:T(8,128)S(1)}, u32[]{:S(2)}, u32[]{:S(2)}) collective-permute-start(f32[8,128]{1,0:T(8,128)S(1)} %add.7._), channel_id=1, source_target_pairs={{0,4},{1,5},{2,6},{3,7},{4,0},{5,1},{6,2},{7,3},{8,12},{9,13},{10,... | collective-permute-start | bytes 12296 | tf_op jit(solution)/shard_map/ppermute | solution.py:231
  11.2 0.0 slice-done
  11.3 0.0 slice-done.1
  11.3 0.0 slice-done.2
  11.3 0.0 slice-done.3
  11.3 2.1 %past_parts.1 = (f32[8,16,1024]{2,1,0:T(8,128)S(1)}, bf16[8,16,1024]{2,1,0:T(8,128)(2,1)S(1)}) custom-call(s32[1]{0:T(128)S(6)} %copy.15.table_ref, s32[1]{0:T(128)S(6)} %copy.16.step_ref, s32[1]{0:T(128)S(6)} %copy.17.cycle_ref, f32[64,257]{1,0:T(8,128)S(1)} %copy-done.2, f32[16,8,2,16,1024]{4,3,2,1,0:T(8,128)S(1)} %bitcast.5, f32[8,128]{1,0:T(8,128)S(1)} %add.7._), custom_call_target="tpu_custom_call" | custom-call | flops 1 | bytes 1 | tf_op jit(solution)/shard_map/past_parts/pallas_call | solution.py:81
  13.4 0.0 collective-permute-done.1
  13.4 1.4 %collective-permute-start.2 = (f32[8,128]{1,0:T(8,128)S(1)}, f32[8,128]{1,0:T(8,128)S(1)}, u32[]{:S(2)}, u32[]{:S(2)}) collective-permute-start(f32[8,128]{1,0:T(8,128)S(1)} %add.8.a_ref), channel_id=1, source_target_pairs={{0,1},{1,0},{2,3},{3,2},{4,5},{5,4},{6,7},{7,6},{8,9},{9,8},{10,11... | collective-permute-start | bytes 12296 | tf_op jit(solution)/shard_map/ppermute | solution.py:233
  14.8 0.7 %collective-permute-start.5 = (bf16[8,16,1024]{2,1,0:T(8,128)(2,1)S(1)}, bf16[8,16,1024]{2,1,0:T(8,128)(2,1)S(1)}, u32[]{:S(2)}, u32[]{:S(2)}) collective-permute-start(bf16[8,16,1024]{2,1,0:T(8,128)(2,1)S(1)} %get-tuple-element.19), channel_id=1, source_target_pairs={{0,8},{8,0},{16,24},{24,16},{32,40},{40,32},{48,56},{56,48},{64,72... | collective-permute-start | bytes 786440 | tf_op jit(solution)/shard_map/ppermute | solution.py:230
  15.5 0.4 collective-permute-done.2.b_ref
  15.9 0.0 copy-start.6
  15.9 2.8 %collective-permute-start.3 = (f32[8,128]{1,0:T(8,128)S(1)}, f32[8,128]{1,0:T(8,128)S(1)}, u32[]{:S(2)}, u32[]{:S(2)}) collective-permute-start(f32[8,128]{1,0:T(8,128)S(1)} %add.9.sums_ref), channel_id=1, source_target_pairs={{0,3},{1,2},{2,1},{3,0},{4,7},{5,6},{6,5},{7,4},{8,11},{9,10},{10,... | collective-permute-start | bytes 12296 | tf_op jit(solution)/shard_map/ppermute | solution.py:234
  18.8 1.0 %collective-permute-done.3.last_ref = f32[8,128]{1,0:T(8,128)S(1)} collective-permute-done((f32[8,128]{1,0:T(8,128)S(1)}, f32[8,128]{1,0:T(8,128)S(1)}, u32[]{:S(2)}, u32[]{:S(2)}) %collective-permute-start.3) | collective-permute-done | bytes 4128 | tf_op jit(solution)/shard_map/ppermute | solution.py:234
  19.8 0.0 collective-permute-done.5.got_ref
  19.8 0.0 collective-permute-done.4.other_ref
  19.8 0.6 %pack.1 = bf16[8,2,16,1024]{3,2,1,0:T(8,128)(2,1)S(1)} custom-call(f32[8,128]{1,0:T(8,128)S(1)} %add.9.sums_ref, f32[8,128]{1,0:T(8,128)S(1)} %collective-permute-done.3.last_ref, bf16[4,8,2,16,1024]{4,3,2,1,0:T(8,128)(2,1)S(1)} %bitcast.8, bf16[4,8,2,16,1024]{4,3,2,1,0:T(8,128)(2,1)S(1)} %collective-permute-done.4.other_ref, ...), custom_call_target="tpu_custom_call" | custom-call | flops 4194304 | bytes 5242880 | tf_op jit(solution)/shard_map/pack/pallas_call | solution.py:130
  20.4 12.1 %all_to_all.10.parts_ref = bf16[8,2,16,1024]{3,2,1,0:T(8,128)(2,1)S(1)} all-to-all(bf16[8,2,16,1024]{3,2,1,0:T(8,128)(2,1)S(1)} %pack.1), channel_id=1, replica_groups={{0,16,32,48,64,80,96,112},{8,24,40,56,72,88,104,120},{1,17,33,49,65,81,..., dimensions={0} | all-to-all | bytes 1048576 | tf_op jit(solution)/shard_map/all_to_all | solution.py:236
  32.5 0.0 copy-done.4
  32.5 0.8 %adam.1 = (f32[16,1024]{1,0:T(8,128)}, f32[16,1024]{1,0:T(8,128)}, f32[16,1024]{1,0:T(8,128)}, f32[16,1024]{1,0:T(8,128)}, bf16[8,16,1024]{2,1,0:T(8,128)(2,1)S(1)}) custom-call(s32[1]{0:T(128)S(6)} %copy.15.table_ref, s32[1]{0:T(128)S(6)} %copy.16.step_ref, f32[64,257]{1,0:T(8,128)S(1)} %copy-done.2, bf16[8,2,16,1024]{3,2,1,0:T(8,128)(2,1)S(1)} %all_to_all.10.parts_ref, ...), custom_call_target="tpu_custom_call" | custom-call | flops 1048576 | bytes 2097152 | tf_op jit(solution)/shard_map/adam/pallas_call | solution.py:172
  33.3 8.5 %all_to_all.11.own_ref = bf16[8,16,1024]{2,1,0:T(8,128)(2,1)S(1)} all-to-all(bf16[8,16,1024]{2,1,0:T(8,128)(2,1)S(1)} %get-tuple-element.24), channel_id=1, replica_groups={{0,16,32,48,64,80,96,112},{8,24,40,56,72,88,104,120},{1,17,33,49,65,81,..., dimensions={0} | all-to-all | bytes 524288 | tf_op jit(solution)/shard_map/all_to_all | solution.py:240
  41.9 5.0 %collective-permute-start.6 = (bf16[8,16,1024]{2,1,0:T(8,128)(2,1)S(1)}, bf16[8,16,1024]{2,1,0:T(8,128)(2,1)S(1)}, u32[]{:S(2)}, u32[]{:S(2)}) collective-permute-start(bf16[8,16,1024]{2,1,0:T(8,128)(2,1)S(1)} %all_to_all.11.own_ref), channel_id=1, source_target_pairs={{0,8},{8,0},{16,24},{24,16},{32,40},{40,32},{48,56},{56,48},{64,72... | collective-permute-start | bytes 786440 | tf_op jit(solution)/shard_map/ppermute | solution.py:241
  46.9 1.2 %collective-permute-done.6.other_ref = bf16[8,16,1024]{2,1,0:T(8,128)(2,1)S(1)} collective-permute-done((bf16[8,16,1024]{2,1,0:T(8,128)(2,1)S(1)}, bf16[8,16,1024]{2,1,0:T(8,128)(2,1)S(1)}, u32[]{:S(2)}, u32[]{:S(2)}) %collective-permute-start.6) | collective-permute-done | bytes 262176 | tf_op jit(solution)/shard_map/ppermute | solution.py:241
  48.1 0.8 %weave.1 = bf16[8,2,16,1024]{3,2,1,0:T(8,128)(2,1)} custom-call(bf16[8,16,1024]{2,1,0:T(8,128)(2,1)S(1)} %all_to_all.11.own_ref, bf16[8,16,1024]{2,1,0:T(8,128)(2,1)S(1)} %collective-permute-done.6.other_ref), custom_call_target="tpu_custom_call" | custom-call | tf_op jit(solution)/shard_map/weave/pallas_call | solution.py:194
  (15 shorter events, 0.0 us)
Async XLA Ops:
  0.6 10.6 %slice-start = ((s8[16777216]{0:T(1024)(128)(4,1)}), s8[4194304]{0:T(1024)(128)(4,1)S(1)}, s32[]{:S(2)}) async-start(s8[16777216]{0:T(1024)(128)(4,1)} %bitcast.3), calls=%async_computation.2 | async-start | bytes 8388608
  0.6 1.7 %copy-start = (bf16[4,256,1024]{2,1,0:T(8,128)(2,1)S(1)}, bf16[4,256,1024]{2,1,0:T(8,128)(2,1)}, u32[]{:S(2)}) copy-start(bf16[4,256,1024]{2,1,0:T(8,128)(2,1)} %param.11) | copy-start | bytes 6291460
  2.4 2.9 %copy-start.1 = (bf16[4,256,1024]{2,1,0:T(8,128)(2,1)S(1)}, bf16[4,256,1024]{2,1,0:T(8,128)(2,1)}, u32[]{:S(2)}) copy-start(bf16[4,256,1024]{2,1,0:T(8,128)(2,1)} %param.11) | copy-start | bytes 6291460
  2.4 8.9 %slice-start.1 = ((s8[16777216]{0:T(1024)(128)(4,1)}), s8[4194304]{0:T(1024)(128)(4,1)S(1)}, s32[]{:S(2)}) async-start(s8[16777216]{0:T(1024)(128)(4,1)} %bitcast.3), calls=%async_computation.3 | async-start | bytes 8388608
  2.4 8.9 %slice-start.2 = ((s8[16777216]{0:T(1024)(128)(4,1)}), s8[4194304]{0:T(1024)(128)(4,1)S(1)}, s32[]{:S(2)}) async-start(s8[16777216]{0:T(1024)(128)(4,1)} %bitcast.3), calls=%async_computation.4 | async-start | bytes 8388608
  2.4 8.9 %slice-start.3 = ((s8[16777216]{0:T(1024)(128)(4,1)}), s8[4194304]{0:T(1024)(128)(4,1)S(1)}, s32[]{:S(2)}) async-start(s8[16777216]{0:T(1024)(128)(4,1)} %bitcast.3), calls=%async_computation.5 | async-start | bytes 8388608
  2.4 8.9 %copy-start.2 = (f32[64,257]{1,0:T(8,128)S(1)}, f32[64,257]{1,0:T(8,128)}, u32[]{:S(2)}) copy-start(f32[64,257]{1,0:T(8,128)} %coef_ref.3) | copy-start | bytes 197380
  2.9 2.3 %collective-permute-start = (f32[8,128]{1,0:T(8,128)S(1)}, f32[8,128]{1,0:T(8,128)S(1)}, u32[]{:S(2)}, u32[]{:S(2)}) collective-permute-start(f32[8,128]{1,0:T(8,128)S(1)} %squares.1), channel_id=1, source_target_pairs={{0,8},{8,0},{16,24},{24,16},{32,40},{40,32},{48,56},{56,48},{64,72... | collective-permute-start | bytes 12296 | tf_op jit(solution)/shard_map/ppermute | solution.py:224
  5.3 14.5 %collective-permute-start.4 = (bf16[4,8,2,16,1024]{4,3,2,1,0:T(8,128)(2,1)S(1)}, bf16[4,8,2,16,1024]{4,3,2,1,0:T(8,128)(2,1)S(1)}, u32[]{:S(2)}, u32[]{:S(2)}) collective-permute-start(bf16[4,8,2,16,1024]{4,3,2,1,0:T(8,128)(2,1)S(1)} %bitcast.7), channel_id=1, source_target_pairs={{0,8},{8,0},{16,24},{24,16},{32,40},{40,32},{48,56},{56,48},{64,72... | collective-permute-start | bytes 6291464 | tf_op jit(solution)/shard_map/ppermute | solution.py:226
  5.6 7.7 %collective-permute-start.1 = (f32[8,128]{1,0:T(8,128)S(1)}, f32[8,128]{1,0:T(8,128)S(1)}, u32[]{:S(2)}, u32[]{:S(2)}) collective-permute-start(f32[8,128]{1,0:T(8,128)S(1)} %add.7._), channel_id=1, source_target_pairs={{0,4},{1,5},{2,6},{3,7},{4,0},{5,1},{6,2},{7,3},{8,12},{9,13},{10,... | collective-permute-start | bytes 12296 | tf_op jit(solution)/shard_map/ppermute | solution.py:231
  13.4 2.5 %collective-permute-start.2 = (f32[8,128]{1,0:T(8,128)S(1)}, f32[8,128]{1,0:T(8,128)S(1)}, u32[]{:S(2)}, u32[]{:S(2)}) collective-permute-start(f32[8,128]{1,0:T(8,128)S(1)} %add.8.a_ref), channel_id=1, source_target_pairs={{0,1},{1,0},{2,3},{3,2},{4,5},{5,4},{6,7},{7,6},{8,9},{9,8},{10,11... | collective-permute-start | bytes 12296 | tf_op jit(solution)/shard_map/ppermute | solution.py:233
  14.8 5.0 %collective-permute-start.5 = (bf16[8,16,1024]{2,1,0:T(8,128)(2,1)S(1)}, bf16[8,16,1024]{2,1,0:T(8,128)(2,1)S(1)}, u32[]{:S(2)}, u32[]{:S(2)}) collective-permute-start(bf16[8,16,1024]{2,1,0:T(8,128)(2,1)S(1)} %get-tuple-element.19), channel_id=1, source_target_pairs={{0,8},{8,0},{16,24},{24,16},{32,40},{40,32},{48,56},{56,48},{64,72... | collective-permute-start | bytes 786440 | tf_op jit(solution)/shard_map/ppermute | solution.py:230
  15.9 16.6 %copy-start.3 = (f32[16,1024]{1,0:T(8,128)S(1)}, f32[16,1024]{1,0:T(8,128)}, u32[]{:S(2)}) copy-start(f32[16,1024]{1,0:T(8,128)} %fresh_ref.1) | copy-start | bytes 196612
  15.9 16.6 %copy-start.4 = (f32[16,1024]{1,0:T(8,128)S(1)}, f32[16,1024]{1,0:T(8,128)}, u32[]{:S(2)}) copy-start(f32[16,1024]{1,0:T(8,128)} %m1_ref.1) | copy-start | bytes 196612
  15.9 16.6 %copy-start.5 = (f32[16,1024]{1,0:T(8,128)S(1)}, f32[16,1024]{1,0:T(8,128)}, u32[]{:S(2)}) copy-start(f32[16,1024]{1,0:T(8,128)} %m2_ref.1) | copy-start | bytes 196612
  15.9 16.6 %copy-start.6 = (f32[16,1024]{1,0:T(8,128)S(1)}, f32[16,1024]{1,0:T(8,128)}, u32[]{:S(2)}) copy-start(f32[16,1024]{1,0:T(8,128)} %master_ref.1) | copy-start | bytes 196612
  15.9 3.8 %collective-permute-start.3 = (f32[8,128]{1,0:T(8,128)S(1)}, f32[8,128]{1,0:T(8,128)S(1)}, u32[]{:S(2)}, u32[]{:S(2)}) collective-permute-start(f32[8,128]{1,0:T(8,128)S(1)} %add.9.sums_ref), channel_id=1, source_target_pairs={{0,3},{1,2},{2,1},{3,0},{4,7},{5,6},{6,5},{7,4},{8,11},{9,10},{10,... | collective-permute-start | bytes 12296 | tf_op jit(solution)/shard_map/ppermute | solution.py:234
  41.9 6.2 %collective-permute-start.6 = (bf16[8,16,1024]{2,1,0:T(8,128)(2,1)S(1)}, bf16[8,16,1024]{2,1,0:T(8,128)(2,1)S(1)}, u32[]{:S(2)}, u32[]{:S(2)}) collective-permute-start(bf16[8,16,1024]{2,1,0:T(8,128)(2,1)S(1)} %all_to_all.11.own_ref), channel_id=1, source_target_pairs={{0,8},{8,0},{16,24},{24,16},{32,40},{40,32},{48,56},{56,48},{64,72... | collective-permute-start | bytes 786440 | tf_op jit(solution)/shard_map/ppermute | solution.py:241

commit v4 on v3

--- a/solution.py
+++ b/solution.py
@@ -27,36 +27,60 @@
     return jnp.sum(jnp.where(row == index, coef_ref[...], 0.0), axis=0, keepdims=True)
 
 
-def square_kernel(grads_ref, out_ref):
-    rows = []
-    for e in range(4):
+def square_kernel(grads_ref, out_ref, grads, sems):
+    n = grads.shape[0]
+    copies = [pltpu.make_async_copy(grads_ref.at[e], grads.at[e], sems.at[e]) for e in range(n)]
+    for copy in copies:
+        copy.start()
+    for e in range(n):
+        copies[e].wait()
         total = [jnp.zeros((16, 128), jnp.float32) for _ in range(4)]
         for r in range(16):
             for c in range(0, 1024, 128):
-                x = grads_ref[e, r // 2, r % 2, :, c : c + 128].astype(jnp.float32)
+                x = grads[e, r // 2, r % 2, :, c : c + 128].astype(jnp.float32)
                 total[(c // 128) % 4] = total[(c // 128) % 4] + x * x
         total = (total[0] + total[1]) + (total[2] + total[3])
-        rows.append(jnp.broadcast_to(jnp.sum(total), (1, 128)))
-    rows = jnp.concatenate(rows * 2, axis=0)
+        out_ref[e] = total[:8] + total[8:]
+
+
+def squares(per_example):
+    return pl.pallas_call(
+        square_kernel,
+        in_specs=[HBM],
+        out_specs=VM,
+        out_shape=jax.ShapeDtypeStruct((4, 8, 128), jnp.float32),
+        scratch_shapes=[
+            pltpu.VMEM(per_example.shape, per_example.dtype),
+            pltpu.SemaphoreType.DMA((per_example.shape[0],)),
+        ],
+        compiler_params=params(8),
+        cost_estimate=pl.CostEstimate(flops=1, bytes_accessed=2 * MIB, transcendentals=0),
+        name="squares",
+    )(pltpu.with_memory_space_constraint(per_example, pltpu.HBM))
+
+
+def place_kernel(squares_ref, out_ref):
+    rows = jnp.sum(squares_ref[...], axis=1)
+    rows = jnp.broadcast_to(jnp.sum(rows, axis=1, keepdims=True), rows.shape)
+    rows = jnp.concatenate([rows, rows], axis=0)
     core = lax.broadcasted_iota(jnp.int32, rows.shape, 0) // 4
     out_ref[...] = jnp.where(core == core_index(), rows, 0.0)
 
 
-def squares(per_example):
-    return pl.pallas_call(
-        square_kernel,
+def place(sums):
+    return pl.pallas_call(
+        place_kernel,
         in_specs=[VM],
         out_specs=VM,
         out_shape=jax.ShapeDtypeStruct((8, 128), jnp.float32),
-        compiler_params=params(8),
-        cost_estimate=pl.CostEstimate(flops=2**37, bytes_accessed=2 * MIB, transcendentals=0),
-        name="squares",
-    )(per_example)
-
-
-def past_kernel(table_ref, step_ref, cycle_ref, coef_ref, history_ref, _, keep_ref, send_ref, weight):
-    slots = history_ref.shape[0]
-    core = core_index()
+        compiler_params=params(4),
+        cost_estimate=pl.CostEstimate(flops=2**37, bytes_accessed=2**14, transcendentals=0),
+        name="place",
+    )(sums)
+
+
+def weights_kernel(table_ref, step_ref, cycle_ref, coef_ref, weight_ref, scalars_ref):
+    slots = weight_ref.shape[0]
     coefs = coef_row(coef_ref, table_ref[0])
     first = lax.axis_index("slot") * slots
     slot = first + lax.broadcasted_iota(jnp.int32, (slots, 1), 0)
@@ -64,33 +88,56 @@
     lane = lax.broadcasted_iota(jnp.int32, (slots, coefs.shape[1]), 1)
     picked = jnp.sum(jnp.where(lane == lag, coefs, 0.0), axis=1, keepdims=True)
     picked = jnp.where(lag <= step_ref[0], picked, 0.0)
-    weight[...] = jnp.broadcast_to(picked, weight.shape)
-
+    weight_ref[...] = jnp.broadcast_to(picked[:, :, None], weight_ref.shape)
+    row = lax.broadcasted_iota(jnp.int32, scalars_ref.shape, 0)
+    count = jnp.full((1, 1), step_ref[0] + 1, jnp.int32).astype(jnp.float32)
+    scalars_ref[...] = jnp.where(row == 0, coefs[:, 0:1], count)
+
+
+def slot_weights(table_index, step_number, cycle_slot, coef_table):
+    return pl.pallas_call(
+        weights_kernel,
+        in_specs=[SM] * 3 + [VM],
+        out_specs=(VM, VM),
+        out_shape=(
+            jax.ShapeDtypeStruct((16, 8, 128), jnp.float32),
+            jax.ShapeDtypeStruct((8, 128), jnp.float32),
+        ),
+        compiler_params=params(4),
+        cost_estimate=pl.CostEstimate(flops=1, bytes_accessed=1, transcendentals=0),
+        name="slot_weights",
+    )(table_index, step_number, cycle_slot, coef_table)
+
+
+def past_kernel(weight_ref, history_ref, _, keep_ref, send_ref):
+    slots = history_ref.shape[0]
+    core = core_index()
     for part, out_ref in ((1 - core, send_ref), (core, keep_ref)):
 
         @pl.loop(0, 8)
         def _(b, part=part, out_ref=out_ref):
+            scale = [weight_ref[s] for s in range(slots)]
             for r in (0, 8):
-                total = weight[0:1, :] * history_ref[0, b, part, r : r + 8, :]
-                for s in range(1, slots):
-                    total = total + weight[s : s + 1, :] * history_ref[s, b, part, r : r + 8, :]
-                out_ref[b, r : r + 8, :] = total.astype(out_ref.dtype)
-
-
-def past_parts(table_index, step_number, cycle_slot, coef_table, history, after):
+                for c in range(0, 1024, 128):
+                    total = scale[0] * history_ref[0, b, part, r : r + 8, c : c + 128]
+                    for s in range(1, slots):
+                        total = total + scale[s] * history_ref[s, b, part, r : r + 8, c : c + 128]
+                    out_ref[b, r : r + 8, c : c + 128] = total.astype(out_ref.dtype)
+
+
+def past_parts(weight, history, after):
     return pl.pallas_call(
         past_kernel,
-        in_specs=[SM] * 3 + [VM] * 2 + [HBM],
+        in_specs=[VM, VM, HBM],
         out_specs=(VM, VM),
         out_shape=(
             jax.ShapeDtypeStruct((8, 16, 1024), jnp.float32),
             jax.ShapeDtypeStruct((8, 16, 1024), jnp.bfloat16),
         ),
-        scratch_shapes=[pltpu.VMEM((16, 1024), jnp.float32)],
         compiler_params=params(4),
         cost_estimate=pl.CostEstimate(flops=1, bytes_accessed=1, transcendentals=0),
         name="past_parts",
-    )(table_index, step_number, cycle_slot, coef_table, history, after)
+    )(weight, history, after)
 
 
 def add_kernel(a_ref, b_ref, out_ref):
@@ -140,7 +187,7 @@
 
 
 def adam_kernel(
-    table_ref, step_ref, coef_ref, parts_ref, fresh_ref, m1_ref, m2_ref, master_ref,
+    scalars_ref, parts_ref, fresh_ref, m1_ref, m2_ref, master_ref,
     noise_out, m1_out, m2_out, master_out, weights_out,
 ):
     past = parts_ref[0, 0].astype(jnp.float32)
@@ -148,10 +195,10 @@
     for k in range(1, 8):
         past = past + parts_ref[k, 0].astype(jnp.float32)
         clipped = clipped + parts_ref[k, 1].astype(jnp.float32)
-    first = coef_row(coef_ref, table_ref[0])[:, 0:1]
+    first = scalars_ref[0:1, 0:1]
     new_noise = (fresh_ref[...] - past) / first
     noisy = clipped + new_noise
-    count = jnp.full((1, 1), step_ref[0] + 1, jnp.int32).astype(jnp.float32)
+    count = scalars_ref[1:2, 0:1]
     first_fix = 1.0 - jnp.power(jnp.float32(0.9), count)
     second_fix = 1.0 - jnp.power(jnp.float32(0.999), count)
     m1 = 0.9 * m1_ref[...] + 0.1 * noisy
@@ -167,17 +214,17 @@
         weights_out[k] = weights
 
 
-def adam(table_index, step_number, coef_table, parts, fresh, moment1, moment2, master):
+def adam(scalars, parts, fresh, moment1, moment2, master):
     row = jax.ShapeDtypeStruct(fresh.shape, jnp.float32)
     return pl.pallas_call(
         adam_kernel,
-        in_specs=[SM] * 2 + [VM] * 6,
+        in_specs=[VM] * 6,
         out_specs=(VM,) * 5,
         out_shape=(row, row, row, row, jax.ShapeDtypeStruct((8, 16, 1024), jnp.bfloat16)),
         compiler_params=params(8),
         cost_estimate=pl.CostEstimate(flops=MIB, bytes_accessed=2 * MIB, transcendentals=0),
         name="adam",
-    )(table_index, step_number, coef_table, parts, fresh, moment1, moment2, master)
+    )(scalars, parts, fresh, moment1, moment2, master)
 
 
 def weave_kernel(own_ref, other_ref, out_ref, sems):
@@ -216,26 +263,25 @@
 ):
     swap = [(i, i ^ 1) for i in range(16)]
     one_core = [[2 * k + c for k in range(8)] for c in range(2)]
-    near = [(i, i ^ 1) for i in range(8)]
-    far = [(i, i ^ 3) for i in range(8)]
-    across = [(i, i ^ 4) for i in range(8)]
+    both = "param"
+    across, near, far = ([(p, p ^ flip) for p in range(8)] for flip in (4, 1, 3))
     examples = per_example.reshape(4, 8, 2, 16, 1024)
-    sums = squares(examples)
+    sums = place(squares(examples))
     sums = sums + lax.ppermute(sums, "slot", swap)
+    weight, scalars = slot_weights(table_index, step_number, cycle_slot, coef_table)
     _, early = lax.optimization_barrier((sums, examples))
     other = lax.ppermute(early, "slot", swap)
-    keep, send = past_parts(
-        table_index, step_number, cycle_slot, coef_table, history.reshape(16, 8, 2, 16, 1024), sums
-    )
+    sums = sums + lax.ppermute(sums, both, across)
+    sums, weight = lax.optimization_barrier((sums, weight))
+    keep, send = past_parts(weight, history.reshape(16, 8, 2, 16, 1024), sums)
     got = lax.ppermute(send, "slot", swap)
-    sums = sums + lax.ppermute(sums, "param", across)
+    sums = add(sums, lax.ppermute(sums, both, near))
     sums, keep = lax.optimization_barrier((sums, keep))
-    sums = add(sums, lax.ppermute(sums, "param", near))
-    last = lax.ppermute(sums, "param", far)
+    last = lax.ppermute(sums, both, far)
     packed = pack(sums, last, examples, other, keep, got)
     parts = lax.all_to_all(packed, "slot", 0, 0, tiled=True, axis_index_groups=one_core)
     new_noise, m1, m2, master_new, weights = adam(
-        table_index, step_number, coef_table, parts, fresh, moment1, moment2, master
+        scalars, parts, fresh, moment1, moment2, master
     )
     gathered = lax.all_to_all(weights, "slot", 0, 0, tiled=True, axis_index_groups=one_core)
     gathered = weave(gathered, lax.ppermute(gathered, "slot", swap))

time: 49.1 us -> 47.1 us (0.959)
  local copies, waits for them, and re-layouts: 1.78 us -> 0.06 us
  starting transfers between devices: 15.5 us -> 14.1 us
  Pallas kernels: 4.79 us -> 5.48 us
    unnamed x22 -> x20, local copies, waits for them, and re-layouts: 1.78 us -> 0.06 us
    ppermute x3, starting transfers between devices: 7.87 us -> 7.07 us  [the longest x1 3.68 us: shards(): sums = sums + lax.ppermute(sums, both, across)]
    ppermute x1, starting transfers between devices: 5.05 us -> 4.32 us  [shards(): gathered = weave(gathered, lax.ppermute(gathered, 'slot', swap))]
    pallas_call x3 -> x5, Pallas kernels: 3.38 us -> 4.07 us  [the longest x1 1.81 us: squares(): pl.pallas_call(square_kernel, in_specs=[HBM], out_specs=VM, out_shape=jax...]
  transfers between devices with their start and end apart: 7 -> 7, of which waited for: 4 -> 3; matrix products, arithmetic and copies ran while one was open for 0% -> 0% of each run, Pallas kernels for 4% -> 3%
where the time goes in v4:
time: 47.1 us; the launch traced here: 46.9 us
  blocking collectives  20.8 us (44%)
  starting transfers between devices  14.1 us (30%)
  Pallas kernels  5.48 us (12%)
  waiting for transfers between devices  3.73 us (8%)
  between operations  2.72 us (6%)
    all_to_all x1, blocking collectives, shards(): lax.all_to_all(packed, 'slot', 0, 0, tiled=True, axis_index_groups=one_core)  12.2 us
    all_to_all x1, blocking collectives, shards(): lax.all_to_all(weights, 'slot', 0, 0, tiled=True, axis_index_groups=one_c...  8.61 us
    ppermute x1, starting transfers between devices, shards(): gathered = weave(gathered, lax.ppermute(gathered, 'slot', swap))  4.32 us
    ppermute x1, starting transfers between devices, shards(): sums = sums + lax.ppermute(sums, both, across)  3.68 us
    ppermute x1, starting transfers between devices, shards(): last = lax.ppermute(sums, both, far)  2.01 us
    pallas_call x1, Pallas kernels, squares(): pl.pallas_call(square_kernel, in_specs=[HBM], out_specs=VM, out_shape=jax...  1.81 us
    ppermute x1, waiting for transfers between devices, shards(): last = lax.ppermute(sums, both, far)  1.74 us
    ppermute x1, starting transfers between devices, shards(): sums = sums + lax.ppermute(sums, 'slot', swap)  1.44 us
  transfers between devices with their start and end apart: 7, of which 3 were waited for; matrix products, arithmetic and copies ran while one was open for 0% of the time, Pallas kernels for 3%

profile of v4, /device:TPU:1, one launch (start us, length us, event | category | flops | bytes accessed | tf_op | source)
XLA Modules:
  0.0 46.9 jit_solution(13372245280663398261)
XLA Ops:
  0.6 0.0 slice-start
  0.6 1.8 %squares.1.squares_ref = f32[4,8,128]{2,1,0:T(8,128)S(1)} custom-call(bf16[4,8,2,16,1024]{4,3,2,1,0:T(8,128)(2,1)} %bitcast.6), custom_call_target="tpu_custom_call" | custom-call | flops 1 | bytes 2097152 | tf_op jit(solution)/shard_map/squares/pallas_call | solution.py:47
  2.5 0.0 copy-start
  2.5 0.0 copy-start.1
  2.5 0.0 slice-start.1
  2.5 0.0 slice-start.2
  2.5 0.0 slice-start.3
  2.5 0.1 place.1
  2.6 1.4 %collective-permute-start = (f32[8,128]{1,0:T(8,128)S(1)}, f32[8,128]{1,0:T(8,128)S(1)}, u32[]{:S(2)}, u32[]{:S(2)}) collective-permute-start(f32[8,128]{1,0:T(8,128)S(1)} %place.1), channel_id=1, source_target_pairs={{0,8},{8,0},{16,24},{24,16},{32,40},{40,32},{48,56},{56,48},{64,72... | collective-permute-start | bytes 12296 | tf_op jit(solution)/shard_map/ppermute | solution.py:270
  4.0 0.8 %collective-permute-done = f32[8,128]{1,0:T(8,128)S(1)} collective-permute-done((f32[8,128]{1,0:T(8,128)S(1)}, f32[8,128]{1,0:T(8,128)S(1)}, u32[]{:S(2)}, u32[]{:S(2)}) %collective-permute-start) | collective-permute-done | bytes 4128 | tf_op jit(solution)/shard_map/ppermute | solution.py:270
  4.9 0.7 %collective-permute-start.4 = (bf16[4,8,2,16,1024]{4,3,2,1,0:T(8,128)(2,1)S(1)}, bf16[4,8,2,16,1024]{4,3,2,1,0:T(8,128)(2,1)S(1)}, u32[]{:S(2)}, u32[]{:S(2)}) collective-permute-start(bf16[4,8,2,16,1024]{4,3,2,1,0:T(8,128)(2,1)S(1)} %bitcast.7), channel_id=1, source_target_pairs={{0,8},{8,0},{16,24},{24,16},{32,40},{40,32},{48,56},{56,48},{64,72... | collective-permute-start | bytes 6291464 | tf_op jit(solution)/shard_map/ppermute | solution.py:273
  5.5 3.7 %collective-permute-start.1 = (f32[8,128]{1,0:T(8,128)S(1)}, f32[8,128]{1,0:T(8,128)S(1)}, u32[]{:S(2)}, u32[]{:S(2)}) collective-permute-start(f32[8,128]{1,0:T(8,128)S(1)} %add.7), channel_id=1, source_target_pairs={{0,4},{1,5},{2,6},{3,7},{4,0},{5,1},{6,2},{7,3},{8,12},{9,13},{10,... | collective-permute-start | bytes 12296 | tf_op jit(solution)/shard_map/ppermute | solution.py:274
  11.2 0.1 slot_weights.1
  11.3 0.0 collective-permute-done.1
  11.3 1.4 %collective-permute-start.2 = (f32[8,128]{1,0:T(8,128)S(1)}, f32[8,128]{1,0:T(8,128)S(1)}, u32[]{:S(2)}, u32[]{:S(2)}) collective-permute-start(f32[8,128]{1,0:T(8,128)S(1)} %add.8.a_ref._), channel_id=1, source_target_pairs={{0,1},{1,0},{2,3},{3,2},{4,5},{5,4},{6,7},{7,6},{8,9},{9,8},{10,11... | collective-permute-start | bytes 12296 | tf_op jit(solution)/shard_map/ppermute | solution.py:278
  12.7 1.3 %past_parts.1 = (f32[8,16,1024]{2,1,0:T(8,128)S(1)}, bf16[8,16,1024]{2,1,0:T(8,128)(2,1)S(1)}) custom-call(f32[16,8,128]{2,1,0:T(8,128)S(1)} %get-tuple-element.22.weight_ref, f32[16,8,2,16,1024]{4,3,2,1,0:T(8,128)S(1)} %bitcast.5, f32[8,128]{1,0:T(8,128)S(1)} %add.8.a_ref._), custom_call_target="tpu_custom_call" | custom-call | flops 1 | bytes 1 | tf_op jit(solution)/shard_map/past_parts/pallas_call | solution.py:129
  14.0 0.6 %collective-permute-start.5 = (bf16[8,16,1024]{2,1,0:T(8,128)(2,1)S(1)}, bf16[8,16,1024]{2,1,0:T(8,128)(2,1)S(1)}, u32[]{:S(2)}, u32[]{:S(2)}) collective-permute-start(bf16[8,16,1024]{2,1,0:T(8,128)(2,1)S(1)} %get-tuple-element.27), channel_id=1, source_target_pairs={{0,8},{8,0},{16,24},{24,16},{32,40},{40,32},{48,56},{56,48},{64,72... | collective-permute-start | bytes 786440 | tf_op jit(solution)/shard_map/ppermute | solution.py:277
  14.6 0.0 collective-permute-done.2.b_ref
  14.6 0.0 copy-start.3
  14.6 0.0 copy-start.4
  14.7 0.0 copy-start.5
  14.7 2.0 %collective-permute-start.3 = (f32[8,128]{1,0:T(8,128)S(1)}, f32[8,128]{1,0:T(8,128)S(1)}, u32[]{:S(2)}, u32[]{:S(2)}) collective-permute-start(f32[8,128]{1,0:T(8,128)S(1)} %add.9.sums_ref), channel_id=1, source_target_pairs={{0,3},{1,2},{2,1},{3,0},{4,7},{5,6},{6,5},{7,4},{8,11},{9,10},{10,... | collective-permute-start | bytes 12296 | tf_op jit(solution)/shard_map/ppermute | solution.py:280
  16.7 1.7 %collective-permute-done.3.last_ref = f32[8,128]{1,0:T(8,128)S(1)} collective-permute-done((f32[8,128]{1,0:T(8,128)S(1)}, f32[8,128]{1,0:T(8,128)S(1)}, u32[]{:S(2)}, u32[]{:S(2)}) %collective-permute-start.3) | collective-permute-done | bytes 4128 | tf_op jit(solution)/shard_map/ppermute | solution.py:280
  18.4 0.0 collective-permute-done.5.got_ref
  18.4 0.0 collective-permute-done.4.other_ref
  18.4 0.6 %pack.1 = bf16[8,2,16,1024]{3,2,1,0:T(8,128)(2,1)S(1)} custom-call(f32[8,128]{1,0:T(8,128)S(1)} %add.9.sums_ref, f32[8,128]{1,0:T(8,128)S(1)} %collective-permute-done.3.last_ref, bf16[4,8,2,16,1024]{4,3,2,1,0:T(8,128)(2,1)S(1)} %bitcast.8, bf16[4,8,2,16,1024]{4,3,2,1,0:T(8,128)(2,1)S(1)} %collective-permute-done.4.other_ref, ...), custom_call_target="tpu_custom_call" | custom-call | flops 4194304 | bytes 5242880 | tf_op jit(solution)/shard_map/pack/pallas_call | solution.py:177
  19.0 12.2 %all_to_all.10.parts_ref = bf16[8,2,16,1024]{3,2,1,0:T(8,128)(2,1)S(1)} all-to-all(bf16[8,2,16,1024]{3,2,1,0:T(8,128)(2,1)S(1)} %pack.1), channel_id=1, replica_groups={{0,16,32,48,64,80,96,112},{8,24,40,56,72,88,104,120},{1,17,33,49,65,81,..., dimensions={0} | all-to-all | bytes 1048576 | tf_op jit(solution)/shard_map/all_to_all | solution.py:282
  31.2 0.8 %adam.1 = (f32[16,1024]{1,0:T(8,128)}, f32[16,1024]{1,0:T(8,128)}, f32[16,1024]{1,0:T(8,128)}, f32[16,1024]{1,0:T(8,128)}, bf16[8,16,1024]{2,1,0:T(8,128)(2,1)S(1)}) custom-call(f32[8,128]{1,0:T(8,128)S(1)} %get-tuple-element.19.scalars_ref, bf16[8,2,16,1024]{3,2,1,0:T(8,128)(2,1)S(1)} %all_to_all.10.parts_ref, f32[16,1024]{1,0:T(8,128)S(1)} %copy-done.2, ...), custom_call_target="tpu_custom_call" | custom-call | flops 1048576 | bytes 2097152 | tf_op jit(solution)/shard_map/adam/pallas_call | solution.py:219
  32.0 8.6 %all_to_all.11.own_ref = bf16[8,16,1024]{2,1,0:T(8,128)(2,1)S(1)} all-to-all(bf16[8,16,1024]{2,1,0:T(8,128)(2,1)S(1)} %get-tuple-element.32), channel_id=1, replica_groups={{0,16,32,48,64,80,96,112},{8,24,40,56,72,88,104,120},{1,17,33,49,65,81,..., dimensions={0} | all-to-all | bytes 524288 | tf_op jit(solution)/shard_map/all_to_all | solution.py:286
  40.6 4.3 %collective-permute-start.6 = (bf16[8,16,1024]{2,1,0:T(8,128)(2,1)S(1)}, bf16[8,16,1024]{2,1,0:T(8,128)(2,1)S(1)}, u32[]{:S(2)}, u32[]{:S(2)}) collective-permute-start(bf16[8,16,1024]{2,1,0:T(8,128)(2,1)S(1)} %all_to_all.11.own_ref), channel_id=1, source_target_pairs={{0,8},{8,0},{16,24},{24,16},{32,40},{40,32},{48,56},{56,48},{64,72... | collective-permute-start | bytes 786440 | tf_op jit(solution)/shard_map/ppermute | solution.py:287
  45.0 1.2 %collective-permute-done.6.other_ref = bf16[8,16,1024]{2,1,0:T(8,128)(2,1)S(1)} collective-permute-done((bf16[8,16,1024]{2,1,0:T(8,128)(2,1)S(1)}, bf16[8,16,1024]{2,1,0:T(8,128)(2,1)S(1)}, u32[]{:S(2)}, u32[]{:S(2)}) %collective-permute-start.6) | collective-permute-done | bytes 262176 | tf_op jit(solution)/shard_map/ppermute | solution.py:287
  46.1 0.8 %weave.1 = bf16[8,2,16,1024]{3,2,1,0:T(8,128)(2,1)} custom-call(bf16[8,16,1024]{2,1,0:T(8,128)(2,1)S(1)} %all_to_all.11.own_ref, bf16[8,16,1024]{2,1,0:T(8,128)(2,1)S(1)} %collective-permute-done.6.other_ref), custom_call_target="tpu_custom_call" | custom-call | tf_op jit(solution)/shard_map/weave/pallas_call | solution.py:241
  (15 shorter events, 0.0 us)
Async XLA Ops:
  0.6 12.0 %slice-start = ((s8[16777216]{0:T(1024)(128)(4,1)}), s8[4194304]{0:T(1024)(128)(4,1)S(1)}, s32[]{:S(2)}) async-start(s8[16777216]{0:T(1024)(128)(4,1)} %bitcast.3), calls=%async_computation.2 | async-start | bytes 8388608
  2.5 2.4 %copy-start = (bf16[4,256,1024]{2,1,0:T(8,128)(2,1)S(1)}, bf16[4,256,1024]{2,1,0:T(8,128)(2,1)}, u32[]{:S(2)}) copy-start(bf16[4,256,1024]{2,1,0:T(8,128)(2,1)} %param.11) | copy-start | bytes 6291460
  2.5 8.7 %copy-start.1 = (f32[64,257]{1,0:T(8,128)S(1)}, f32[64,257]{1,0:T(8,128)}, u32[]{:S(2)}) copy-start(f32[64,257]{1,0:T(8,128)} %coef_ref.1) | copy-start | bytes 197380
  2.5 10.2 %slice-start.1 = ((s8[16777216]{0:T(1024)(128)(4,1)}), s8[4194304]{0:T(1024)(128)(4,1)S(1)}, s32[]{:S(2)}) async-start(s8[16777216]{0:T(1024)(128)(4,1)} %bitcast.3), calls=%async_computation.3 | async-start | bytes 8388608
  2.5 10.2 %slice-start.2 = ((s8[16777216]{0:T(1024)(128)(4,1)}), s8[4194304]{0:T(1024)(128)(4,1)S(1)}, s32[]{:S(2)}) async-start(s8[16777216]{0:T(1024)(128)(4,1)} %bitcast.3), calls=%async_computation.4 | async-start | bytes 8388608
  2.5 10.2 %slice-start.3 = ((s8[16777216]{0:T(1024)(128)(4,1)}), s8[4194304]{0:T(1024)(128)(4,1)S(1)}, s32[]{:S(2)}) async-start(s8[16777216]{0:T(1024)(128)(4,1)} %bitcast.3), calls=%async_computation.5 | async-start | bytes 8388608
  2.6 2.3 %collective-permute-start = (f32[8,128]{1,0:T(8,128)S(1)}, f32[8,128]{1,0:T(8,128)S(1)}, u32[]{:S(2)}, u32[]{:S(2)}) collective-permute-start(f32[8,128]{1,0:T(8,128)S(1)} %place.1), channel_id=1, source_target_pairs={{0,8},{8,0},{16,24},{24,16},{32,40},{40,32},{48,56},{56,48},{64,72... | collective-permute-start | bytes 12296 | tf_op jit(solution)/shard_map/ppermute | solution.py:270
  4.9 13.5 %collective-permute-start.4 = (bf16[4,8,2,16,1024]{4,3,2,1,0:T(8,128)(2,1)S(1)}, bf16[4,8,2,16,1024]{4,3,2,1,0:T(8,128)(2,1)S(1)}, u32[]{:S(2)}, u32[]{:S(2)}) collective-permute-start(bf16[4,8,2,16,1024]{4,3,2,1,0:T(8,128)(2,1)S(1)} %bitcast.7), channel_id=1, source_target_pairs={{0,8},{8,0},{16,24},{24,16},{32,40},{40,32},{48,56},{56,48},{64,72... | collective-permute-start | bytes 6291464 | tf_op jit(solution)/shard_map/ppermute | solution.py:273
  5.5 5.7 %collective-permute-start.1 = (f32[8,128]{1,0:T(8,128)S(1)}, f32[8,128]{1,0:T(8,128)S(1)}, u32[]{:S(2)}, u32[]{:S(2)}) collective-permute-start(f32[8,128]{1,0:T(8,128)S(1)} %add.7), channel_id=1, source_target_pairs={{0,4},{1,5},{2,6},{3,7},{4,0},{5,1},{6,2},{7,3},{8,12},{9,13},{10,... | collective-permute-start | bytes 12296 | tf_op jit(solution)/shard_map/ppermute | solution.py:274
  11.3 3.3 %collective-permute-start.2 = (f32[8,128]{1,0:T(8,128)S(1)}, f32[8,128]{1,0:T(8,128)S(1)}, u32[]{:S(2)}, u32[]{:S(2)}) collective-permute-start(f32[8,128]{1,0:T(8,128)S(1)} %add.8.a_ref._), channel_id=1, source_target_pairs={{0,1},{1,0},{2,3},{3,2},{4,5},{5,4},{6,7},{7,6},{8,9},{9,8},{10,11... | collective-permute-start | bytes 12296 | tf_op jit(solution)/shard_map/ppermute | solution.py:278
  14.0 4.4 %collective-permute-start.5 = (bf16[8,16,1024]{2,1,0:T(8,128)(2,1)S(1)}, bf16[8,16,1024]{2,1,0:T(8,128)(2,1)S(1)}, u32[]{:S(2)}, u32[]{:S(2)}) collective-permute-start(bf16[8,16,1024]{2,1,0:T(8,128)(2,1)S(1)} %get-tuple-element.27), channel_id=1, source_target_pairs={{0,8},{8,0},{16,24},{24,16},{32,40},{40,32},{48,56},{56,48},{64,72... | collective-permute-start | bytes 786440 | tf_op jit(solution)/shard_map/ppermute | solution.py:277
  14.6 16.6 %copy-start.2 = (f32[16,1024]{1,0:T(8,128)S(1)}, f32[16,1024]{1,0:T(8,128)}, u32[]{:S(2)}) copy-start(f32[16,1024]{1,0:T(8,128)} %fresh_ref.1) | copy-start | bytes 196612
  14.6 16.6 %copy-start.3 = (f32[16,1024]{1,0:T(8,128)S(1)}, f32[16,1024]{1,0:T(8,128)}, u32[]{:S(2)}) copy-start(f32[16,1024]{1,0:T(8,128)} %m1_ref.1) | copy-start | bytes 196612
  14.6 16.6 %copy-start.4 = (f32[16,1024]{1,0:T(8,128)S(1)}, f32[16,1024]{1,0:T(8,128)}, u32[]{:S(2)}) copy-start(f32[16,1024]{1,0:T(8,128)} %m2_ref.1) | copy-start | bytes 196612
  14.7 16.6 %copy-start.5 = (f32[16,1024]{1,0:T(8,128)S(1)}, f32[16,1024]{1,0:T(8,128)}, u32[]{:S(2)}) copy-start(f32[16,1024]{1,0:T(8,128)} %master_ref.1) | copy-start | bytes 196612
  14.7 3.7 %collective-permute-start.3 = (f32[8,128]{1,0:T(8,128)S(1)}, f32[8,128]{1,0:T(8,128)S(1)}, u32[]{:S(2)}, u32[]{:S(2)}) collective-permute-start(f32[8,128]{1,0:T(8,128)S(1)} %add.9.sums_ref), channel_id=1, source_target_pairs={{0,3},{1,2},{2,1},{3,0},{4,7},{5,6},{6,5},{7,4},{8,11},{9,10},{10,... | collective-permute-start | bytes 12296 | tf_op jit(solution)/shard_map/ppermute | solution.py:280
  40.6 5.5 %collective-permute-start.6 = (bf16[8,16,1024]{2,1,0:T(8,128)(2,1)S(1)}, bf16[8,16,1024]{2,1,0:T(8,128)(2,1)S(1)}, u32[]{:S(2)}, u32[]{:S(2)}) collective-permute-start(bf16[8,16,1024]{2,1,0:T(8,128)(2,1)S(1)} %all_to_all.11.own_ref), channel_id=1, source_target_pairs={{0,8},{8,0},{16,24},{24,16},{32,40},{40,32},{48,56},{56,48},{64,72... | collective-permute-start | bytes 786440 | tf_op jit(solution)/shard_map/ppermute | solution.py:287

commit v5 on v4

--- a/solution.py
+++ b/solution.py
@@ -227,26 +227,48 @@
     )(scalars, parts, fresh, moment1, moment2, master)
 
 
-def weave_kernel(own_ref, other_ref, out_ref, sems):
-    core = core_index()
-    a = pltpu.make_async_copy(own_ref, out_ref.at[:, core], sems.at[0])
-    b = pltpu.make_async_copy(other_ref, out_ref.at[:, 1 - core], sems.at[1])
-    a.start()
-    b.start()
-    a.wait()
-    b.wait()
-
-
-def weave(own, other):
+def store_kernel(own_ref, *refs):
+    rows, out_ref, stored, sems = refs[:4], refs[4], refs[5:9], refs[9]
+    copies = [pltpu.make_async_copy(own_ref, out_ref.at[:, core_index()], sems.at[0])]
+    for k in range(4):
+        copies.append(pltpu.make_async_copy(rows[k], stored[k], sems.at[1 + k]))
+    for copy in copies:
+        copy.start()
+    for copy in copies:
+        copy.wait()
+
+
+def store(own, rows):
+    row = jax.ShapeDtypeStruct(rows[0].shape, rows[0].dtype)
+    return pl.pallas_call(
+        store_kernel,
+        in_specs=[VM] * 5,
+        out_specs=(HBM,) * 5,
+        out_shape=(jax.ShapeDtypeStruct((8, 2, 16, 1024), jnp.bfloat16), row, row, row, row),
+        scratch_shapes=[pltpu.SemaphoreType.DMA((5,))],
+        compiler_params=params(4),
+        cost_estimate=pl.CostEstimate(flops=1, bytes_accessed=2**20, transcendentals=0),
+        name="store",
+    )(own, *rows)
+
+
+def weave_kernel(other_ref, _, out_ref, sem):
+    copy = pltpu.make_async_copy(other_ref, out_ref.at[:, 1 - core_index()], sem)
+    copy.start()
+    copy.wait()
+
+
+def weave(other, woven):
     return pl.pallas_call(
         weave_kernel,
-        in_specs=[HBM, HBM],
+        in_specs=[VM, HBM],
         out_specs=HBM,
-        out_shape=jax.ShapeDtypeStruct((8, 2, 16, 1024), jnp.bfloat16),
-        scratch_shapes=[pltpu.SemaphoreType.DMA((2,))],
+        out_shape=jax.ShapeDtypeStruct(woven.shape, woven.dtype),
+        input_output_aliases={1: 0},
+        scratch_shapes=[pltpu.SemaphoreType.DMA],
         compiler_params=params(4),
         name="weave",
-    )(own, other)
+    )(other, woven)
 
 
 def shards(
@@ -284,8 +306,9 @@
         scalars, parts, fresh, moment1, moment2, master
     )
     gathered = lax.all_to_all(weights, "slot", 0, 0, tiled=True, axis_index_groups=one_core)
-    gathered = weave(gathered, lax.ppermute(gathered, "slot", swap))
-    return (new_noise, m1, m2, master_new, gathered.reshape(256, 1024))
+    other_rows = lax.ppermute(gathered, "slot", swap)
+    woven, *rows = store(gathered, (new_noise, m1, m2, master_new))
+    return (*rows, weave(other_rows, woven).reshape(256, 1024))
 
 
 def solution(mesh):

time: 47.1 us -> 46.4 us (0.985)
  waiting for transfers between devices: 3.73 us -> 2.9 us
    ppermute x1, waiting for transfers between devices: 1.16 us -> 0.33 us  [shards(): other_rows = lax.ppermute(gathered, 'slot', swap)]
    pallas_call x1 -> x2, Pallas kernels: 0.8 us -> 1.53 us  [the longest x1 0.82 us: store(): pl.pallas_call(store_kernel, in_specs=[VM] * 5, out_specs=(HBM,) * 5, out...]
    pallas_call x1, Pallas kernels: 0.8 us -> 0.16 us  [adam(): pl.pallas_call(adam_kernel, in_specs=[VM] * 6, out_specs=(VM,) * 5, out_s...]
  transfers between devices with their start and end apart: 7 -> 7, of which waited for: 3 -> 3; matrix products, arithmetic and copies ran while one was open for 0% -> 0% of each run, Pallas kernels for 3% -> 5%
where the time goes in v5:
time: 46.4 us; the launch traced here: 46.2 us
  blocking collectives  20.8 us (45%)
  starting transfers between devices  14.1 us (30%)
  Pallas kernels  5.58 us (12%)
  waiting for transfers between devices  2.9 us (6%)
  between operations  2.74 us (6%)
    all_to_all x1, blocking collectives, shards(): lax.all_to_all(packed, 'slot', 0, 0, tiled=True, axis_index_groups=one_core)  12.2 us
    all_to_all x1, blocking collectives, shards(): lax.all_to_all(weights, 'slot', 0, 0, tiled=True, axis_index_groups=one_c...  8.62 us
    ppermute x1, starting transfers between devices, shards(): other_rows = lax.ppermute(gathered, 'slot', swap)  4.32 us
    ppermute x1, starting transfers between devices, shards(): sums = sums + lax.ppermute(sums, both, across)  3.68 us
    ppermute x1, starting transfers between devices, shards(): last = lax.ppermute(sums, both, far)  2.01 us
    pallas_call x1, Pallas kernels, squares(): pl.pallas_call(square_kernel, in_specs=[HBM], out_specs=VM, out_shape=jax...  1.81 us
    ppermute x1, waiting for transfers between devices, shards(): last = lax.ppermute(sums, both, far)  1.74 us
    ppermute x1, starting transfers between devices, shards(): sums = sums + lax.ppermute(sums, 'slot', swap)  1.44 us
  transfers between devices with their start and end apart: 7, of which 3 were waited for; matrix products, arithmetic and copies ran while one was open for 0% of the time, Pallas kernels for 5%

profile of v5, /device:TPU:1, one launch (start us, length us, event | category | flops | bytes accessed | tf_op | source)
XLA Modules:
  0.0 46.2 jit_solution(3125995702423411263)
XLA Ops:
  0.6 0.0 slice-start
  0.6 1.8 %squares.1.squares_ref = f32[4,8,128]{2,1,0:T(8,128)S(1)} custom-call(bf16[4,8,2,16,1024]{4,3,2,1,0:T(8,128)(2,1)} %bitcast.6), custom_call_target="tpu_custom_call" | custom-call | flops 1 | bytes 2097152 | tf_op jit(solution)/shard_map/squares/pallas_call | solution.py:47
  2.5 0.0 copy-start
  2.5 0.0 copy-start.1
  2.5 0.0 slice-start.1
  2.5 0.0 slice-start.2
  2.5 0.0 slice-start.3
  2.5 0.1 place.1
  2.6 1.4 %collective-permute-start = (f32[8,128]{1,0:T(8,128)S(1)}, f32[8,128]{1,0:T(8,128)S(1)}, u32[]{:S(2)}, u32[]{:S(2)}) collective-permute-start(f32[8,128]{1,0:T(8,128)S(1)} %place.1), channel_id=1, source_target_pairs={{0,8},{8,0},{16,24},{24,16},{32,40},{40,32},{48,56},{56,48},{64,72... | collective-permute-start | bytes 12296 | tf_op jit(solution)/shard_map/ppermute | solution.py:292
  4.0 0.8 %collective-permute-done = f32[8,128]{1,0:T(8,128)S(1)} collective-permute-done((f32[8,128]{1,0:T(8,128)S(1)}, f32[8,128]{1,0:T(8,128)S(1)}, u32[]{:S(2)}, u32[]{:S(2)}) %collective-permute-start) | collective-permute-done | bytes 4128 | tf_op jit(solution)/shard_map/ppermute | solution.py:292
  4.9 0.7 %collective-permute-start.4 = (bf16[4,8,2,16,1024]{4,3,2,1,0:T(8,128)(2,1)S(1)}, bf16[4,8,2,16,1024]{4,3,2,1,0:T(8,128)(2,1)S(1)}, u32[]{:S(2)}, u32[]{:S(2)}) collective-permute-start(bf16[4,8,2,16,1024]{4,3,2,1,0:T(8,128)(2,1)S(1)} %bitcast.7), channel_id=1, source_target_pairs={{0,8},{8,0},{16,24},{24,16},{32,40},{40,32},{48,56},{56,48},{64,72... | collective-permute-start | bytes 6291464 | tf_op jit(solution)/shard_map/ppermute | solution.py:295
  5.5 3.7 %collective-permute-start.1 = (f32[8,128]{1,0:T(8,128)S(1)}, f32[8,128]{1,0:T(8,128)S(1)}, u32[]{:S(2)}, u32[]{:S(2)}) collective-permute-start(f32[8,128]{1,0:T(8,128)S(1)} %add.7), channel_id=1, source_target_pairs={{0,4},{1,5},{2,6},{3,7},{4,0},{5,1},{6,2},{7,3},{8,12},{9,13},{10,... | collective-permute-start | bytes 12296 | tf_op jit(solution)/shard_map/ppermute | solution.py:296
  11.2 0.1 slot_weights.1
  11.3 0.0 collective-permute-done.1
  11.3 1.4 %collective-permute-start.2 = (f32[8,128]{1,0:T(8,128)S(1)}, f32[8,128]{1,0:T(8,128)S(1)}, u32[]{:S(2)}, u32[]{:S(2)}) collective-permute-start(f32[8,128]{1,0:T(8,128)S(1)} %add.8.a_ref._), channel_id=1, source_target_pairs={{0,1},{1,0},{2,3},{3,2},{4,5},{5,4},{6,7},{7,6},{8,9},{9,8},{10,11... | collective-permute-start | bytes 12296 | tf_op jit(solution)/shard_map/ppermute | solution.py:300
  12.7 1.3 %past_parts.1 = (f32[8,16,1024]{2,1,0:T(8,128)S(1)}, bf16[8,16,1024]{2,1,0:T(8,128)(2,1)S(1)}) custom-call(f32[16,8,128]{2,1,0:T(8,128)S(1)} %get-tuple-element.27.weight_ref, f32[16,8,2,16,1024]{4,3,2,1,0:T(8,128)S(1)} %bitcast.5, f32[8,128]{1,0:T(8,128)S(1)} %add.8.a_ref._), custom_call_target="tpu_custom_call" | custom-call | flops 1 | bytes 1 | tf_op jit(solution)/shard_map/past_parts/pallas_call | solution.py:129
  14.0 0.6 %collective-permute-start.5 = (bf16[8,16,1024]{2,1,0:T(8,128)(2,1)S(1)}, bf16[8,16,1024]{2,1,0:T(8,128)(2,1)S(1)}, u32[]{:S(2)}, u32[]{:S(2)}) collective-permute-start(bf16[8,16,1024]{2,1,0:T(8,128)(2,1)S(1)} %get-tuple-element.32), channel_id=1, source_target_pairs={{0,8},{8,0},{16,24},{24,16},{32,40},{40,32},{48,56},{56,48},{64,72... | collective-permute-start | bytes 786440 | tf_op jit(solution)/shard_map/ppermute | solution.py:299
  14.6 0.0 collective-permute-done.2.b_ref
  14.6 0.0 copy-start.3
  14.6 0.0 copy-start.4
  14.7 0.0 copy-start.5
  14.7 2.0 %collective-permute-start.3 = (f32[8,128]{1,0:T(8,128)S(1)}, f32[8,128]{1,0:T(8,128)S(1)}, u32[]{:S(2)}, u32[]{:S(2)}) collective-permute-start(f32[8,128]{1,0:T(8,128)S(1)} %add.9.sums_ref), channel_id=1, source_target_pairs={{0,3},{1,2},{2,1},{3,0},{4,7},{5,6},{6,5},{7,4},{8,11},{9,10},{10,... | collective-permute-start | bytes 12296 | tf_op jit(solution)/shard_map/ppermute | solution.py:302
  16.7 1.7 %collective-permute-done.3.last_ref = f32[8,128]{1,0:T(8,128)S(1)} collective-permute-done((f32[8,128]{1,0:T(8,128)S(1)}, f32[8,128]{1,0:T(8,128)S(1)}, u32[]{:S(2)}, u32[]{:S(2)}) %collective-permute-start.3) | collective-permute-done | bytes 4128 | tf_op jit(solution)/shard_map/ppermute | solution.py:302
  18.4 0.0 collective-permute-done.5.got_ref
  18.4 0.6 %pack.1 = bf16[8,2,16,1024]{3,2,1,0:T(8,128)(2,1)S(1)} custom-call(f32[8,128]{1,0:T(8,128)S(1)} %add.9.sums_ref, f32[8,128]{1,0:T(8,128)S(1)} %collective-permute-done.3.last_ref, bf16[4,8,2,16,1024]{4,3,2,1,0:T(8,128)(2,1)S(1)} %bitcast.8, bf16[4,8,2,16,1024]{4,3,2,1,0:T(8,128)(2,1)S(1)} %collective-permute-done.4.other_ref, ...), custom_call_target="tpu_custom_call" | custom-call | flops 4194304 | bytes 5242880 | tf_op jit(solution)/shard_map/pack/pallas_call | solution.py:177
  19.0 12.2 %all_to_all.10.parts_ref = bf16[8,2,16,1024]{3,2,1,0:T(8,128)(2,1)S(1)} all-to-all(bf16[8,2,16,1024]{3,2,1,0:T(8,128)(2,1)S(1)} %pack.1), channel_id=1, replica_groups={{0,16,32,48,64,80,96,112},{8,24,40,56,72,88,104,120},{1,17,33,49,65,81,..., dimensions={0} | all-to-all | bytes 1048576 | tf_op jit(solution)/shard_map/all_to_all | solution.py:304
  31.2 0.2 adam.1
  31.4 8.6 %all_to_all.11.own_ref = bf16[8,16,1024]{2,1,0:T(8,128)(2,1)S(1)} all-to-all(bf16[8,16,1024]{2,1,0:T(8,128)(2,1)S(1)} %get-tuple-element.33), channel_id=1, replica_groups={{0,16,32,48,64,80,96,112},{8,24,40,56,72,88,104,120},{1,17,33,49,65,81,..., dimensions={0} | all-to-all | bytes 524288 | tf_op jit(solution)/shard_map/all_to_all | solution.py:308
  40.0 4.3 %collective-permute-start.6 = (bf16[8,16,1024]{2,1,0:T(8,128)(2,1)S(1)}, bf16[8,16,1024]{2,1,0:T(8,128)(2,1)S(1)}, u32[]{:S(2)}, u32[]{:S(2)}) collective-permute-start(bf16[8,16,1024]{2,1,0:T(8,128)(2,1)S(1)} %all_to_all.11.own_ref), channel_id=1, source_target_pairs={{0,8},{8,0},{16,24},{24,16},{32,40},{40,32},{48,56},{56,48},{64,72... | collective-permute-start | bytes 786440 | tf_op jit(solution)/shard_map/ppermute | solution.py:309
  44.4 0.8 %store.1 = (bf16[8,2,16,1024]{3,2,1,0:T(8,128)(2,1)}, f32[16,1024]{1,0:T(8,128)}, f32[16,1024]{1,0:T(8,128)}, f32[16,1024]{1,0:T(8,128)}, f32[16,1024]{1,0:T(8,128)}) custom-call(bf16[8,16,1024]{2,1,0:T(8,128)(2,1)S(1)} %all_to_all.11.own_ref, f32[16,1024]{1,0:T(8,128)S(1)} %get-tuple-element.34.refs_0_, f32[16,1024]{1,0:T(8,128)S(1)} %get-tuple-element.35.refs_1_, ...), custom_call_target="tpu_custom_call" | custom-call | flops 1 | bytes 1048576 | tf_op jit(solution)/shard_map/store/pallas_call | solution.py:243
  45.2 0.3 collective-permute-done.6.other_ref
  45.5 0.7 %weave.1 = bf16[8,2,16,1024]{3,2,1,0:T(8,128)(2,1)} custom-call(bf16[8,16,1024]{2,1,0:T(8,128)(2,1)S(1)} %collective-permute-done.6.other_ref, bf16[8,2,16,1024]{3,2,1,0:T(8,128)(2,1)} %get-tuple-element.42._), custom_call_target="tpu_custom_call", output_to_operand_aliasing={{}: (1, {})} | custom-call | tf_op jit(solution)/shard_map/weave/pallas_call | solution.py:262
  (16 shorter events, 0.0 us)
Async XLA Ops:
  0.6 12.0 %slice-start = ((s8[16777216]{0:T(1024)(128)(4,1)}), s8[4194304]{0:T(1024)(128)(4,1)S(1)}, s32[]{:S(2)}) async-start(s8[16777216]{0:T(1024)(128)(4,1)} %bitcast.3), calls=%async_computation.2 | async-start | bytes 8388608
  2.5 2.4 %copy-start = (bf16[4,256,1024]{2,1,0:T(8,128)(2,1)S(1)}, bf16[4,256,1024]{2,1,0:T(8,128)(2,1)}, u32[]{:S(2)}) copy-start(bf16[4,256,1024]{2,1,0:T(8,128)(2,1)} %param.11) | copy-start | bytes 6291460
  2.5 8.7 %copy-start.1 = (f32[64,257]{1,0:T(8,128)S(1)}, f32[64,257]{1,0:T(8,128)}, u32[]{:S(2)}) copy-start(f32[64,257]{1,0:T(8,128)} %coef_ref.1) | copy-start | bytes 197380
  2.5 10.2 %slice-start.1 = ((s8[16777216]{0:T(1024)(128)(4,1)}), s8[4194304]{0:T(1024)(128)(4,1)S(1)}, s32[]{:S(2)}) async-start(s8[16777216]{0:T(1024)(128)(4,1)} %bitcast.3), calls=%async_computation.3 | async-start | bytes 8388608
  2.5 10.2 %slice-start.2 = ((s8[16777216]{0:T(1024)(128)(4,1)}), s8[4194304]{0:T(1024)(128)(4,1)S(1)}, s32[]{:S(2)}) async-start(s8[16777216]{0:T(1024)(128)(4,1)} %bitcast.3), calls=%async_computation.4 | async-start | bytes 8388608
  2.5 10.2 %slice-start.3 = ((s8[16777216]{0:T(1024)(128)(4,1)}), s8[4194304]{0:T(1024)(128)(4,1)S(1)}, s32[]{:S(2)}) async-start(s8[16777216]{0:T(1024)(128)(4,1)} %bitcast.3), calls=%async_computation.5 | async-start | bytes 8388608
  2.6 2.3 %collective-permute-start = (f32[8,128]{1,0:T(8,128)S(1)}, f32[8,128]{1,0:T(8,128)S(1)}, u32[]{:S(2)}, u32[]{:S(2)}) collective-permute-start(f32[8,128]{1,0:T(8,128)S(1)} %place.1), channel_id=1, source_target_pairs={{0,8},{8,0},{16,24},{24,16},{32,40},{40,32},{48,56},{56,48},{64,72... | collective-permute-start | bytes 12296 | tf_op jit(solution)/shard_map/ppermute | solution.py:292
  4.9 13.5 %collective-permute-start.4 = (bf16[4,8,2,16,1024]{4,3,2,1,0:T(8,128)(2,1)S(1)}, bf16[4,8,2,16,1024]{4,3,2,1,0:T(8,128)(2,1)S(1)}, u32[]{:S(2)}, u32[]{:S(2)}) collective-permute-start(bf16[4,8,2,16,1024]{4,3,2,1,0:T(8,128)(2,1)S(1)} %bitcast.7), channel_id=1, source_target_pairs={{0,8},{8,0},{16,24},{24,16},{32,40},{40,32},{48,56},{56,48},{64,72... | collective-permute-start | bytes 6291464 | tf_op jit(solution)/shard_map/ppermute | solution.py:295
  5.5 5.7 %collective-permute-start.1 = (f32[8,128]{1,0:T(8,128)S(1)}, f32[8,128]{1,0:T(8,128)S(1)}, u32[]{:S(2)}, u32[]{:S(2)}) collective-permute-start(f32[8,128]{1,0:T(8,128)S(1)} %add.7), channel_id=1, source_target_pairs={{0,4},{1,5},{2,6},{3,7},{4,0},{5,1},{6,2},{7,3},{8,12},{9,13},{10,... | collective-permute-start | bytes 12296 | tf_op jit(solution)/shard_map/ppermute | solution.py:296
  11.3 3.3 %collective-permute-start.2 = (f32[8,128]{1,0:T(8,128)S(1)}, f32[8,128]{1,0:T(8,128)S(1)}, u32[]{:S(2)}, u32[]{:S(2)}) collective-permute-start(f32[8,128]{1,0:T(8,128)S(1)} %add.8.a_ref._), channel_id=1, source_target_pairs={{0,1},{1,0},{2,3},{3,2},{4,5},{5,4},{6,7},{7,6},{8,9},{9,8},{10,11... | collective-permute-start | bytes 12296 | tf_op jit(solution)/shard_map/ppermute | solution.py:300
  14.0 4.4 %collective-permute-start.5 = (bf16[8,16,1024]{2,1,0:T(8,128)(2,1)S(1)}, bf16[8,16,1024]{2,1,0:T(8,128)(2,1)S(1)}, u32[]{:S(2)}, u32[]{:S(2)}) collective-permute-start(bf16[8,16,1024]{2,1,0:T(8,128)(2,1)S(1)} %get-tuple-element.32), channel_id=1, source_target_pairs={{0,8},{8,0},{16,24},{24,16},{32,40},{40,32},{48,56},{56,48},{64,72... | collective-permute-start | bytes 786440 | tf_op jit(solution)/shard_map/ppermute | solution.py:299
  14.6 16.6 %copy-start.2 = (f32[16,1024]{1,0:T(8,128)S(1)}, f32[16,1024]{1,0:T(8,128)}, u32[]{:S(2)}) copy-start(f32[16,1024]{1,0:T(8,128)} %fresh_ref.1) | copy-start | bytes 196612
  14.6 16.6 %copy-start.3 = (f32[16,1024]{1,0:T(8,128)S(1)}, f32[16,1024]{1,0:T(8,128)}, u32[]{:S(2)}) copy-start(f32[16,1024]{1,0:T(8,128)} %m1_ref.1) | copy-start | bytes 196612
  14.6 16.6 %copy-start.4 = (f32[16,1024]{1,0:T(8,128)S(1)}, f32[16,1024]{1,0:T(8,128)}, u32[]{:S(2)}) copy-start(f32[16,1024]{1,0:T(8,128)} %m2_ref.1) | copy-start | bytes 196612
  14.7 16.6 %copy-start.5 = (f32[16,1024]{1,0:T(8,128)S(1)}, f32[16,1024]{1,0:T(8,128)}, u32[]{:S(2)}) copy-start(f32[16,1024]{1,0:T(8,128)} %master_ref.1) | copy-start | bytes 196612
  14.7 3.7 %collective-permute-start.3 = (f32[8,128]{1,0:T(8,128)S(1)}, f32[8,128]{1,0:T(8,128)S(1)}, u32[]{:S(2)}, u32[]{:S(2)}) collective-permute-start(f32[8,128]{1,0:T(8,128)S(1)} %add.9.sums_ref), channel_id=1, source_target_pairs={{0,3},{1,2},{2,1},{3,0},{4,7},{5,6},{6,5},{7,4},{8,11},{9,10},{10,... | collective-permute-start | bytes 12296 | tf_op jit(solution)/shard_map/ppermute | solution.py:302
  40.0 5.5 %collective-permute-start.6 = (bf16[8,16,1024]{2,1,0:T(8,128)(2,1)S(1)}, bf16[8,16,1024]{2,1,0:T(8,128)(2,1)S(1)}, u32[]{:S(2)}, u32[]{:S(2)}) collective-permute-start(bf16[8,16,1024]{2,1,0:T(8,128)(2,1)S(1)} %all_to_all.11.own_ref), channel_id=1, source_target_pairs={{0,8},{8,0},{16,24},{24,16},{32,40},{40,32},{48,56},{56,48},{64,72... | collective-permute-start | bytes 786440 | tf_op jit(solution)/shard_map/ppermute | solution.py:309

commit v6 on v5

--- a/solution.py
+++ b/solution.py
@@ -156,34 +156,70 @@
     )(a, b)
 
 
-def pack_kernel(sums_ref, last_ref, own_ref, other_ref, keep_ref, got_ref, out_ref, factor):
+def factors(total):
+    rms = jnp.sqrt(total / (2048.0 * 1024.0))
+    return 1.0 / jnp.maximum(rms, 1.0)
+
+
+def clip_kernel(sums_ref, last_ref, own_ref, keep_ref, got_ref, out_ref, past_ref, one_ref):
     core = core_index()
-    rms = jnp.sqrt((sums_ref[...] + last_ref[...]) / (2048.0 * 1024.0))
-    one = 1.0 / jnp.maximum(rms, 1.0)
-    factor[0] = jnp.broadcast_to(jnp.where(core == 0, one[0:4, 0:1], one[4:8, 0:1]), factor.shape[1:])
-    factor[1] = jnp.broadcast_to(jnp.where(core == 0, one[4:8, 0:1], one[0:4, 0:1]), factor.shape[1:])
+    one = factors(sums_ref[...] + last_ref[...])
+    one_ref[...] = one
+    mine = jnp.where(core == 0, one[0:4], one[4:8])
+    scale = [jnp.broadcast_to(mine[e : e + 1], (16, 128)) for e in range(4)]
 
     @pl.loop(0, 8)
     def _(b):
-        out_ref[b, 0] = (keep_ref[b] + got_ref[b].astype(jnp.float32)).astype(jnp.bfloat16)
-        total = jnp.zeros((16, 1024), jnp.float32)
-        for e in range(4):
-            total = total + factor[0, e : e + 1, :] * own_ref[e, b, core].astype(jnp.float32)
-            total = total + factor[1, e : e + 1, :] * other_ref[e, b, core].astype(jnp.float32)
-        out_ref[b, 1] = total.astype(jnp.bfloat16)
-
-
-def pack(sums, last, own, other, keep, got):
+        past_ref[b] = (keep_ref[b] + got_ref[b].astype(jnp.float32)).astype(jnp.bfloat16)
+        for c in range(0, 1024, 128):
+            total = scale[0] * own_ref[0, b, core, :, c : c + 128].astype(jnp.float32)
+            for e in range(1, 4):
+                total = total + scale[e] * own_ref[e, b, core, :, c : c + 128].astype(jnp.float32)
+            out_ref[b, :, c : c + 128] = total
+
+
+def clip(sums, last, own, keep, got):
+    return pl.pallas_call(
+        clip_kernel,
+        in_specs=[VM] * 5,
+        out_specs=(VM, VM, VM),
+        out_shape=(
+            jax.ShapeDtypeStruct((8, 16, 1024), jnp.float32),
+            jax.ShapeDtypeStruct((8, 16, 1024), jnp.bfloat16),
+            jax.ShapeDtypeStruct((8, 128), jnp.float32),
+        ),
+        compiler_params=params(12),
+        cost_estimate=pl.CostEstimate(flops=2**33, bytes_accessed=1, transcendentals=0),
+        name="clip",
+    )(sums, last, own, keep, got)
+
+
+def pack_kernel(own_ref, past_ref, one_ref, other_ref, out_ref):
+    core = core_index()
+    one = one_ref[...]
+    other = jnp.where(core == 0, one[4:8], one[0:4])
+    scale = [jnp.broadcast_to(other[e : e + 1], (16, 128)) for e in range(4)]
+
+    @pl.loop(0, 8)
+    def _(b):
+        out_ref[b, 0] = past_ref[b]
+        for c in range(0, 1024, 128):
+            total = own_ref[b, :, c : c + 128]
+            for e in range(4):
+                total = total + scale[e] * other_ref[e, b, core, :, c : c + 128].astype(jnp.float32)
+            out_ref[b, 1, :, c : c + 128] = total.astype(jnp.bfloat16)
+
+
+def pack(clipped, past, one, other):
     return pl.pallas_call(
         pack_kernel,
-        in_specs=[VM] * 6,
+        in_specs=[VM] * 4,
         out_specs=VM,
         out_shape=jax.ShapeDtypeStruct((8, 2, 16, 1024), jnp.bfloat16),
-        scratch_shapes=[pltpu.VMEM((2, 4, 1024), jnp.float32)],
         compiler_params=params(12),
-        cost_estimate=pl.CostEstimate(flops=4 * MIB, bytes_accessed=5 * MIB, transcendentals=0),
+        cost_estimate=pl.CostEstimate(flops=1, bytes_accessed=1, transcendentals=0),
         name="pack",
-    )(sums, last, own, other, keep, got)
+    )(clipped, past, one, other)
 
 
 def adam_kernel(
@@ -300,7 +336,7 @@
     sums = add(sums, lax.ppermute(sums, both, near))
     sums, keep = lax.optimization_barrier((sums, keep))
     last = lax.ppermute(sums, both, far)
-    packed = pack(sums, last, examples, other, keep, got)
+    packed = pack(*clip(sums, last, examples, keep, got), other)
     parts = lax.all_to_all(packed, "slot", 0, 0, tiled=True, axis_index_groups=one_core)
     new_noise, m1, m2, master_new, weights = adam(
         scalars, parts, fresh, moment1, moment2, master

time: 46.4 us -> 46.3 us (level)
  starting transfers between devices: 14.1 us -> 13.2 us
  blocking collectives: 20.8 us -> 21.4 us
    all_to_all x1, blocking collectives: 12.2 us -> 12.8 us  [shards(): lax.all_to_all(packed, 'slot', 0, 0, tiled=True, axis_index_groups=one_core)]
    ppermute x1, starting transfers between devices: 4.32 us -> 3.76 us  [shards(): other_rows = lax.ppermute(gathered, 'slot', swap)]
    ppermute x1, starting transfers between devices: 0.64 us -> 0.1 us  [shards(): got = lax.ppermute(send, 'slot', swap)]
  transfers between devices with their start and end apart: 7 -> 7, of which waited for: 3 -> 3; matrix products, arithmetic and copies ran while one was open for 0% -> 0% of each run, Pallas kernels for 5% -> 6%
where the time goes in v6:
time: 46.3 us; the launch traced here: 46 us
  blocking collectives  21.4 us (46%)
  starting transfers between devices  13.2 us (29%)
  Pallas kernels  5.65 us (12%)
  waiting for transfers between devices  2.93 us (6%)
  between operations  2.76 us (6%)
    all_to_all x1, blocking collectives, shards(): lax.all_to_all(packed, 'slot', 0, 0, tiled=True, axis_index_groups=one_core)  12.8 us
    all_to_all x1, blocking collectives, shards(): lax.all_to_all(weights, 'slot', 0, 0, tiled=True, axis_index_groups=one_c...  8.59 us
    ppermute x1, starting transfers between devices, shards(): other_rows = lax.ppermute(gathered, 'slot', swap)  3.76 us
    ppermute x1, starting transfers between devices, shards(): sums = sums + lax.ppermute(sums, both, across)  3.68 us
    ppermute x1, starting transfers between devices, shards(): last = lax.ppermute(sums, both, far)  1.98 us
    pallas_call x1, Pallas kernels, squares(): pl.pallas_call(square_kernel, in_specs=[HBM], out_specs=VM, out_shape=jax...  1.81 us
    ppermute x1, waiting for transfers between devices, shards(): last = lax.ppermute(sums, both, far)  1.77 us
    ppermute x1, starting transfers between devices, shards(): sums = sums + lax.ppermute(sums, 'slot', swap)  1.44 us
  transfers between devices with their start and end apart: 7, of which 3 were waited for; matrix products, arithmetic and copies ran while one was open for 0% of the time, Pallas kernels for 6%

profile of v6, /device:TPU:1, one launch (start us, length us, event | category | flops | bytes accessed | tf_op | source)
XLA Modules:
  0.0 46.0 jit_solution(9484425901561991520)
XLA Ops:
  0.6 0.0 slice-start
  0.6 1.8 %squares.1.squares_ref = f32[4,8,128]{2,1,0:T(8,128)S(1)} custom-call(bf16[4,8,2,16,1024]{4,3,2,1,0:T(8,128)(2,1)} %bitcast.6), custom_call_target="tpu_custom_call" | custom-call | flops 1 | bytes 2097152 | tf_op jit(solution)/shard_map/squares/pallas_call | solution.py:47
  2.5 0.0 copy-start.1
  2.5 0.0 copy-start
  2.5 0.0 slice-start.1
  2.5 0.0 slice-start.3
  2.5 0.1 place.1
  2.6 1.4 %collective-permute-start = (f32[8,128]{1,0:T(8,128)S(1)}, f32[8,128]{1,0:T(8,128)S(1)}, u32[]{:S(2)}, u32[]{:S(2)}) collective-permute-start(f32[8,128]{1,0:T(8,128)S(1)} %place.1), channel_id=1, source_target_pairs={{0,8},{8,0},{16,24},{24,16},{32,40},{40,32},{48,56},{56,48},{64,72... | collective-permute-start | bytes 12296 | tf_op jit(solution)/shard_map/ppermute | solution.py:328
  4.0 0.8 %collective-permute-done = f32[8,128]{1,0:T(8,128)S(1)} collective-permute-done((f32[8,128]{1,0:T(8,128)S(1)}, f32[8,128]{1,0:T(8,128)S(1)}, u32[]{:S(2)}, u32[]{:S(2)}) %collective-permute-start) | collective-permute-done | bytes 4128 | tf_op jit(solution)/shard_map/ppermute | solution.py:328
  4.9 3.7 %collective-permute-start.1 = (f32[8,128]{1,0:T(8,128)S(1)}, f32[8,128]{1,0:T(8,128)S(1)}, u32[]{:S(2)}, u32[]{:S(2)}) collective-permute-start(f32[8,128]{1,0:T(8,128)S(1)} %add.7), channel_id=1, source_target_pairs={{0,4},{1,5},{2,6},{3,7},{4,0},{5,1},{6,2},{7,3},{8,12},{9,13},{10,... | collective-permute-start | bytes 12296 | tf_op jit(solution)/shard_map/ppermute | solution.py:332
  10.5 0.1 slot_weights.1
  10.6 1.4 %collective-permute-start.2 = (f32[8,128]{1,0:T(8,128)S(1)}, f32[8,128]{1,0:T(8,128)S(1)}, u32[]{:S(2)}, u32[]{:S(2)}) collective-permute-start(f32[8,128]{1,0:T(8,128)S(1)} %add.8.a_ref._), channel_id=1, source_target_pairs={{0,1},{1,0},{2,3},{3,2},{4,5},{5,4},{6,7},{7,6},{8,9},{9,8},{10,11... | collective-permute-start | bytes 12296 | tf_op jit(solution)/shard_map/ppermute | solution.py:336
  12.0 0.9 %collective-permute-start.5 = (bf16[4,8,2,16,1024]{4,3,2,1,0:T(8,128)(2,1)S(1)}, bf16[4,8,2,16,1024]{4,3,2,1,0:T(8,128)(2,1)S(1)}, u32[]{:S(2)}, u32[]{:S(2)}) collective-permute-start(bf16[4,8,2,16,1024]{4,3,2,1,0:T(8,128)(2,1)S(1)} %bitcast.7), channel_id=1, source_target_pairs={{0,8},{8,0},{16,24},{24,16},{32,40},{40,32},{48,56},{56,48},{64,72... | collective-permute-start | bytes 6291464 | tf_op jit(solution)/shard_map/ppermute | solution.py:331
  12.9 1.3 %past_parts.1 = (f32[8,16,1024]{2,1,0:T(8,128)S(1)}, bf16[8,16,1024]{2,1,0:T(8,128)(2,1)S(1)}) custom-call(f32[16,8,128]{2,1,0:T(8,128)S(1)} %get-tuple-element.30.weight_ref, f32[16,8,2,16,1024]{4,3,2,1,0:T(8,128)S(1)} %bitcast.5, f32[8,128]{1,0:T(8,128)S(1)} %add.8.a_ref._), custom_call_target="tpu_custom_call" | custom-call | flops 1 | bytes 1 | tf_op jit(solution)/shard_map/past_parts/pallas_call | solution.py:129
  14.3 0.1 collective-permute-start.4
  14.4 0.0 collective-permute-done.2.b_ref
  14.4 2.0 %collective-permute-start.3 = (f32[8,128]{1,0:T(8,128)S(1)}, f32[8,128]{1,0:T(8,128)S(1)}, u32[]{:S(2)}, u32[]{:S(2)}) collective-permute-start(f32[8,128]{1,0:T(8,128)S(1)} %add.9.sums_ref), channel_id=1, source_target_pairs={{0,3},{1,2},{2,1},{3,0},{4,7},{5,6},{6,5},{7,4},{8,11},{9,10},{10,... | collective-permute-start | bytes 12296 | tf_op jit(solution)/shard_map/ppermute | solution.py:338
  16.4 1.8 %collective-permute-done.3.last_ref = f32[8,128]{1,0:T(8,128)S(1)} collective-permute-done((f32[8,128]{1,0:T(8,128)S(1)}, f32[8,128]{1,0:T(8,128)S(1)}, u32[]{:S(2)}, u32[]{:S(2)}) %collective-permute-start.3) | collective-permute-done | bytes 4128 | tf_op jit(solution)/shard_map/ppermute | solution.py:338
  18.1 0.3 clip.1
  18.5 0.0 collective-permute-done.5.other_ref
  18.5 0.0 copy-start.2
  18.5 0.0 copy-start.3
  18.5 0.0 copy-start.4
  18.5 0.0 copy-start.5
  18.5 0.3 pack.1
  18.8 12.8 %all_to_all.10.parts_ref = bf16[8,2,16,1024]{3,2,1,0:T(8,128)(2,1)S(1)} all-to-all(bf16[8,2,16,1024]{3,2,1,0:T(8,128)(2,1)S(1)} %pack.1), channel_id=1, replica_groups={{0,16,32,48,64,80,96,112},{8,24,40,56,72,88,104,120},{1,17,33,49,65,81,..., dimensions={0} | all-to-all | bytes 1048576 | tf_op jit(solution)/shard_map/all_to_all | solution.py:340
  31.7 0.2 adam.1
  31.8 8.6 %all_to_all.11.own_ref = bf16[8,16,1024]{2,1,0:T(8,128)(2,1)S(1)} all-to-all(bf16[8,16,1024]{2,1,0:T(8,128)(2,1)S(1)} %get-tuple-element.39), channel_id=1, replica_groups={{0,16,32,48,64,80,96,112},{8,24,40,56,72,88,104,120},{1,17,33,49,65,81,..., dimensions={0} | all-to-all | bytes 524288 | tf_op jit(solution)/shard_map/all_to_all | solution.py:344
  40.4 3.8 %collective-permute-start.6 = (bf16[8,16,1024]{2,1,0:T(8,128)(2,1)S(1)}, bf16[8,16,1024]{2,1,0:T(8,128)(2,1)S(1)}, u32[]{:S(2)}, u32[]{:S(2)}) collective-permute-start(bf16[8,16,1024]{2,1,0:T(8,128)(2,1)S(1)} %all_to_all.11.own_ref), channel_id=1, source_target_pairs={{0,8},{8,0},{16,24},{24,16},{32,40},{40,32},{48,56},{56,48},{64,72... | collective-permute-start | bytes 786440 | tf_op jit(solution)/shard_map/ppermute | solution.py:345
  44.2 0.8 %store.1 = (bf16[8,2,16,1024]{3,2,1,0:T(8,128)(2,1)}, f32[16,1024]{1,0:T(8,128)}, f32[16,1024]{1,0:T(8,128)}, f32[16,1024]{1,0:T(8,128)}, f32[16,1024]{1,0:T(8,128)}) custom-call(bf16[8,16,1024]{2,1,0:T(8,128)(2,1)S(1)} %all_to_all.11.own_ref, f32[16,1024]{1,0:T(8,128)S(1)} %get-tuple-element.40.refs_0_, f32[16,1024]{1,0:T(8,128)S(1)} %get-tuple-element.41.refs_1_, ...), custom_call_target="tpu_custom_call" | custom-call | flops 1 | bytes 1048576 | tf_op jit(solution)/shard_map/store/pallas_call | solution.py:279
  45.0 0.3 collective-permute-done.6.other_ref
  45.3 0.7 %weave.1 = bf16[8,2,16,1024]{3,2,1,0:T(8,128)(2,1)} custom-call(bf16[8,16,1024]{2,1,0:T(8,128)(2,1)S(1)} %collective-permute-done.6.other_ref, bf16[8,2,16,1024]{3,2,1,0:T(8,128)(2,1)} %get-tuple-element.48._), custom_call_target="tpu_custom_call", output_to_operand_aliasing={{}: (1, {})} | custom-call | tf_op jit(solution)/shard_map/weave/pallas_call | solution.py:298
  (17 shorter events, 0.0 us)
Async XLA Ops:
  0.6 12.3 %slice-start = ((s8[16777216]{0:T(1024)(128)(4,1)}), s8[4194304]{0:T(1024)(128)(4,1)S(1)}, s32[]{:S(2)}) async-start(s8[16777216]{0:T(1024)(128)(4,1)} %bitcast.3), calls=%async_computation.2 | async-start | bytes 8388608
  2.5 8.0 %copy-start.1 = (f32[64,257]{1,0:T(8,128)S(1)}, f32[64,257]{1,0:T(8,128)}, u32[]{:S(2)}) copy-start(f32[64,257]{1,0:T(8,128)} %coef_ref.1) | copy-start | bytes 197380
  2.5 9.5 %copy-start = (bf16[4,256,1024]{2,1,0:T(8,128)(2,1)S(1)}, bf16[4,256,1024]{2,1,0:T(8,128)(2,1)}, u32[]{:S(2)}) copy-start(bf16[4,256,1024]{2,1,0:T(8,128)(2,1)} %param.11) | copy-start | bytes 6291460
  2.5 10.4 %slice-start.1 = ((s8[16777216]{0:T(1024)(128)(4,1)}), s8[4194304]{0:T(1024)(128)(4,1)S(1)}, s32[]{:S(2)}) async-start(s8[16777216]{0:T(1024)(128)(4,1)} %bitcast.3), calls=%async_computation.3 | async-start | bytes 8388608
  2.5 10.4 %slice-start.2 = ((s8[16777216]{0:T(1024)(128)(4,1)}), s8[4194304]{0:T(1024)(128)(4,1)S(1)}, s32[]{:S(2)}) async-start(s8[16777216]{0:T(1024)(128)(4,1)} %bitcast.3), calls=%async_computation.4 | async-start | bytes 8388608
  2.5 10.4 %slice-start.3 = ((s8[16777216]{0:T(1024)(128)(4,1)}), s8[4194304]{0:T(1024)(128)(4,1)S(1)}, s32[]{:S(2)}) async-start(s8[16777216]{0:T(1024)(128)(4,1)} %bitcast.3), calls=%async_computation.5 | async-start | bytes 8388608
  2.6 2.3 %collective-permute-start = (f32[8,128]{1,0:T(8,128)S(1)}, f32[8,128]{1,0:T(8,128)S(1)}, u32[]{:S(2)}, u32[]{:S(2)}) collective-permute-start(f32[8,128]{1,0:T(8,128)S(1)} %place.1), channel_id=1, source_target_pairs={{0,8},{8,0},{16,24},{24,16},{32,40},{40,32},{48,56},{56,48},{64,72... | collective-permute-start | bytes 12296 | tf_op jit(solution)/shard_map/ppermute | solution.py:328
  4.9 5.7 %collective-permute-start.1 = (f32[8,128]{1,0:T(8,128)S(1)}, f32[8,128]{1,0:T(8,128)S(1)}, u32[]{:S(2)}, u32[]{:S(2)}) collective-permute-start(f32[8,128]{1,0:T(8,128)S(1)} %add.7), channel_id=1, source_target_pairs={{0,4},{1,5},{2,6},{3,7},{4,0},{5,1},{6,2},{7,3},{8,12},{9,13},{10,... | collective-permute-start | bytes 12296 | tf_op jit(solution)/shard_map/ppermute | solution.py:332
  10.6 3.8 %collective-permute-start.2 = (f32[8,128]{1,0:T(8,128)S(1)}, f32[8,128]{1,0:T(8,128)S(1)}, u32[]{:S(2)}, u32[]{:S(2)}) collective-permute-start(f32[8,128]{1,0:T(8,128)S(1)} %add.8.a_ref._), channel_id=1, source_target_pairs={{0,1},{1,0},{2,3},{3,2},{4,5},{5,4},{6,7},{7,6},{8,9},{9,8},{10,11... | collective-permute-start | bytes 12296 | tf_op jit(solution)/shard_map/ppermute | solution.py:336
  12.0 6.4 %collective-permute-start.5 = (bf16[4,8,2,16,1024]{4,3,2,1,0:T(8,128)(2,1)S(1)}, bf16[4,8,2,16,1024]{4,3,2,1,0:T(8,128)(2,1)S(1)}, u32[]{:S(2)}, u32[]{:S(2)}) collective-permute-start(bf16[4,8,2,16,1024]{4,3,2,1,0:T(8,128)(2,1)S(1)} %bitcast.7), channel_id=1, source_target_pairs={{0,8},{8,0},{16,24},{24,16},{32,40},{40,32},{48,56},{56,48},{64,72... | collective-permute-start | bytes 6291464 | tf_op jit(solution)/shard_map/ppermute | solution.py:331
  14.3 3.9 %collective-permute-start.4 = (bf16[8,16,1024]{2,1,0:T(8,128)(2,1)S(1)}, bf16[8,16,1024]{2,1,0:T(8,128)(2,1)S(1)}, u32[]{:S(2)}, u32[]{:S(2)}) collective-permute-start(bf16[8,16,1024]{2,1,0:T(8,128)(2,1)S(1)} %get-tuple-element.34), channel_id=1, source_target_pairs={{0,8},{8,0},{16,24},{24,16},{32,40},{40,32},{48,56},{56,48},{64,72... | collective-permute-start | bytes 786440 | tf_op jit(solution)/shard_map/ppermute | solution.py:335
  14.4 3.7 %collective-permute-start.3 = (f32[8,128]{1,0:T(8,128)S(1)}, f32[8,128]{1,0:T(8,128)S(1)}, u32[]{:S(2)}, u32[]{:S(2)}) collective-permute-start(f32[8,128]{1,0:T(8,128)S(1)} %add.9.sums_ref), channel_id=1, source_target_pairs={{0,3},{1,2},{2,1},{3,0},{4,7},{5,6},{6,5},{7,4},{8,11},{9,10},{10,... | collective-permute-start | bytes 12296 | tf_op jit(solution)/shard_map/ppermute | solution.py:338
  18.5 13.2 %copy-start.2 = (f32[16,1024]{1,0:T(8,128)S(1)}, f32[16,1024]{1,0:T(8,128)}, u32[]{:S(2)}) copy-start(f32[16,1024]{1,0:T(8,128)} %fresh_ref.1) | copy-start | bytes 196612
  18.5 13.2 %copy-start.3 = (f32[16,1024]{1,0:T(8,128)S(1)}, f32[16,1024]{1,0:T(8,128)}, u32[]{:S(2)}) copy-start(f32[16,1024]{1,0:T(8,128)} %m1_ref.1) | copy-start | bytes 196612
  18.5 13.2 %copy-start.4 = (f32[16,1024]{1,0:T(8,128)S(1)}, f32[16,1024]{1,0:T(8,128)}, u32[]{:S(2)}) copy-start(f32[16,1024]{1,0:T(8,128)} %m2_ref.1) | copy-start | bytes 196612
  18.5 13.1 %copy-start.5 = (f32[16,1024]{1,0:T(8,128)S(1)}, f32[16,1024]{1,0:T(8,128)}, u32[]{:S(2)}) copy-start(f32[16,1024]{1,0:T(8,128)} %master_ref.1) | copy-start | bytes 196612
  40.4 4.9 %collective-permute-start.6 = (bf16[8,16,1024]{2,1,0:T(8,128)(2,1)S(1)}, bf16[8,16,1024]{2,1,0:T(8,128)(2,1)S(1)}, u32[]{:S(2)}, u32[]{:S(2)}) collective-permute-start(bf16[8,16,1024]{2,1,0:T(8,128)(2,1)S(1)} %all_to_all.11.own_ref), channel_id=1, source_target_pairs={{0,8},{8,0},{16,24},{24,16},{32,40},{40,32},{48,56},{56,48},{64,72... | collective-permute-start | bytes 786440 | tf_op jit(solution)/shard_map/ppermute | solution.py:345

commit v7 on v6

--- a/solution.py
+++ b/solution.py
@@ -117,12 +117,14 @@
         @pl.loop(0, 8)
         def _(b, part=part, out_ref=out_ref):
             scale = [weight_ref[s] for s in range(slots)]
-            for r in (0, 8):
-                for c in range(0, 1024, 128):
+            for c in range(0, 1024, 128):
+                halves = []
+                for r in (0, 8):
                     total = scale[0] * history_ref[0, b, part, r : r + 8, c : c + 128]
                     for s in range(1, slots):
                         total = total + scale[s] * history_ref[s, b, part, r : r + 8, c : c + 128]
-                    out_ref[b, r : r + 8, c : c + 128] = total.astype(out_ref.dtype)
+                    halves.append(total)
+                out_ref[b, :, c : c + 128] = jnp.concatenate(halves, axis=0).astype(out_ref.dtype)
 
 
 def past_parts(weight, history, after):
@@ -329,13 +331,13 @@
     weight, scalars = slot_weights(table_index, step_number, cycle_slot, coef_table)
     _, early = lax.optimization_barrier((sums, examples))
     other = lax.ppermute(early, "slot", swap)
-    sums = sums + lax.ppermute(sums, both, across)
+    sums = sums + lax.ppermute(sums, both, far)
     sums, weight = lax.optimization_barrier((sums, weight))
     keep, send = past_parts(weight, history.reshape(16, 8, 2, 16, 1024), sums)
     got = lax.ppermute(send, "slot", swap)
     sums = add(sums, lax.ppermute(sums, both, near))
     sums, keep = lax.optimization_barrier((sums, keep))
-    last = lax.ppermute(sums, both, far)
+    last = lax.ppermute(sums, both, across)
     packed = pack(*clip(sums, last, examples, keep, got), other)
     parts = lax.all_to_all(packed, "slot", 0, 0, tiled=True, axis_index_groups=one_core)
     new_noise, m1, m2, master_new, weights = adam(

time: 46.3 us -> 46.1 us (level)
  starting transfers between devices: 13.2 us -> 14.2 us
  waiting for transfers between devices: 2.93 us -> 2.16 us
  blocking collectives: 21.4 us -> 20.9 us
    ppermute x2, starting transfers between devices: 5.66 us -> 6.49 us  [the longest x1 3.68 us: shards(): last = lax.ppermute(sums, both, across)]
    ppermute x1, starting transfers between devices: 3.76 us -> 4.56 us  [shards(): other_rows = lax.ppermute(gathered, 'slot', swap)]
    ppermute x2, waiting for transfers between devices: 1.77 us -> 1 us  [the longest x1 1 us: shards(): last = lax.ppermute(sums, both, across)]
    ppermute x1, starting transfers between devices: 1.38 us -> 0.72 us  [shards(): sums = add(sums, lax.ppermute(sums, both, near))]
where the time goes in v7:
time: 46.1 us; the launch traced here: 45.9 us
  blocking collectives  20.9 us (45%)
  starting transfers between devices  14.2 us (31%)
  Pallas kernels  5.75 us (12%)
  between operations  2.76 us (6%)
  waiting for transfers between devices  2.16 us (5%)
    all_to_all x1, blocking collectives, shards(): lax.all_to_all(packed, 'slot', 0, 0, tiled=True, axis_index_groups=one_core)  12.4 us
    all_to_all x1, blocking collectives, shards(): lax.all_to_all(weights, 'slot', 0, 0, tiled=True, axis_index_groups=one_c...  8.55 us
    ppermute x1, starting transfers between devices, shards(): other_rows = lax.ppermute(gathered, 'slot', swap)  4.56 us
    ppermute x1, starting transfers between devices, shards(): last = lax.ppermute(sums, both, across)  3.68 us
    ppermute x1, starting transfers between devices, shards(): sums = sums + lax.ppermute(sums, both, far)  2.82 us
    pallas_call x1, Pallas kernels, squares(): pl.pallas_call(square_kernel, in_specs=[HBM], out_specs=VM, out_shape=jax...  1.81 us
    pallas_call x1, Pallas kernels, past_parts(): pl.pallas_call(past_kernel, in_specs=[VM, VM, HBM], out_specs=(VM, VM), o...  1.45 us
    ppermute x1, starting transfers between devices, shards(): sums = sums + lax.ppermute(sums, 'slot', swap)  1.44 us
  transfers between devices with their start and end apart: 7, of which 3 were waited for; matrix products, arithmetic and copies ran while one was open for 0% of the time, Pallas kernels for 6%

profile of v7, /device:TPU:1, one launch (start us, length us, event | category | flops | bytes accessed | tf_op | source)
XLA Modules:
  0.0 45.9 jit_solution(16326460335862927010)
XLA Ops:
  0.6 0.0 slice-start
  0.6 1.8 %squares.1.squares_ref = f32[4,8,128]{2,1,0:T(8,128)S(1)} custom-call(bf16[4,8,2,16,1024]{4,3,2,1,0:T(8,128)(2,1)} %bitcast.6), custom_call_target="tpu_custom_call" | custom-call | flops 1 | bytes 2097152 | tf_op jit(solution)/shard_map/squares/pallas_call | solution.py:47
  2.5 0.0 copy-start.1
  2.5 0.0 copy-start
  2.5 0.0 slice-start.1
  2.5 0.0 slice-start.2
  2.5 0.1 place.1
  2.6 1.4 %collective-permute-start = (f32[8,128]{1,0:T(8,128)S(1)}, f32[8,128]{1,0:T(8,128)S(1)}, u32[]{:S(2)}, u32[]{:S(2)}) collective-permute-start(f32[8,128]{1,0:T(8,128)S(1)} %place.1), channel_id=1, source_target_pairs={{0,8},{8,0},{16,24},{24,16},{32,40},{40,32},{48,56},{56,48},{64,72... | collective-permute-start | bytes 12296 | tf_op jit(solution)/shard_map/ppermute | solution.py:330
  4.0 0.8 %collective-permute-done = f32[8,128]{1,0:T(8,128)S(1)} collective-permute-done((f32[8,128]{1,0:T(8,128)S(1)}, f32[8,128]{1,0:T(8,128)S(1)}, u32[]{:S(2)}, u32[]{:S(2)}) %collective-permute-start) | collective-permute-done | bytes 4128 | tf_op jit(solution)/shard_map/ppermute | solution.py:330
  4.9 2.8 %collective-permute-start.1 = (f32[8,128]{1,0:T(8,128)S(1)}, f32[8,128]{1,0:T(8,128)S(1)}, u32[]{:S(2)}, u32[]{:S(2)}) collective-permute-start(f32[8,128]{1,0:T(8,128)S(1)} %add.7), channel_id=1, source_target_pairs={{0,3},{1,2},{2,1},{3,0},{4,7},{5,6},{6,5},{7,4},{8,11},{9,10},{10,... | collective-permute-start | bytes 12296 | tf_op jit(solution)/shard_map/ppermute | solution.py:334
  9.6 0.1 slot_weights.1
  9.8 0.7 %collective-permute-start.2 = (f32[8,128]{1,0:T(8,128)S(1)}, f32[8,128]{1,0:T(8,128)S(1)}, u32[]{:S(2)}, u32[]{:S(2)}) collective-permute-start(f32[8,128]{1,0:T(8,128)S(1)} %add.8.a_ref._), channel_id=1, source_target_pairs={{0,1},{1,0},{2,3},{3,2},{4,5},{5,4},{6,7},{7,6},{8,9},{9,8},{10,11... | collective-permute-start | bytes 12296 | tf_op jit(solution)/shard_map/ppermute | solution.py:338
  10.5 0.9 %collective-permute-start.5 = (bf16[4,8,2,16,1024]{4,3,2,1,0:T(8,128)(2,1)S(1)}, bf16[4,8,2,16,1024]{4,3,2,1,0:T(8,128)(2,1)S(1)}, u32[]{:S(2)}, u32[]{:S(2)}) collective-permute-start(bf16[4,8,2,16,1024]{4,3,2,1,0:T(8,128)(2,1)S(1)} %bitcast.7), channel_id=1, source_target_pairs={{0,8},{8,0},{16,24},{24,16},{32,40},{40,32},{48,56},{56,48},{64,72... | collective-permute-start | bytes 6291464 | tf_op jit(solution)/shard_map/ppermute | solution.py:333
  11.4 1.4 %past_parts.1 = (f32[8,16,1024]{2,1,0:T(8,128)S(1)}, bf16[8,16,1024]{2,1,0:T(8,128)(2,1)S(1)}) custom-call(f32[16,8,128]{2,1,0:T(8,128)S(1)} %get-tuple-element.30.weight_ref, f32[16,8,2,16,1024]{4,3,2,1,0:T(8,128)S(1)} %bitcast.5, f32[8,128]{1,0:T(8,128)S(1)} %add.8.a_ref._), custom_call_target="tpu_custom_call" | custom-call | flops 1 | bytes 1 | tf_op jit(solution)/shard_map/past_parts/pallas_call | solution.py:131
  12.9 0.1 collective-permute-start.4
  13.0 0.0 collective-permute-done.2.b_ref
  13.0 3.7 %collective-permute-start.3 = (f32[8,128]{1,0:T(8,128)S(1)}, f32[8,128]{1,0:T(8,128)S(1)}, u32[]{:S(2)}, u32[]{:S(2)}) collective-permute-start(f32[8,128]{1,0:T(8,128)S(1)} %add.9.sums_ref), channel_id=1, source_target_pairs={{0,4},{1,5},{2,6},{3,7},{4,0},{5,1},{6,2},{7,3},{8,12},{9,13},{10,... | collective-permute-start | bytes 12296 | tf_op jit(solution)/shard_map/ppermute | solution.py:340
  16.7 1.0 %collective-permute-done.3.last_ref = f32[8,128]{1,0:T(8,128)S(1)} collective-permute-done((f32[8,128]{1,0:T(8,128)S(1)}, f32[8,128]{1,0:T(8,128)S(1)}, u32[]{:S(2)}, u32[]{:S(2)}) %collective-permute-start.3) | collective-permute-done | bytes 4128 | tf_op jit(solution)/shard_map/ppermute | solution.py:340
  17.7 0.3 clip.1
  18.0 0.0 collective-permute-done.5.other_ref
  18.0 0.0 copy-start.2
  18.0 0.0 copy-start.3
  18.0 0.0 copy-start.4
  18.0 0.0 copy-start.5
  18.0 0.3 pack.1
  18.3 12.4 %all_to_all.10.parts_ref = bf16[8,2,16,1024]{3,2,1,0:T(8,128)(2,1)S(1)} all-to-all(bf16[8,2,16,1024]{3,2,1,0:T(8,128)(2,1)S(1)} %pack.1), channel_id=1, replica_groups={{0,16,32,48,64,80,96,112},{8,24,40,56,72,88,104,120},{1,17,33,49,65,81,..., dimensions={0} | all-to-all | bytes 1048576 | tf_op jit(solution)/shard_map/all_to_all | solution.py:342
  30.7 0.2 adam.1
  30.9 8.5 %all_to_all.11.own_ref = bf16[8,16,1024]{2,1,0:T(8,128)(2,1)S(1)} all-to-all(bf16[8,16,1024]{2,1,0:T(8,128)(2,1)S(1)} %get-tuple-element.39), channel_id=1, replica_groups={{0,16,32,48,64,80,96,112},{8,24,40,56,72,88,104,120},{1,17,33,49,65,81,..., dimensions={0} | all-to-all | bytes 524288 | tf_op jit(solution)/shard_map/all_to_all | solution.py:346
  39.5 4.6 %collective-permute-start.6 = (bf16[8,16,1024]{2,1,0:T(8,128)(2,1)S(1)}, bf16[8,16,1024]{2,1,0:T(8,128)(2,1)S(1)}, u32[]{:S(2)}, u32[]{:S(2)}) collective-permute-start(bf16[8,16,1024]{2,1,0:T(8,128)(2,1)S(1)} %all_to_all.11.own_ref), channel_id=1, source_target_pairs={{0,8},{8,0},{16,24},{24,16},{32,40},{40,32},{48,56},{56,48},{64,72... | collective-permute-start | bytes 786440 | tf_op jit(solution)/shard_map/ppermute | solution.py:347
  44.0 0.8 %store.1 = (bf16[8,2,16,1024]{3,2,1,0:T(8,128)(2,1)}, f32[16,1024]{1,0:T(8,128)}, f32[16,1024]{1,0:T(8,128)}, f32[16,1024]{1,0:T(8,128)}, f32[16,1024]{1,0:T(8,128)}) custom-call(bf16[8,16,1024]{2,1,0:T(8,128)(2,1)S(1)} %all_to_all.11.own_ref, f32[16,1024]{1,0:T(8,128)S(1)} %get-tuple-element.40.refs_0_, f32[16,1024]{1,0:T(8,128)S(1)} %get-tuple-element.41.refs_1_, ...), custom_call_target="tpu_custom_call" | custom-call | flops 1 | bytes 1048576 | tf_op jit(solution)/shard_map/store/pallas_call | solution.py:281
  44.9 0.3 collective-permute-done.6.other_ref
  45.2 0.7 %weave.1 = bf16[8,2,16,1024]{3,2,1,0:T(8,128)(2,1)} custom-call(bf16[8,16,1024]{2,1,0:T(8,128)(2,1)S(1)} %collective-permute-done.6.other_ref, bf16[8,2,16,1024]{3,2,1,0:T(8,128)(2,1)} %get-tuple-element.48._), custom_call_target="tpu_custom_call", output_to_operand_aliasing={{}: (1, {})} | custom-call | tf_op jit(solution)/shard_map/weave/pallas_call | solution.py:300
  (17 shorter events, 0.0 us)
Async XLA Ops:
  0.6 10.8 %slice-start = ((s8[16777216]{0:T(1024)(128)(4,1)}), s8[4194304]{0:T(1024)(128)(4,1)S(1)}, s32[]{:S(2)}) async-start(s8[16777216]{0:T(1024)(128)(4,1)} %bitcast.3), calls=%async_computation.2 | async-start | bytes 8388608
  2.5 7.2 %copy-start.1 = (f32[64,257]{1,0:T(8,128)S(1)}, f32[64,257]{1,0:T(8,128)}, u32[]{:S(2)}) copy-start(f32[64,257]{1,0:T(8,128)} %coef_ref.1) | copy-start | bytes 197380
  2.5 8.0 %copy-start = (bf16[4,256,1024]{2,1,0:T(8,128)(2,1)S(1)}, bf16[4,256,1024]{2,1,0:T(8,128)(2,1)}, u32[]{:S(2)}) copy-start(bf16[4,256,1024]{2,1,0:T(8,128)(2,1)} %param.11) | copy-start | bytes 6291460
  2.5 8.9 %slice-start.1 = ((s8[16777216]{0:T(1024)(128)(4,1)}), s8[4194304]{0:T(1024)(128)(4,1)S(1)}, s32[]{:S(2)}) async-start(s8[16777216]{0:T(1024)(128)(4,1)} %bitcast.3), calls=%async_computation.3 | async-start | bytes 8388608
  2.5 8.9 %slice-start.2 = ((s8[16777216]{0:T(1024)(128)(4,1)}), s8[4194304]{0:T(1024)(128)(4,1)S(1)}, s32[]{:S(2)}) async-start(s8[16777216]{0:T(1024)(128)(4,1)} %bitcast.3), calls=%async_computation.4 | async-start | bytes 8388608
  2.5 8.9 %slice-start.3 = ((s8[16777216]{0:T(1024)(128)(4,1)}), s8[4194304]{0:T(1024)(128)(4,1)S(1)}, s32[]{:S(2)}) async-start(s8[16777216]{0:T(1024)(128)(4,1)} %bitcast.3), calls=%async_computation.5 | async-start | bytes 8388608
  2.6 2.3 %collective-permute-start = (f32[8,128]{1,0:T(8,128)S(1)}, f32[8,128]{1,0:T(8,128)S(1)}, u32[]{:S(2)}, u32[]{:S(2)}) collective-permute-start(f32[8,128]{1,0:T(8,128)S(1)} %place.1), channel_id=1, source_target_pairs={{0,8},{8,0},{16,24},{24,16},{32,40},{40,32},{48,56},{56,48},{64,72... | collective-permute-start | bytes 12296 | tf_op jit(solution)/shard_map/ppermute | solution.py:330
  4.9 4.9 %collective-permute-start.1 = (f32[8,128]{1,0:T(8,128)S(1)}, f32[8,128]{1,0:T(8,128)S(1)}, u32[]{:S(2)}, u32[]{:S(2)}) collective-permute-start(f32[8,128]{1,0:T(8,128)S(1)} %add.7), channel_id=1, source_target_pairs={{0,3},{1,2},{2,1},{3,0},{4,7},{5,6},{6,5},{7,4},{8,11},{9,10},{10,... | collective-permute-start | bytes 12296 | tf_op jit(solution)/shard_map/ppermute | solution.py:334
  9.8 3.2 %collective-permute-start.2 = (f32[8,128]{1,0:T(8,128)S(1)}, f32[8,128]{1,0:T(8,128)S(1)}, u32[]{:S(2)}, u32[]{:S(2)}) collective-permute-start(f32[8,128]{1,0:T(8,128)S(1)} %add.8.a_ref._), channel_id=1, source_target_pairs={{0,1},{1,0},{2,3},{3,2},{4,5},{5,4},{6,7},{7,6},{8,9},{9,8},{10,11... | collective-permute-start | bytes 12296 | tf_op jit(solution)/shard_map/ppermute | solution.py:338
  10.5 7.5 %collective-permute-start.5 = (bf16[4,8,2,16,1024]{4,3,2,1,0:T(8,128)(2,1)S(1)}, bf16[4,8,2,16,1024]{4,3,2,1,0:T(8,128)(2,1)S(1)}, u32[]{:S(2)}, u32[]{:S(2)}) collective-permute-start(bf16[4,8,2,16,1024]{4,3,2,1,0:T(8,128)(2,1)S(1)} %bitcast.7), channel_id=1, source_target_pairs={{0,8},{8,0},{16,24},{24,16},{32,40},{40,32},{48,56},{56,48},{64,72... | collective-permute-start | bytes 6291464 | tf_op jit(solution)/shard_map/ppermute | solution.py:333
  12.9 4.8 %collective-permute-start.4 = (bf16[8,16,1024]{2,1,0:T(8,128)(2,1)S(1)}, bf16[8,16,1024]{2,1,0:T(8,128)(2,1)S(1)}, u32[]{:S(2)}, u32[]{:S(2)}) collective-permute-start(bf16[8,16,1024]{2,1,0:T(8,128)(2,1)S(1)} %get-tuple-element.34), channel_id=1, source_target_pairs={{0,8},{8,0},{16,24},{24,16},{32,40},{40,32},{48,56},{56,48},{64,72... | collective-permute-start | bytes 786440 | tf_op jit(solution)/shard_map/ppermute | solution.py:337
  13.0 4.7 %collective-permute-start.3 = (f32[8,128]{1,0:T(8,128)S(1)}, f32[8,128]{1,0:T(8,128)S(1)}, u32[]{:S(2)}, u32[]{:S(2)}) collective-permute-start(f32[8,128]{1,0:T(8,128)S(1)} %add.9.sums_ref), channel_id=1, source_target_pairs={{0,4},{1,5},{2,6},{3,7},{4,0},{5,1},{6,2},{7,3},{8,12},{9,13},{10,... | collective-permute-start | bytes 12296 | tf_op jit(solution)/shard_map/ppermute | solution.py:340
  18.0 12.7 %copy-start.2 = (f32[16,1024]{1,0:T(8,128)S(1)}, f32[16,1024]{1,0:T(8,128)}, u32[]{:S(2)}) copy-start(f32[16,1024]{1,0:T(8,128)} %fresh_ref.1) | copy-start | bytes 196612
  18.0 12.7 %copy-start.3 = (f32[16,1024]{1,0:T(8,128)S(1)}, f32[16,1024]{1,0:T(8,128)}, u32[]{:S(2)}) copy-start(f32[16,1024]{1,0:T(8,128)} %m1_ref.1) | copy-start | bytes 196612
  18.0 12.7 %copy-start.4 = (f32[16,1024]{1,0:T(8,128)S(1)}, f32[16,1024]{1,0:T(8,128)}, u32[]{:S(2)}) copy-start(f32[16,1024]{1,0:T(8,128)} %m2_ref.1) | copy-start | bytes 196612
  18.0 12.7 %copy-start.5 = (f32[16,1024]{1,0:T(8,128)S(1)}, f32[16,1024]{1,0:T(8,128)}, u32[]{:S(2)}) copy-start(f32[16,1024]{1,0:T(8,128)} %master_ref.1) | copy-start | bytes 196612
  39.5 5.7 %collective-permute-start.6 = (bf16[8,16,1024]{2,1,0:T(8,128)(2,1)S(1)}, bf16[8,16,1024]{2,1,0:T(8,128)(2,1)S(1)}, u32[]{:S(2)}, u32[]{:S(2)}) collective-permute-start(bf16[8,16,1024]{2,1,0:T(8,128)(2,1)S(1)} %all_to_all.11.own_ref), channel_id=1, source_target_pairs={{0,8},{8,0},{16,24},{24,16},{32,40},{40,32},{48,56},{56,48},{64,72... | collective-permute-start | bytes 786440 | tf_op jit(solution)/shard_map/ppermute | solution.py:347

commit v8 on v7

--- a/solution.py
+++ b/solution.py
@@ -329,12 +329,12 @@
     sums = place(squares(examples))
     sums = sums + lax.ppermute(sums, "slot", swap)
     weight, scalars = slot_weights(table_index, step_number, cycle_slot, coef_table)
-    _, early = lax.optimization_barrier((sums, examples))
-    other = lax.ppermute(early, "slot", swap)
     sums = sums + lax.ppermute(sums, both, far)
     sums, weight = lax.optimization_barrier((sums, weight))
     keep, send = past_parts(weight, history.reshape(16, 8, 2, 16, 1024), sums)
     got = lax.ppermute(send, "slot", swap)
+    _, early = lax.optimization_barrier((send, examples))
+    other = lax.ppermute(early, "slot", swap)
     sums = add(sums, lax.ppermute(sums, both, near))
     sums, keep = lax.optimization_barrier((sums, keep))
     last = lax.ppermute(sums, both, across)

time: 46.1 us -> 46.1 us (level)
    ppermute x1, starting transfers between devices: 0.1 us -> 0.99 us  [shards(): got = lax.ppermute(send, 'slot', swap)]
    ppermute x1, starting transfers between devices: 0.9 us -> 0.1 us  [shards(): other = lax.ppermute(early, 'slot', swap)]
where the time goes in v8:
time: 46.1 us; the launch traced here: 45.9 us
  blocking collectives  20.9 us (45%)
  starting transfers between devices  14.2 us (31%)
  Pallas kernels  5.75 us (12%)
  between operations  2.76 us (6%)
  waiting for transfers between devices  2.16 us (5%)
    all_to_all x1, blocking collectives, shards(): lax.all_to_all(packed, 'slot', 0, 0, tiled=True, axis_index_groups=one_core)  12.4 us
    all_to_all x1, blocking collectives, shards(): lax.all_to_all(weights, 'slot', 0, 0, tiled=True, axis_index_groups=one_c...  8.55 us
    ppermute x1, starting transfers between devices, shards(): other_rows = lax.ppermute(gathered, 'slot', swap)  4.56 us
    ppermute x1, starting transfers between devices, shards(): last = lax.ppermute(sums, both, across)  3.61 us
    ppermute x1, starting transfers between devices, shards(): sums = sums + lax.ppermute(sums, both, far)  2.82 us
    pallas_call x1, Pallas kernels, squares(): pl.pallas_call(square_kernel, in_specs=[HBM], out_specs=VM, out_shape=jax...  1.81 us
    pallas_call x1, Pallas kernels, past_parts(): pl.pallas_call(past_kernel, in_specs=[VM, VM, HBM], out_specs=(VM, VM), o...  1.45 us
    ppermute x1, starting transfers between devices, shards(): sums = sums + lax.ppermute(sums, 'slot', swap)  1.44 us
  transfers between devices with their start and end apart: 7, of which 3 were waited for; matrix products, arithmetic and copies ran while one was open for 0% of the time, Pallas kernels for 6%

profile of v8, /device:TPU:1, one launch (start us, length us, event | category | flops | bytes accessed | tf_op | source)
XLA Modules:
  0.0 45.9 jit_solution(10047775253057995759)
XLA Ops:
  0.6 0.0 slice-start
  0.6 1.8 %squares.1.squares_ref = f32[4,8,128]{2,1,0:T(8,128)S(1)} custom-call(bf16[4,8,2,16,1024]{4,3,2,1,0:T(8,128)(2,1)} %bitcast.6), custom_call_target="tpu_custom_call" | custom-call | flops 1 | bytes 2097152 | tf_op jit(solution)/shard_map/squares/pallas_call | solution.py:47
  2.5 0.0 copy-start.1
  2.5 0.0 slice-start.1
  2.5 0.0 slice-start.2
  2.5 0.0 slice-start.3
  2.5 0.1 place.1
  2.6 1.4 %collective-permute-start = (f32[8,128]{1,0:T(8,128)S(1)}, f32[8,128]{1,0:T(8,128)S(1)}, u32[]{:S(2)}, u32[]{:S(2)}) collective-permute-start(f32[8,128]{1,0:T(8,128)S(1)} %place.1), channel_id=1, source_target_pairs={{0,8},{8,0},{16,24},{24,16},{32,40},{40,32},{48,56},{56,48},{64,72... | collective-permute-start | bytes 12296 | tf_op jit(solution)/shard_map/ppermute | solution.py:330
  4.0 0.8 %collective-permute-done = f32[8,128]{1,0:T(8,128)S(1)} collective-permute-done((f32[8,128]{1,0:T(8,128)S(1)}, f32[8,128]{1,0:T(8,128)S(1)}, u32[]{:S(2)}, u32[]{:S(2)}) %collective-permute-start) | collective-permute-done | bytes 4128 | tf_op jit(solution)/shard_map/ppermute | solution.py:330
  4.9 2.8 %collective-permute-start.1 = (f32[8,128]{1,0:T(8,128)S(1)}, f32[8,128]{1,0:T(8,128)S(1)}, u32[]{:S(2)}, u32[]{:S(2)}) collective-permute-start(f32[8,128]{1,0:T(8,128)S(1)} %add.7), channel_id=1, source_target_pairs={{0,3},{1,2},{2,1},{3,0},{4,7},{5,6},{6,5},{7,4},{8,11},{9,10},{10,... | collective-permute-start | bytes 12296 | tf_op jit(solution)/shard_map/ppermute | solution.py:332
  9.6 0.1 slot_weights.1
  9.8 0.7 %collective-permute-start.2 = (f32[8,128]{1,0:T(8,128)S(1)}, f32[8,128]{1,0:T(8,128)S(1)}, u32[]{:S(2)}, u32[]{:S(2)}) collective-permute-start(f32[8,128]{1,0:T(8,128)S(1)} %add.8.a_ref._), channel_id=1, source_target_pairs={{0,1},{1,0},{2,3},{3,2},{4,5},{5,4},{6,7},{7,6},{8,9},{9,8},{10,11... | collective-permute-start | bytes 12296 | tf_op jit(solution)/shard_map/ppermute | solution.py:338
  10.5 0.0 copy-start
  10.5 1.4 %past_parts.1 = (f32[8,16,1024]{2,1,0:T(8,128)S(1)}, bf16[8,16,1024]{2,1,0:T(8,128)(2,1)S(1)}) custom-call(f32[16,8,128]{2,1,0:T(8,128)S(1)} %get-tuple-element.30.weight_ref, f32[16,8,2,16,1024]{4,3,2,1,0:T(8,128)S(1)} %bitcast.5, f32[8,128]{1,0:T(8,128)S(1)} %add.8.a_ref._), custom_call_target="tpu_custom_call" | custom-call | flops 1 | bytes 1 | tf_op jit(solution)/shard_map/past_parts/pallas_call | solution.py:131
  11.9 1.0 %collective-permute-start.4 = (bf16[8,16,1024]{2,1,0:T(8,128)(2,1)S(1)}, bf16[8,16,1024]{2,1,0:T(8,128)(2,1)S(1)}, u32[]{:S(2)}, u32[]{:S(2)}) collective-permute-start(bf16[8,16,1024]{2,1,0:T(8,128)(2,1)S(1)} %get-tuple-element.34), channel_id=1, source_target_pairs={{0,8},{8,0},{16,24},{24,16},{32,40},{40,32},{48,56},{56,48},{64,72... | collective-permute-start | bytes 786440 | tf_op jit(solution)/shard_map/ppermute | solution.py:335
  12.9 0.1 collective-permute-start.5
  13.0 3.6 %collective-permute-start.3 = (f32[8,128]{1,0:T(8,128)S(1)}, f32[8,128]{1,0:T(8,128)S(1)}, u32[]{:S(2)}, u32[]{:S(2)}) collective-permute-start(f32[8,128]{1,0:T(8,128)S(1)} %add.9.sums_ref), channel_id=1, source_target_pairs={{0,4},{1,5},{2,6},{3,7},{4,0},{5,1},{6,2},{7,3},{8,12},{9,13},{10,... | collective-permute-start | bytes 12296 | tf_op jit(solution)/shard_map/ppermute | solution.py:340
  16.6 1.0 %collective-permute-done.3.last_ref = f32[8,128]{1,0:T(8,128)S(1)} collective-permute-done((f32[8,128]{1,0:T(8,128)S(1)}, f32[8,128]{1,0:T(8,128)S(1)}, u32[]{:S(2)}, u32[]{:S(2)}) %collective-permute-start.3) | collective-permute-done | bytes 4128 | tf_op jit(solution)/shard_map/ppermute | solution.py:340
  17.6 0.0 collective-permute-done.4.got_ref
  17.6 0.3 clip.1
  17.9 0.0 copy-start.2
  18.0 0.0 copy-start.3
  18.0 0.0 copy-start.4
  18.0 0.0 copy-start.5
  18.0 0.3 pack.1
  18.3 12.4 %all_to_all.10.parts_ref = bf16[8,2,16,1024]{3,2,1,0:T(8,128)(2,1)S(1)} all-to-all(bf16[8,2,16,1024]{3,2,1,0:T(8,128)(2,1)S(1)} %pack.1), channel_id=1, replica_groups={{0,16,32,48,64,80,96,112},{8,24,40,56,72,88,104,120},{1,17,33,49,65,81,..., dimensions={0} | all-to-all | bytes 1048576 | tf_op jit(solution)/shard_map/all_to_all | solution.py:342
  30.7 0.2 adam.1
  30.9 8.5 %all_to_all.11.own_ref = bf16[8,16,1024]{2,1,0:T(8,128)(2,1)S(1)} all-to-all(bf16[8,16,1024]{2,1,0:T(8,128)(2,1)S(1)} %get-tuple-element.39), channel_id=1, replica_groups={{0,16,32,48,64,80,96,112},{8,24,40,56,72,88,104,120},{1,17,33,49,65,81,..., dimensions={0} | all-to-all | bytes 524288 | tf_op jit(solution)/shard_map/all_to_all | solution.py:346
  39.4 4.6 %collective-permute-start.6 = (bf16[8,16,1024]{2,1,0:T(8,128)(2,1)S(1)}, bf16[8,16,1024]{2,1,0:T(8,128)(2,1)S(1)}, u32[]{:S(2)}, u32[]{:S(2)}) collective-permute-start(bf16[8,16,1024]{2,1,0:T(8,128)(2,1)S(1)} %all_to_all.11.own_ref), channel_id=1, source_target_pairs={{0,8},{8,0},{16,24},{24,16},{32,40},{40,32},{48,56},{56,48},{64,72... | collective-permute-start | bytes 786440 | tf_op jit(solution)/shard_map/ppermute | solution.py:347
  44.0 0.8 %store.1 = (bf16[8,2,16,1024]{3,2,1,0:T(8,128)(2,1)}, f32[16,1024]{1,0:T(8,128)}, f32[16,1024]{1,0:T(8,128)}, f32[16,1024]{1,0:T(8,128)}, f32[16,1024]{1,0:T(8,128)}) custom-call(bf16[8,16,1024]{2,1,0:T(8,128)(2,1)S(1)} %all_to_all.11.own_ref, f32[16,1024]{1,0:T(8,128)S(1)} %get-tuple-element.40.refs_0_, f32[16,1024]{1,0:T(8,128)S(1)} %get-tuple-element.41.refs_1_, ...), custom_call_target="tpu_custom_call" | custom-call | flops 1 | bytes 1048576 | tf_op jit(solution)/shard_map/store/pallas_call | solution.py:281
  44.8 0.3 collective-permute-done.6.other_ref
  45.2 0.7 %weave.1 = bf16[8,2,16,1024]{3,2,1,0:T(8,128)(2,1)} custom-call(bf16[8,16,1024]{2,1,0:T(8,128)(2,1)S(1)} %collective-permute-done.6.other_ref, bf16[8,2,16,1024]{3,2,1,0:T(8,128)(2,1)} %get-tuple-element.48._), custom_call_target="tpu_custom_call", output_to_operand_aliasing={{}: (1, {})} | custom-call | tf_op jit(solution)/shard_map/weave/pallas_call | solution.py:300
  (17 shorter events, 0.0 us)
Async XLA Ops:
  0.6 9.8 %slice-start = ((s8[16777216]{0:T(1024)(128)(4,1)}), s8[4194304]{0:T(1024)(128)(4,1)S(1)}, s32[]{:S(2)}) async-start(s8[16777216]{0:T(1024)(128)(4,1)} %bitcast.3), calls=%async_computation.2 | async-start | bytes 8388608
  2.5 7.2 %copy-start.1 = (f32[64,257]{1,0:T(8,128)S(1)}, f32[64,257]{1,0:T(8,128)}, u32[]{:S(2)}) copy-start(f32[64,257]{1,0:T(8,128)} %coef_ref.1) | copy-start | bytes 197380
  2.5 8.0 %slice-start.1 = ((s8[16777216]{0:T(1024)(128)(4,1)}), s8[4194304]{0:T(1024)(128)(4,1)S(1)}, s32[]{:S(2)}) async-start(s8[16777216]{0:T(1024)(128)(4,1)} %bitcast.3), calls=%async_computation.3 | async-start | bytes 8388608
  2.5 8.0 %slice-start.2 = ((s8[16777216]{0:T(1024)(128)(4,1)}), s8[4194304]{0:T(1024)(128)(4,1)S(1)}, s32[]{:S(2)}) async-start(s8[16777216]{0:T(1024)(128)(4,1)} %bitcast.3), calls=%async_computation.4 | async-start | bytes 8388608
  2.5 8.0 %slice-start.3 = ((s8[16777216]{0:T(1024)(128)(4,1)}), s8[4194304]{0:T(1024)(128)(4,1)S(1)}, s32[]{:S(2)}) async-start(s8[16777216]{0:T(1024)(128)(4,1)} %bitcast.3), calls=%async_computation.5 | async-start | bytes 8388608
  2.6 2.3 %collective-permute-start = (f32[8,128]{1,0:T(8,128)S(1)}, f32[8,128]{1,0:T(8,128)S(1)}, u32[]{:S(2)}, u32[]{:S(2)}) collective-permute-start(f32[8,128]{1,0:T(8,128)S(1)} %place.1), channel_id=1, source_target_pairs={{0,8},{8,0},{16,24},{24,16},{32,40},{40,32},{48,56},{56,48},{64,72... | collective-permute-start | bytes 12296 | tf_op jit(solution)/shard_map/ppermute | solution.py:330
  4.9 4.9 %collective-permute-start.1 = (f32[8,128]{1,0:T(8,128)S(1)}, f32[8,128]{1,0:T(8,128)S(1)}, u32[]{:S(2)}, u32[]{:S(2)}) collective-permute-start(f32[8,128]{1,0:T(8,128)S(1)} %add.7), channel_id=1, source_target_pairs={{0,3},{1,2},{2,1},{3,0},{4,7},{5,6},{6,5},{7,4},{8,11},{9,10},{10,... | collective-permute-start | bytes 12296 | tf_op jit(solution)/shard_map/ppermute | solution.py:332
  9.8 3.3 %collective-permute-start.2 = (f32[8,128]{1,0:T(8,128)S(1)}, f32[8,128]{1,0:T(8,128)S(1)}, u32[]{:S(2)}, u32[]{:S(2)}) collective-permute-start(f32[8,128]{1,0:T(8,128)S(1)} %add.8.a_ref._), channel_id=1, source_target_pairs={{0,1},{1,0},{2,3},{3,2},{4,5},{5,4},{6,7},{7,6},{8,9},{9,8},{10,11... | collective-permute-start | bytes 12296 | tf_op jit(solution)/shard_map/ppermute | solution.py:338
  10.5 2.5 %copy-start = (bf16[4,256,1024]{2,1,0:T(8,128)(2,1)S(1)}, bf16[4,256,1024]{2,1,0:T(8,128)(2,1)}, u32[]{:S(2)}) copy-start(bf16[4,256,1024]{2,1,0:T(8,128)(2,1)} %param.11) | copy-start | bytes 6291460
  11.9 5.7 %collective-permute-start.4 = (bf16[8,16,1024]{2,1,0:T(8,128)(2,1)S(1)}, bf16[8,16,1024]{2,1,0:T(8,128)(2,1)S(1)}, u32[]{:S(2)}, u32[]{:S(2)}) collective-permute-start(bf16[8,16,1024]{2,1,0:T(8,128)(2,1)S(1)} %get-tuple-element.34), channel_id=1, source_target_pairs={{0,8},{8,0},{16,24},{24,16},{32,40},{40,32},{48,56},{56,48},{64,72... | collective-permute-start | bytes 786440 | tf_op jit(solution)/shard_map/ppermute | solution.py:335
  12.9 5.0 %collective-permute-start.5 = (bf16[4,8,2,16,1024]{4,3,2,1,0:T(8,128)(2,1)S(1)}, bf16[4,8,2,16,1024]{4,3,2,1,0:T(8,128)(2,1)S(1)}, u32[]{:S(2)}, u32[]{:S(2)}) collective-permute-start(bf16[4,8,2,16,1024]{4,3,2,1,0:T(8,128)(2,1)S(1)} %bitcast.7), channel_id=1, source_target_pairs={{0,8},{8,0},{16,24},{24,16},{32,40},{40,32},{48,56},{56,48},{64,72... | collective-permute-start | bytes 6291464 | tf_op jit(solution)/shard_map/ppermute | solution.py:337
  13.0 4.6 %collective-permute-start.3 = (f32[8,128]{1,0:T(8,128)S(1)}, f32[8,128]{1,0:T(8,128)S(1)}, u32[]{:S(2)}, u32[]{:S(2)}) collective-permute-start(f32[8,128]{1,0:T(8,128)S(1)} %add.9.sums_ref), channel_id=1, source_target_pairs={{0,4},{1,5},{2,6},{3,7},{4,0},{5,1},{6,2},{7,3},{8,12},{9,13},{10,... | collective-permute-start | bytes 12296 | tf_op jit(solution)/shard_map/ppermute | solution.py:340
  17.9 12.8 %copy-start.2 = (f32[16,1024]{1,0:T(8,128)S(1)}, f32[16,1024]{1,0:T(8,128)}, u32[]{:S(2)}) copy-start(f32[16,1024]{1,0:T(8,128)} %fresh_ref.1) | copy-start | bytes 196612
  18.0 12.8 %copy-start.3 = (f32[16,1024]{1,0:T(8,128)S(1)}, f32[16,1024]{1,0:T(8,128)}, u32[]{:S(2)}) copy-start(f32[16,1024]{1,0:T(8,128)} %m1_ref.1) | copy-start | bytes 196612
  18.0 12.7 %copy-start.4 = (f32[16,1024]{1,0:T(8,128)S(1)}, f32[16,1024]{1,0:T(8,128)}, u32[]{:S(2)}) copy-start(f32[16,1024]{1,0:T(8,128)} %m2_ref.1) | copy-start | bytes 196612
  18.0 12.7 %copy-start.5 = (f32[16,1024]{1,0:T(8,128)S(1)}, f32[16,1024]{1,0:T(8,128)}, u32[]{:S(2)}) copy-start(f32[16,1024]{1,0:T(8,128)} %master_ref.1) | copy-start | bytes 196612
  39.4 5.7 %collective-permute-start.6 = (bf16[8,16,1024]{2,1,0:T(8,128)(2,1)S(1)}, bf16[8,16,1024]{2,1,0:T(8,128)(2,1)S(1)}, u32[]{:S(2)}, u32[]{:S(2)}) collective-permute-start(bf16[8,16,1024]{2,1,0:T(8,128)(2,1)S(1)} %all_to_all.11.own_ref), channel_id=1, source_target_pairs={{0,8},{8,0},{16,24},{24,16},{32,40},{40,32},{48,56},{56,48},{64,72... | collective-permute-start | bytes 786440 | tf_op jit(solution)/shard_map/ppermute | solution.py:347
